TPU v7x, 32 devices: a whole 2x2x4 slice. The times are simulated.
32 devices in a mesh: dp: 4 (over x, core), ctx: 8 (over z, y).
Axes of the slice: x: 2, y: 2, z: 4, core: 2. Of those that a mesh axis runs over, the one named last changes fastest.
Arguments:
- layer_in: bfloat16 [4096, 2048], P(('dp', 'ctx')), may hold values from -6 to 6
- positions: int32 [4096], P(('dp', 'ctx')), may hold values from 0 to 1023, as said below
- doc_starts: int32 [4, 3], P('dp'), may hold values from 0 to 1023, as said below
- out_grad: bfloat16 [4096, 2048], P(('dp', 'ctx')), may hold values from -6 to 6
- norm_gains: float32 [2, 2048], P(None, ('dp', 'ctx')), may hold values from 0.5 to 1.5
- norm_gains_m: float32 [2, 2048], P(None, ('dp', 'ctx')), may hold values from -160 to 160
- norm_gains_v: float32 [2, 2048], P(None, ('dp', 'ctx')), may hold values from 3440.64 to 13926.4
- w_query: float32 [2048, 2048], P(('dp', 'ctx')), may hold values from -0.25 to 0.25
- w_query_m: float32 [2048, 2048], P(('dp', 'ctx')), may hold values from -64 to 64
- w_query_v: float32 [2048, 2048], P(('dp', 'ctx')), may hold values from 655.36 to 2580.48
- key_value_weight: float32 [2048, 1024], P(('dp', 'ctx')), may hold values from -0.125 to 0.125
- key_value_first_moment: float32 [2048, 1024], P(('dp', 'ctx')), may hold values from -224 to 224
- key_value_second_moment: float32 [2048, 1024], P(('dp', 'ctx')), may hold values from 5324.8 to 21708.8
- w_out: float32 [2048, 2048], P(('dp', 'ctx')), may hold values from -0.25 to 0.25
- w_out_m: float32 [2048, 2048], P(('dp', 'ctx')), may hold values from -32 to 32
- w_out_v: float32 [2048, 2048], P(('dp', 'ctx')), may hold values from 148 to 592
- w_gate_up: float32 [2048, 16384], P(('dp', 'ctx')), may hold values from -0.125 to 0.125
- w_gate_up_m: float32 [2048, 16384], P(('dp', 'ctx')), may hold values from -32 to 32
- w_gate_up_v: float32 [2048, 16384], P(('dp', 'ctx')), may hold values from 139.264 to 552.96
- w_down: float32 [8192, 2048], P(('dp', 'ctx')), may hold values from -0.09375 to 0.09375
- w_down_m: float32 [8192, 2048], P(('dp', 'ctx')), may hold values from -24 to 24
- w_down_v: float32 [8192, 2048], P(('dp', 'ctx')), may hold values from 77.824 to 311.296
Outputs:
- layer_out: bfloat16 [4096, 2048], P(('dp', 'ctx'))
- in_grad: float32 [4096, 2048], P(('dp', 'ctx'))
- norm_gains_grad: float32 [2, 2048], P(None, ('dp', 'ctx'))
- norm_gains_m_new: float32 [2, 2048], P(None, ('dp', 'ctx'))
- norm_gains_v_new: float32 [2, 2048], P(None, ('dp', 'ctx'))
- norm_gains_new: float32 [2, 2048], P(None, ('dp', 'ctx'))
- w_query_grad: float32 [2048, 2048], P(('dp', 'ctx'))
- w_query_m_new: float32 [2048, 2048], P(('dp', 'ctx'))
- w_query_v_new: float32 [2048, 2048], P(('dp', 'ctx'))
- w_query_new: float32 [2048, 2048], P(('dp', 'ctx'))
- w_keyval_grad: float32 [2048, 1024], P(('dp', 'ctx'))
- w_keyval_m_new: float32 [2048, 1024], P(('dp', 'ctx'))
- w_keyval_v_new: float32 [2048, 1024], P(('dp', 'ctx'))
- w_keyval_new: float32 [2048, 1024], P(('dp', 'ctx'))
- w_out_grad: float32 [2048, 2048], P(('dp', 'ctx'))
- w_out_m_new: float32 [2048, 2048], P(('dp', 'ctx'))
- w_out_v_new: float32 [2048, 2048], P(('dp', 'ctx'))
- w_out_new: float32 [2048, 2048], P(('dp', 'ctx'))
- w_gate_up_grad: float32 [2048, 16384], P(('dp', 'ctx'))
- w_gate_up_m_new: float32 [2048, 16384], P(('dp', 'ctx'))
- w_gate_up_v_new: float32 [2048, 16384], P(('dp', 'ctx'))
- w_gate_up_new: float32 [2048, 16384], P(('dp', 'ctx'))
- w_down_grad: float32 [8192, 2048], P(('dp', 'ctx'))
- w_down_m_new: float32 [8192, 2048], P(('dp', 'ctx'))
- w_down_v_new: float32 [8192, 2048], P(('dp', 'ctx'))
- w_down_new: float32 [8192, 2048], P(('dp', 'ctx'))
Inputs may be any that keep to these rules, and one draw needn't show every extreme that they name: Each sequence's positions are a permutation of 0 to 1023 made of 16 runs of 64 consecutive positions, each run starting at a multiple of 64, the runs in an order drawn for each sequence. `doc_starts`: in each sequence the 3 starts rise strictly over the whole sequence, the first is 0; a document runs from its start to the next start or to the sequence's end.
All inputs are finite; a program needn't handle non-finite values.
Results may differ from a plain program's by a relative error of at most 0.018.
The roundings to bfloat16 on the way count: a program that leaves them out, or rounds other values in their place, can miss the bound.
Values may be sent and summed in bfloat16 or wider, within the bound.
A program may use at most 512 MiB of HBM per device.

v0:
```python
import math

import jax
import jax.numpy as jnp
from jax import lax
from jax.sharding import PartitionSpec as P

MODEL_WIDTH = 2048
QUERY_HEADS = 32
KEY_VALUE_HEADS = 8
HEAD_SIZE = 64
FF = 8192
STEP = 10


eps_norm = 1e-05
rope_base = 500000.0
beta_one = 0.9
beta_two = 0.95
eps_adam = 1e-08
weight_decay = 0.1
masked_score = -1e30


def rates_for(seq_len):
    return (
        0.6,
        0.8 / math.sqrt(MODEL_WIDTH // 4),
        0.8 / math.sqrt(MODEL_WIDTH),
        0.8 / math.sqrt(max(220 * MODEL_WIDTH // seq_len, 1)),
        0.8 / math.sqrt(MODEL_WIDTH),
        0.8 / math.sqrt(FF // 2),
    )


def adamw(weight, grad_sum, first, second, rate, decay):
    first_new = beta_one * first + (1.0 - beta_one) * grad_sum
    second_new = beta_two * second + (1.0 - beta_two) * grad_sum * grad_sum
    first_hat = first_new / (1.0 - beta_one**STEP)
    second_hat = second_new / (1.0 - beta_two**STEP)
    weight_new = weight - rate * (first_hat / (jnp.sqrt(second_hat) + eps_adam) + decay * weight)
    return (first_new, second_new, weight_new)


def norm_forward(layer_rows):
    inverse = lax.rsqrt(jnp.mean(layer_rows * layer_rows, axis=-1, keepdims=True) + eps_norm)
    return (layer_rows * inverse, inverse)


def norm_backward(grad_out, normed, inverse, gain_row):
    scaled = grad_out * gain_row
    grad_in = inverse * (scaled - normed * jnp.mean(scaled * normed, axis=-1, keepdims=True))
    return (grad_in, jnp.sum(grad_out * normed, axis=0))


def rope_tables(token_placement, head_dim):
    half_dim = head_dim // 2
    frequencies = jnp.exp(
        jnp.arange(half_dim, dtype=jnp.float32) * (-2.0 * math.log(rope_base) / head_dim)
    )
    angles = token_placement.astype(jnp.float32)[:, None] * frequencies[None, :]
    return (jnp.cos(angles)[:, None, :], jnp.sin(angles)[:, None, :])


def apply_rotation(value_rows, cosine_table, sine_table):
    half_dim = value_rows.shape[-1] // 2
    first_half = value_rows[..., :half_dim]
    second_half = value_rows[..., half_dim:]
    return jnp.concatenate(
        [
            first_half * cosine_table - second_half * sine_table,
            second_half * cosine_table + first_half * sine_table,
        ],
        axis=-1,
    )


def reverse_rotation(grad_rows, cosine_table, sine_table):
    half_dim = grad_rows.shape[-1] // 2
    first_half = grad_rows[..., :half_dim]
    second_half = grad_rows[..., half_dim:]
    return jnp.concatenate(
        [
            first_half * cosine_table + second_half * sine_table,
            second_half * cosine_table - first_half * sine_table,
        ],
        axis=-1,
    )


def doc_lookup(token_placement, starts):
    return jnp.sum((token_placement[:, None] >= starts[None, :]).astype(jnp.int32), axis=1) - 1


def times_transposed(left, right):
    return lax.dot_general(
        left, right, (((1,), (1,)), ((), ())), preferred_element_type=jnp.float32
    )


def transposed_times(left, right):
    return lax.dot_general(
        left, right, (((0,), (0,)), ((), ())), preferred_element_type=jnp.float32
    )


def body(
    layer_in,
    positions,
    doc_starts,
    out_grad,
    norm_gains,
    norm_gains_m,
    norm_gains_v,
    w_query,
    w_query_m,
    w_query_v,
    key_value_weight,
    key_value_first_moment,
    key_value_second_moment,
    w_out,
    w_out_m,
    w_out_v,
    w_gate_up,
    w_gate_up_m,
    w_gate_up_v,
    w_down,
    w_down_m,
    w_down_v,
):
    number_of_tokens = layer_in.shape[0]
    ctx_count = lax.axis_size("ctx")
    seq_len = number_of_tokens * ctx_count
    key_value_width = KEY_VALUE_HEADS * HEAD_SIZE
    query_group_size = QUERY_HEADS // KEY_VALUE_HEADS
    score_scale = 1.0 / math.sqrt(HEAD_SIZE)
    needed = -(-512 // number_of_tokens)
    shard_span = min(ctx_count, 1 << max(0, (needed - 1).bit_length()))
    width_of_block = shard_span * number_of_tokens
    count_of_blocks = ctx_count // shard_span
    key_places = lax.all_gather(positions, "ctx", axis=0, tiled=True)
    starts = doc_starts[0]
    own_docs = doc_lookup(positions, starts)
    key_docs = doc_lookup(key_places, starts)
    query_full, keyval_full, out_full, gains_full = (
        lax.all_gather(w_query.astype(jnp.bfloat16), ("dp", "ctx"), axis=0, tiled=True),
        lax.all_gather(key_value_weight.astype(jnp.bfloat16), ("dp", "ctx"), axis=0, tiled=True),
        lax.all_gather(w_out.astype(jnp.bfloat16), ("dp", "ctx"), axis=0, tiled=True),
        lax.all_gather(norm_gains.astype(jnp.bfloat16), ("dp", "ctx"), axis=1, tiled=True),
    )
    gain_one = gains_full[0].astype(jnp.float32)
    gain_two = gains_full[1].astype(jnp.float32)
    layer_rows = layer_in.astype(jnp.float32)
    normed_one, inverse_one = norm_forward(layer_rows)
    input_one = (normed_one * gain_one).astype(jnp.bfloat16)
    query_pre = jnp.dot(input_one, query_full, preferred_element_type=jnp.float32)
    key_value_projected = jnp.dot(input_one, keyval_full, preferred_element_type=jnp.float32)
    cosine_table, sine_table = rope_tables(positions, HEAD_SIZE)
    query_rows = (
        apply_rotation(
            query_pre.reshape(number_of_tokens, QUERY_HEADS, HEAD_SIZE), cosine_table, sine_table
        )
        .astype(jnp.bfloat16)
        .reshape(number_of_tokens, KEY_VALUE_HEADS, query_group_size, HEAD_SIZE)
    )
    keys_own = (
        apply_rotation(
            key_value_projected[:, :key_value_width].reshape(
                number_of_tokens, KEY_VALUE_HEADS, HEAD_SIZE
            ),
            cosine_table,
            sine_table,
        )
        .astype(jnp.bfloat16)
        .reshape(number_of_tokens, key_value_width)
    )
    values_own = key_value_projected[:, key_value_width:].astype(jnp.bfloat16)
    every_key, every_value = (
        lax.all_gather(keys_own, "ctx", axis=0, tiled=True),
        lax.all_gather(values_own, "ctx", axis=0, tiled=True),
    )
    blocked_keys = every_key.reshape(count_of_blocks, width_of_block, KEY_VALUE_HEADS, HEAD_SIZE)
    blocked_values = every_value.reshape(
        count_of_blocks, width_of_block, KEY_VALUE_HEADS, HEAD_SIZE
    )
    place_blocks = key_places.reshape(count_of_blocks, width_of_block)
    doc_blocks = key_docs.reshape(count_of_blocks, width_of_block)

    def visible(place_blk, doc_blk):
        allowed = (place_blk[None, :] <= positions[:, None]) & (
            doc_blk[None, :] == own_docs[:, None]
        )
        return allowed[:, None, None, :]

    def scores_of(key_blk):
        return (
            jnp.einsum("tkgd,nkd->tkgn", query_rows, key_blk, preferred_element_type=jnp.float32)
            * score_scale
        )

    def stats_step(carry, block):
        row_top, row_total = carry
        key_blk, place_blk, doc_blk = block
        allowed = visible(place_blk, doc_blk)
        masked = jnp.where(allowed, scores_of(key_blk), masked_score)
        new_top = jnp.maximum(row_top, jnp.max(masked, axis=-1, keepdims=True))
        row_total = row_total * jnp.exp(row_top - new_top) + jnp.sum(
            jnp.where(allowed, jnp.exp(masked - new_top), 0.0), axis=-1, keepdims=True
        )
        return ((new_top, row_total), None)

    statistic_shape = (number_of_tokens, KEY_VALUE_HEADS, query_group_size, 1)
    (row_top, row_total), unused = lax.scan(
        stats_step,
        (
            jnp.full(statistic_shape, masked_score, jnp.float32),
            jnp.zeros(statistic_shape, jnp.float32),
        ),
        (blocked_keys, place_blocks, doc_blocks),
    )
    log_total = row_top + jnp.log(row_total)

    def probs_of(key_blk, place_blk, doc_blk):
        allowed = visible(place_blk, doc_blk)
        masked = jnp.where(allowed, scores_of(key_blk), masked_score)
        return jnp.where(allowed, jnp.exp(masked - log_total), 0.0)

    def output_step(carry, block):
        key_blk, value_blk, place_blk, doc_blk = block
        probs_low = probs_of(key_blk, place_blk, doc_blk).astype(jnp.bfloat16)
        added = jnp.einsum(
            "tkgn,nkd->tkgd", probs_low, value_blk, preferred_element_type=jnp.float32
        )
        return (carry + added, None)

    attention_output, unused = lax.scan(
        output_step,
        jnp.zeros((number_of_tokens, KEY_VALUE_HEADS, query_group_size, HEAD_SIZE), jnp.float32),
        (blocked_keys, blocked_values, place_blocks, doc_blocks),
    )
    mixed = attention_output.reshape(number_of_tokens, QUERY_HEADS * HEAD_SIZE).astype(jnp.bfloat16)
    middle = layer_rows + jnp.dot(mixed, out_full, preferred_element_type=jnp.float32)
    normed_two, inverse_two = norm_forward(middle)
    input_two = (normed_two * gain_two).astype(jnp.bfloat16)
    gate_up_low = w_gate_up.astype(jnp.bfloat16)
    down_low = w_down.astype(jnp.bfloat16)
    columns = input_two
    gate_up = jnp.dot(
        columns,
        lax.all_gather(gate_up_low, ("dp", "ctx"), axis=0, tiled=True),
        preferred_element_type=jnp.float32,
    )
    gate_part = gate_up[:, :FF]
    up_part = gate_up[:, FF:]
    sigmoid_gate = jax.nn.sigmoid(gate_part)
    silu_gate = gate_part * sigmoid_gate
    hidden = (silu_gate * up_part).astype(jnp.bfloat16)
    columns = hidden
    down_sum = jnp.dot(
        columns,
        lax.all_gather(down_low, ("dp", "ctx"), axis=0, tiled=True),
        preferred_element_type=jnp.float32,
    )
    layer_out = (middle + down_sum).astype(jnp.bfloat16)
    grad_rows = out_grad.astype(jnp.float32)
    grad_hidden = times_transposed(
        out_grad, lax.all_gather(down_low, ("dp", "ctx"), axis=0, tiled=True)
    )
    grad_gate = grad_hidden * up_part * sigmoid_gate * (1.0 + gate_part * (1.0 - sigmoid_gate))
    grad_up = grad_hidden * silu_gate
    grad_gate_up = jnp.concatenate([grad_gate, grad_up], axis=1).astype(jnp.bfloat16)
    down_grad = lax.psum_scatter(
        transposed_times(hidden, out_grad), ("dp", "ctx"), scatter_dimension=0, tiled=True
    )
    grad_normed_two = times_transposed(
        grad_gate_up, lax.all_gather(gate_up_low, ("dp", "ctx"), axis=0, tiled=True)
    )
    gate_up_grad = lax.psum_scatter(
        transposed_times(input_two, grad_gate_up), ("dp", "ctx"), scatter_dimension=0, tiled=True
    )
    grad_norm_two, gain_two_grad = norm_backward(grad_normed_two, normed_two, inverse_two, gain_two)
    grad_middle = grad_rows + grad_norm_two
    grad_middle_low = grad_middle.astype(jnp.bfloat16)
    out_term = transposed_times(mixed, grad_middle_low)
    grad_mixed = (
        times_transposed(grad_middle_low, out_full)
        .astype(jnp.bfloat16)
        .reshape(number_of_tokens, KEY_VALUE_HEADS, query_group_size, HEAD_SIZE)
    )
    delta = jnp.sum(grad_mixed.astype(jnp.float32) * attention_output, axis=-1, keepdims=True)

    def back_step(grad_query, block):
        key_blk, value_blk, place_blk, doc_blk = block
        probs = probs_of(key_blk, place_blk, doc_blk)
        probs_low = probs.astype(jnp.bfloat16)
        grad_probs = jnp.einsum(
            "tkgd,nkd->tkgn", grad_mixed, value_blk, preferred_element_type=jnp.float32
        )
        grad_scores = (probs * (grad_probs - delta) * score_scale).astype(jnp.bfloat16)
        grad_query = grad_query + jnp.einsum(
            "tkgn,nkd->tkgd", grad_scores, key_blk, preferred_element_type=jnp.float32
        )
        key_grad = jnp.einsum(
            "tkgn,tkgd->nkd", grad_scores, query_rows, preferred_element_type=jnp.float32
        )
        value_grad = jnp.einsum(
            "tkgn,tkgd->nkd", probs_low, grad_mixed, preferred_element_type=jnp.float32
        )
        return (grad_query, (key_grad, value_grad))

    grad_query, (key_grads, value_grads) = lax.scan(
        back_step,
        jnp.zeros((number_of_tokens, KEY_VALUE_HEADS, query_group_size, HEAD_SIZE), jnp.float32),
        (blocked_keys, blocked_values, place_blocks, doc_blocks),
    )
    summed_key_gradient, value_sum = (
        lax.psum_scatter(
            key_grads.reshape(seq_len, key_value_width).astype(jnp.bfloat16),
            "ctx",
            scatter_dimension=0,
            tiled=True,
        ).astype(jnp.float32),
        lax.psum_scatter(
            value_grads.reshape(seq_len, key_value_width).astype(jnp.bfloat16),
            "ctx",
            scatter_dimension=0,
            tiled=True,
        ).astype(jnp.float32),
    )
    key_gradient_unrotated = reverse_rotation(
        summed_key_gradient.reshape(number_of_tokens, KEY_VALUE_HEADS, HEAD_SIZE),
        cosine_table,
        sine_table,
    ).reshape(number_of_tokens, key_value_width)
    grad_keyval = jnp.concatenate([key_gradient_unrotated, value_sum], axis=1).astype(jnp.bfloat16)
    grad_query_low = (
        reverse_rotation(
            grad_query.reshape(number_of_tokens, QUERY_HEADS, HEAD_SIZE), cosine_table, sine_table
        )
        .reshape(number_of_tokens, QUERY_HEADS * HEAD_SIZE)
        .astype(jnp.bfloat16)
    )
    grad_normed_one = times_transposed(grad_query_low, query_full) + times_transposed(
        grad_keyval, keyval_full
    )
    query_term = transposed_times(input_one, grad_query_low)
    keyval_term = transposed_times(input_one, grad_keyval)
    grad_norm_one, gain_one_grad = norm_backward(grad_normed_one, normed_one, inverse_one, gain_one)
    in_grad = grad_middle + grad_norm_one
    gain_term = jnp.stack([gain_one_grad, gain_two_grad])
    query_grad, keyval_grad, out_weight_grad, gains_grad = (
        lax.psum_scatter(query_term, ("dp", "ctx"), scatter_dimension=0, tiled=True),
        lax.psum_scatter(keyval_term, ("dp", "ctx"), scatter_dimension=0, tiled=True),
        lax.psum_scatter(out_term, ("dp", "ctx"), scatter_dimension=0, tiled=True),
        lax.psum_scatter(gain_term, ("dp", "ctx"), scatter_dimension=1, tiled=True),
    )
    rates = rates_for(seq_len)
    gains_m_new, gains_v_new, gains_new = adamw(
        norm_gains, gains_grad, norm_gains_m, norm_gains_v, rates[0], 0.0
    )
    query_m_new, query_v_new, query_new = adamw(
        w_query, query_grad, w_query_m, w_query_v, rates[1], weight_decay
    )
    keyval_m_new, keyval_v_new, keyval_new = adamw(
        key_value_weight,
        keyval_grad,
        key_value_first_moment,
        key_value_second_moment,
        rates[2],
        weight_decay,
    )
    out_m_new, out_v_new, out_new = adamw(
        w_out, out_weight_grad, w_out_m, w_out_v, rates[3], weight_decay
    )
    gate_up_m_new, gate_up_v_new, gate_up_new = adamw(
        w_gate_up, gate_up_grad, w_gate_up_m, w_gate_up_v, rates[4], weight_decay
    )
    down_m_new, down_v_new, down_new = adamw(
        w_down, down_grad, w_down_m, w_down_v, rates[5], weight_decay
    )
    return (
        layer_out,
        in_grad,
        gains_grad,
        gains_m_new,
        gains_v_new,
        gains_new,
        query_grad,
        query_m_new,
        query_v_new,
        query_new,
        keyval_grad,
        keyval_m_new,
        keyval_v_new,
        keyval_new,
        out_weight_grad,
        out_m_new,
        out_v_new,
        out_new,
        gate_up_grad,
        gate_up_m_new,
        gate_up_v_new,
        gate_up_new,
        down_grad,
        down_m_new,
        down_v_new,
        down_new,
    )


def solution(mesh):
    return jax.shard_map(
        body,
        mesh=mesh,
        in_specs=(
            P(("dp", "ctx"), None),
            P(("dp", "ctx")),
            P("dp", None),
            P(("dp", "ctx"), None),
            P(None, ("dp", "ctx")),
            P(None, ("dp", "ctx")),
            P(None, ("dp", "ctx")),
            P(("dp", "ctx"), None),
            P(("dp", "ctx"), None),
            P(("dp", "ctx"), None),
            P(("dp", "ctx"), None),
            P(("dp", "ctx"), None),
            P(("dp", "ctx"), None),
            P(("dp", "ctx"), None),
            P(("dp", "ctx"), None),
            P(("dp", "ctx"), None),
            P(("dp", "ctx"), None),
            P(("dp", "ctx"), None),
            P(("dp", "ctx"), None),
            P(("dp", "ctx"), None),
            P(("dp", "ctx"), None),
            P(("dp", "ctx"), None),
        ),
        out_specs=(
            P(("dp", "ctx"), None),
            P(("dp", "ctx"), None),
            P(None, ("dp", "ctx")),
            P(None, ("dp", "ctx")),
            P(None, ("dp", "ctx")),
            P(None, ("dp", "ctx")),
            P(("dp", "ctx"), None),
            P(("dp", "ctx"), None),
            P(("dp", "ctx"), None),
            P(("dp", "ctx"), None),
            P(("dp", "ctx"), None),
            P(("dp", "ctx"), None),
            P(("dp", "ctx"), None),
            P(("dp", "ctx"), None),
            P(("dp", "ctx"), None),
            P(("dp", "ctx"), None),
            P(("dp", "ctx"), None),
            P(("dp", "ctx"), None),
            P(("dp", "ctx"), None),
            P(("dp", "ctx"), None),
            P(("dp", "ctx"), None),
            P(("dp", "ctx"), None),
            P(("dp", "ctx"), None),
            P(("dp", "ctx"), None),
            P(("dp", "ctx"), None),
            P(("dp", "ctx"), None),
        ),
        check_vma=False,
    )
```

profile of v0, /device:TPU:0, one launch (start us, length us, event | category | flops | bytes accessed | tf_op | source)
XLA Modules:
  0.0 6377.4 jit_solution(6527087637309665214)
XLA Ops:
  9.7 69.4 %all-gather = bf16[32,64,2]{1,2,0:T(2,128)(2,1)S(1)} all-gather(bf16[1,64,2]{1,2,0:T(2,128)(2,1)S(1)} %convert_bitcast_fusion), channel_id=1, replica_groups=mesh['dp'=4,'ctx'=8] {'dp','ctx'}, dimensions={0}, use_global_device_ids=true | all-gather | bytes 8448 | tf_op jit(solution)/shard_map/all_gather | solution.py:149
  92.5 16.3 all-gather.1
  126.4 35.9 all-gather.14.cloned.1.call-done
  164.3 77.7 %all-gather.16.cloned.1.call-done = bf16[2048,2048]{1,0:T(8,128)(2,1)} async-done(((bf16[64,2048]{1,0:T(8,128)(2,1)}), bf16[2048,2048]{1,0:T(8,128)(2,1)}) %all-gather.16.cloned.1.call-update) | async-done | bytes 8388624 | tf_op jit(solution)/shard_map/all_gather | solution.py:146
  249.0 18.9 while.39
  280.4 41.0 all-gather.18.cloned.1.call-done
  326.4 353.4 %all-gather.20.cloned.1.call-done = bf16[2048,16384]{1,0:T(8,128)(2,1)} async-done(((bf16[64,16384]{1,0:T(8,128)(2,1)}), bf16[2048,16384]{1,0:T(8,128)(2,1)}) %all-gather.20.cloned.1.call-update) | async-done | bytes 67108880 | tf_op jit(solution)/shard_map/all_gather | solution.py:250
  679.8 27.4 fusion.91
  707.2 169.2 %all-gather.22.cloned.1.call-done = bf16[8192,2048]{1,0:T(8,128)(2,1)} async-done(((bf16[256,2048]{1,0:T(8,128)(2,1)}), bf16[8192,2048]{1,0:T(8,128)(2,1)}) %all-gather.22.cloned.1.call-update) | async-done | bytes 33554448 | tf_op jit(solution)/shard_map/all_gather | solution.py:261
  876.4 21.0 multiply_convert_fusion.1
  897.4 30.3 multiply_reduce_fusion
  941.0 32.4 while.41
  994.5 48.2 reduce-scatter.26.cloned.1.call-done
  1043.8 65.6 %reduce-scatter.28.cloned.1.call-done = bf16[128,512]{1,0:T(8,128)(2,1)} async-done(((bf16[1024,512]{1,0:T(8,128)(2,1)}), bf16[128,512]{1,0:T(8,128)(2,1)}) %reduce-scatter.28.cloned.1.call-update) | async-done | bytes 131088
  1139.6 24.8 fusion.106
  1165.7 45.8 fusion.64
  1211.6 16.6 fusion.66
  1229.6 21.7 reduce-scatter.30.cloned.1.call-done
  1252.8 182.3 %reduce-scatter.20.cloned.1.call-done = f32[64,1024]{1,0:T(8,128)} async-done(((f32[2048,1024]{1,0:T(8,128)}), f32[64,1024]{1,0:T(8,128)}) %reduce-scatter.20.cloned.1.call-update) | async-done | bytes 262160 | tf_op jit(solution)/shard_map/reduce_scatter | solution.py:353
  1437.2 358.5 %reduce-scatter.18.cloned.1.call-done = f32[64,2048]{1,0:T(8,128)} async-done(((f32[2048,2048]{1,0:T(8,128)}), f32[64,2048]{1,0:T(8,128)}) %reduce-scatter.18.cloned.1.call-update) | async-done | bytes 524304 | tf_op jit(solution)/shard_map/reduce_scatter | solution.py:352
  1798.4 357.6 %reduce-scatter.22.cloned.1.call-done = f32[64,2048]{1,0:T(8,128)} async-done(((f32[2048,2048]{1,0:T(8,128)}), f32[64,2048]{1,0:T(8,128)}) %reduce-scatter.22.cloned.1.call-update) | async-done | bytes 524304 | tf_op jit(solution)/shard_map/reduce_scatter | solution.py:354
  2158.7 1401.9 %reduce-scatter.24.cloned.1.call-done = f32[256,2048]{1,0:T(8,128)} async-done(((f32[8192,2048]{1,0:T(8,128)}), f32[256,2048]{1,0:T(8,128)}) %reduce-scatter.24.cloned.1.call-update) | async-done | bytes 2097168 | tf_op jit(solution)/shard_map/reduce_scatter | solution.py:272
  3567.6 2791.7 %reduce-scatter.32.cloned.1.call-done = f32[64,16384]{1,0:T(8,128)} async-done(((f32[2048,16384]{1,0:T(8,128)}), f32[64,16384]{1,0:T(8,128)}) %reduce-scatter.32.cloned.1.call-update) | async-done | bytes 4194320
  6359.3 11.4 multiply_subtract_fusion
  (237 shorter events, 204.6 us)
Async XLA Ops:
  7.2 73.3 %all-gather.10.cloned.1.call-start = ((), (), s32[]{:S(2)}) async-start(), calls=%async_computation.8 | async-start | bytes 4325376 | tf_op jit(solution)/shard_map/all_gather | solution.py:147
  8.9 112.4 %all-gather.12.cloned.1.call-start = ((), (), s32[]{:S(2)}) async-start(), calls=%async_computation.9 | async-start | bytes 1179648 | tf_op jit(solution)/shard_map/all_gather | solution.py:180
  80.5 847.2 %copy-start.14 = (f32[1,2048]{1,0:T(1,128)}, f32[1,2048]{1,0:T(1,128)S(1)}, u32[]{:S(2)}) copy-start(f32[1,2048]{1,0:T(1,128)S(1)} %get-tuple-element.544) | copy-start | bytes 24580
  84.4 77.9 %all-gather.14.cloned.1.call-start = ((), (), s32[]{:S(2)}) async-start(), calls=%async_computation.10 | async-start | bytes 1179648 | tf_op jit(solution)/shard_map/all_gather | solution.py:179
  85.5 156.4 %all-gather.16.cloned.1.call-start = ((), (), s32[]{:S(2)}) async-start(), calls=%async_computation.11 | async-start | bytes 8650752 | tf_op jit(solution)/shard_map/all_gather | solution.py:146
  86.4 235.1 %all-gather.18.cloned.1.call-start = ((), (), s32[]{:S(2)}) async-start(), calls=%async_computation.12 | async-start | bytes 8650752 | tf_op jit(solution)/shard_map/all_gather | solution.py:148
  87.2 592.6 %all-gather.20.cloned.1.call-start = ((), (), s32[]{:S(2)}) async-start(), calls=%async_computation.13 | async-start | bytes 69206016 | tf_op jit(solution)/shard_map/all_gather | solution.py:250
  91.2 785.2 %all-gather.22.cloned.1.call-start = ((), (), s32[]{:S(2)}) async-start(), calls=%async_computation.14 | async-start | bytes 34603008 | tf_op jit(solution)/shard_map/all_gather | solution.py:261
  92.4 950.2 %reduce-scatter.26.cloned.1.call-start = ((), (), s32[]{:S(2)}) async-start(), calls=%async_computation.19 | async-start | bytes 1179648
  326.3 601.3 %copy-start.3 = (f32[128,2048]{1,0:T(8,128)}, f32[128,2048]{1,0:T(8,128)S(1)}, u32[]{:S(2)}) copy-start(f32[128,2048]{1,0:T(8,128)S(1)} %get-tuple-element.549) | copy-start | bytes 3145732
  326.4 601.3 %copy-start.31 = (f32[128]{0:T(128)}, f32[128]{0:T(128)S(1)}, u32[]{:S(2)}) copy-start(f32[128]{0:T(128)S(1)} %add_rsqrt_fusion) | copy-start | bytes 1540
  679.8 196.6 %copy-start.16 = (bf16[128,2048]{1,0:T(8,128)(2,1)S(1)}, bf16[128,2048]{1,0:T(8,128)(2,1)}, u32[]{:S(2)}) copy-start(bf16[128,2048]{1,0:T(8,128)(2,1)} %param.31) | copy-start | bytes 1572868
  981.0 128.4 %reduce-scatter.28.cloned.1.call-start = ((), (), s32[]{:S(2)}) async-start(), calls=%async_computation.20 | async-start | bytes 1179648
  987.6 263.7 %reduce-scatter.30.cloned.1.call-start = ((), (), s32[]{:S(2)}) async-start(), calls=%async_computation.21 | async-start | bytes 1081344
  1117.2 317.9 %reduce-scatter.20.cloned.1.call-start = ((), (), s32[]{:S(2)}) async-start(), calls=%async_computation.16 | async-start | bytes 8650752 | tf_op jit(solution)/shard_map/reduce_scatter | solution.py:353
  1121.9 673.8 %reduce-scatter.18.cloned.1.call-start = ((), (), s32[]{:S(2)}) async-start(), calls=%async_computation.15 | async-start | bytes 17301504 | tf_op jit(solution)/shard_map/reduce_scatter | solution.py:352
  1130.2 1025.8 %reduce-scatter.22.cloned.1.call-start = ((), (), s32[]{:S(2)}) async-start(), calls=%async_computation.17 | async-start | bytes 17301504 | tf_op jit(solution)/shard_map/reduce_scatter | solution.py:354
  1139.6 2421.1 %reduce-scatter.24.cloned.1.call-start = ((), (), s32[]{:S(2)}) async-start(), calls=%async_computation.18 | async-start | bytes 69206016 | tf_op jit(solution)/shard_map/reduce_scatter | solution.py:272
  1164.5 5194.8 %reduce-scatter.32.cloned.1.call-start = ((), (), s32[]{:S(2)}) async-start(), calls=%async_computation.22 | async-start | bytes 138412032
  1211.6 223.5 %copy-start.24 = (f32[64,1024]{1,0:T(8,128)S(1)}, f32[64,1024]{1,0:T(8,128)}, u32[]{:S(2)}) copy-start(f32[64,1024]{1,0:T(8,128)} %param.38) | copy-start | bytes 786436
  1228.3 567.4 %copy-start.18 = (f32[64,2048]{1,0:T(8,128)S(1)}, f32[64,2048]{1,0:T(8,128)}, u32[]{:S(2)}) copy-start(f32[64,2048]{1,0:T(8,128)} %param.35) | copy-start | bytes 1572868
  1229.6 926.3 %copy-start.20 = (f32[64,2048]{1,0:T(8,128)S(1)}, f32[64,2048]{1,0:T(8,128)}, u32[]{:S(2)}) copy-start(f32[64,2048]{1,0:T(8,128)} %param.41) | copy-start | bytes 1572868
  1252.2 906.5 %copy-start.36 = (f32[2,64]{1,0:T(2,128)}, f32[2,64]{1,0:T(2,128)S(1)}, u32[]{:S(2)}) copy-start(f32[2,64]{1,0:T(2,128)S(1)} %copy.126) | copy-start | bytes 1540
  1252.8 2307.9 %copy-start.11 = (f32[256,2048]{1,0:T(8,128)S(1)}, f32[256,2048]{1,0:T(8,128)}, u32[]{:S(2)}) copy-start(f32[256,2048]{1,0:T(8,128)} %param.47) | copy-start | bytes 6291460
  (38 other events, 1548.7 us)
Sparse Core Ops, SparseCore 0:
  11.7 64.6 all-gather.9
  84.5 36.7 all-gather.11
  123.9 38.2 all-gather.13
  165.7 76.2 all-gather.15
  245.4 75.9 all-gather.17
  324.9 354.8 all-gather.19
  683.4 192.9 all-gather.21
  981.1 61.5 reduce-scatter.25
  1047.0 62.3 reduce-scatter.27
  1117.3 134.0 reduce-scatter.29
  1254.3 180.7 reduce-scatter.19
  1437.9 357.7 reduce-scatter.17
  1798.6 357.3 reduce-scatter.21
  2158.9 1401.7 reduce-scatter.23
  3563.6 2795.6 reduce-scatter.31
where the time goes:
time: 6380 us
  waiting for transfers between devices  5920 us (93%)
  matrix products  270 us (4%)
  blocking collectives  85.7 us (1%)
    unnamed x19, waiting for transfers between devices  2930 us
    reduce_scatter x1, waiting for transfers between devices, body(): lax.psum_scatter(transposed_times(hidden, out_grad), ('dp', 'ctx'), scatt...  1400 us
    reduce_scatter x1, waiting for transfers between devices, body(): lax.psum_scatter(query_term, ('dp', 'ctx'), scatter_dimension=0, tiled=True)  358 us
    reduce_scatter x1, waiting for transfers between devices, body(): lax.psum_scatter(out_term, ('dp', 'ctx'), scatter_dimension=0, tiled=True)  358 us
    all_gather x1, waiting for transfers between devices, body(): lax.all_gather(gate_up_low, ('dp', 'ctx'), axis=0, tiled=True)  353 us
    reduce_scatter x1, waiting for transfers between devices, body(): lax.psum_scatter(keyval_term, ('dp', 'ctx'), scatter_dimension=0, tiled=T...  182 us
    all_gather x1, waiting for transfers between devices, body(): lax.all_gather(down_low, ('dp', 'ctx'), axis=0, tiled=True)  169 us
  transfers between devices with their start and end apart: 15, of which 14 were waited for; matrix products, arithmetic and copies ran while one was open for 4% of the time, Pallas kernels for 0%

commit v1 on v0

--- a/solution.py
+++ b/solution.py
@@ -1,8 +1,11 @@
+import functools
 import math
 
 import jax
 import jax.numpy as jnp
 from jax import lax
+from jax.experimental import pallas as pl
+from jax.experimental.pallas import tpu as pltpu
 from jax.sharding import PartitionSpec as P
 
 MODEL_WIDTH = 2048
@@ -102,6 +105,930 @@
     return lax.dot_general(
         left, right, (((0,), (0,)), ((), ())), preferred_element_type=jnp.float32
     )
+
+
+XS = 2
+YS = 2
+ZS = 4
+PLANE = ZS * YS
+RANKS = 2 * XS * PLANE
+MESH = pl.DeviceIdType.MESH
+
+
+def place():
+    d = lax.axis_index("dp")
+    c = lax.axis_index("ctx")
+    return d, c, lax.div(d, 2), lax.rem(d, 2), lax.div(c, YS), lax.rem(c, YS)
+
+
+def remote(src, dst, send_sem, recv_sem, d, c):
+    return pltpu.make_async_remote_copy(
+        src_ref=src,
+        dst_ref=dst,
+        send_sem=send_sem,
+        recv_sem=recv_sem,
+        device_id=(d, c),
+        device_id_type=MESH,
+    )
+
+
+def greet(peers):
+    barrier = pltpu.get_barrier_semaphore()
+    for d, c in peers:
+        pl.semaphore_signal(barrier, inc=1, device_id=(d, c), device_id_type=MESH)
+    pl.semaphore_wait(barrier, len(peers))
+
+
+def plane_peers(d, c):
+    return [(d, lax.rem(c + k, PLANE)) for k in range(1, PLANE)]
+
+
+def chip_peers(d, c, x, core):
+    return [(x * 2 + 1 - core, c), ((1 - x) * 2 + core, c)]
+
+
+class SequenceGather:
+    def __init__(self, own, out, sems, chunks):
+        self.own, self.out, self.chunks = own, out, chunks
+        self.zs, self.zr, self.ys, self.yr, self.local_sem = sems
+        self.d, self.c, _, _, self.z, self.y = place()
+        self.rows = own.shape[0] // chunks
+        self.sent = []
+
+    @staticmethod
+    def scratch(chunks):
+        return [
+            pltpu.SemaphoreType.DMA((ZS, chunks)),
+            pltpu.SemaphoreType.DMA((ZS, chunks)),
+            pltpu.SemaphoreType.DMA((ZS, chunks)),
+            pltpu.SemaphoreType.DMA((ZS, chunks)),
+            pltpu.SemaphoreType.DMA(()),
+        ]
+
+    def part(self, ref, k):
+        return ref.at[pl.ds(k * self.rows, self.rows)]
+
+    def across(self, z, k, src):
+        slot = z * YS + self.y
+        return remote(
+            src,
+            self.part(self.out.at[slot], k),
+            self.ys.at[z, k],
+            self.yr.at[z, k],
+            self.d,
+            self.z * YS + 1 - self.y,
+        )
+
+    def along(self, off, k):
+        to = lax.rem(self.z + off, ZS)
+        return remote(
+            self.part(self.own, k),
+            self.part(self.out.at[self.c], k),
+            self.zs.at[off, k],
+            self.zr.at[self.z, k],
+            self.d,
+            to * YS + self.y,
+        )
+
+    def first(self):
+        self.local = pltpu.make_async_copy(self.own, self.out.at[self.c], self.local_sem)
+        self.local.start()
+        for k in range(self.chunks):
+            for off in (2, 1, 3):
+                copy = self.along(off, k)
+                copy.start()
+                self.sent.append(copy)
+            copy = self.across(self.z, k, self.part(self.own, k))
+            copy.start()
+            self.sent.append(copy)
+
+    def relay(self, k):
+        for off in (1, 3, 2):
+            source = lax.rem(self.z + off, ZS)
+            slot = source * YS + self.y
+            block = self.part(self.out.at[slot], k)
+            remote(
+                block, block, self.zs.at[off, k], self.zr.at[source, k], self.d, slot
+            ).wait_recv()
+            copy = self.across(source, k, block)
+            copy.start()
+            self.sent.append(copy)
+
+    def last(self):
+        for k in range(self.chunks):
+            for z in range(ZS):
+                block = self.part(self.out.at[z * YS + 1 - self.y], k)
+                remote(
+                    block,
+                    block,
+                    self.ys.at[z, k],
+                    self.yr.at[z, k],
+                    self.d,
+                    self.z * YS + 1 - self.y,
+                ).wait_recv()
+        for copy in self.sent:
+            copy.wait_send()
+        self.local.wait()
+
+
+class SequenceScatter:
+    def __init__(self, parts, out, ybuf, stage, zbuf, sems, chunks):
+        self.parts, self.out, self.chunks = parts, out, chunks
+        self.ybuf, self.stage, self.zbuf = ybuf, stage, zbuf
+        self.ys, self.yr, self.zs, self.zr = sems
+        self.d, self.c, _, _, self.z, self.y = place()
+        self.rows = parts.shape[1] // chunks
+        self.sent = []
+
+    @staticmethod
+    def scratch(rows, width, chunks):
+        return [
+            pltpu.VMEM((ZS, rows, width), jnp.bfloat16),
+            pltpu.VMEM((ZS, rows, width), jnp.bfloat16),
+            pltpu.VMEM((ZS, rows, width), jnp.bfloat16),
+            pltpu.SemaphoreType.DMA((ZS, chunks)),
+            pltpu.SemaphoreType.DMA((ZS, chunks)),
+            pltpu.SemaphoreType.DMA((ZS, chunks)),
+            pltpu.SemaphoreType.DMA((ZS, chunks)),
+        ]
+
+    def span(self, k):
+        return pl.ds(k * self.rows, self.rows)
+
+    def across(self, z, k):
+        return remote(
+            self.parts.at[z * YS + 1 - self.y, self.span(k)],
+            self.ybuf.at[z, self.span(k)],
+            self.ys.at[z, k],
+            self.yr.at[z, k],
+            self.d,
+            self.z * YS + 1 - self.y,
+        )
+
+    def along(self, off, k):
+        to = lax.rem(self.z + off, ZS)
+        return remote(
+            self.stage.at[off, self.span(k)],
+            self.zbuf.at[self.z, self.span(k)],
+            self.zs.at[off, k],
+            self.zr.at[self.z, k],
+            self.d,
+            to * YS + self.y,
+        )
+
+    def first(self):
+        for k in range(self.chunks):
+            for off in (2, 1, 3, 0):
+                copy = self.across(lax.rem(self.z + off, ZS), k)
+                copy.start()
+                self.sent.append(copy)
+
+    def relay(self, k):
+        for off in (2, 1, 3):
+            z = lax.rem(self.z + off, ZS)
+            self.across(z, k).wait_recv()
+            self.stage[off, self.span(k)] = (
+                self.parts[z * YS + self.y, self.span(k)].astype(jnp.float32)
+                + self.ybuf[z, self.span(k)].astype(jnp.float32)
+            ).astype(jnp.bfloat16)
+            copy = self.along(off, k)
+            copy.start()
+            self.sent.append(copy)
+
+    def last(self, k):
+        self.across(self.z, k).wait_recv()
+        total = self.parts[self.c, self.span(k)].astype(jnp.float32) + self.ybuf[
+            self.z, self.span(k)
+        ].astype(jnp.float32)
+        for off in (1, 3, 2):
+            source = lax.rem(self.z + off, ZS)
+            block = self.zbuf.at[source, self.span(k)]
+            remote(
+                block,
+                block,
+                self.zs.at[off, k],
+                self.zr.at[source, k],
+                self.d,
+                source * YS + self.y,
+            ).wait_recv()
+            total = total + block[...].astype(jnp.float32)
+        self.out[self.span(k)] = total
+
+    def finish(self):
+        for copy in self.sent:
+            copy.wait_send()
+
+
+class ChipGather:
+    def __init__(self, out, sems, count):
+        self.out, self.count = out, count
+        self.cs, self.cr, self.xs, self.xr = sems
+        self.d, self.c, self.x, self.core, _, _ = place()
+        self.sent = []
+
+    @staticmethod
+    def scratch(count):
+        return [
+            pltpu.SemaphoreType.DMA((2, count)),
+            pltpu.SemaphoreType.DMA((2, count)),
+            pltpu.SemaphoreType.DMA((count,)),
+            pltpu.SemaphoreType.DMA((count,)),
+        ]
+
+    def to_core(self, far, j, src=None):
+        x = 1 - self.x if far else self.x
+        block = self.out.at[(x * 2 + self.core) * self.count + j]
+        return remote(
+            block if src is None else src,
+            block,
+            self.cs.at[far, j],
+            self.cr.at[far, j],
+            self.x * 2 + 1 - self.core,
+            self.c,
+        )
+
+    def to_x(self, j, src=None):
+        block = self.out.at[self.d * self.count + j]
+        return remote(
+            block if src is None else src,
+            block,
+            self.xs.at[j],
+            self.xr.at[j],
+            (1 - self.x) * 2 + self.core,
+            self.c,
+        )
+
+    def start(self, j, src=None):
+        for copy in (self.to_x(j, src), self.to_core(0, j, src)):
+            copy.start()
+            self.sent.append(copy)
+
+    def relay(self, j):
+        self.to_x(j).wait_recv()
+        copy = self.to_core(1, j)
+        copy.start()
+        self.sent.append(copy)
+
+    def last(self):
+        for far in (0, 1):
+            for j in range(self.count):
+                self.to_core(far, j).wait_recv()
+        for copy in self.sent:
+            copy.wait_send()
+
+
+class WeightGather:
+    def __init__(self, blocks, out, sems):
+        self.blocks, self.out = blocks, out
+        self.ps, self.pr, self.local_sem = sems[:3]
+        self.chip = ChipGather(out, sems[3:], PLANE)
+        self.d, self.c = self.chip.d, self.chip.c
+        self.sent = []
+
+    @staticmethod
+    def scratch():
+        return [
+            pltpu.SemaphoreType.DMA((PLANE,)),
+            pltpu.SemaphoreType.DMA((PLANE,)),
+            pltpu.SemaphoreType.DMA(()),
+        ] + ChipGather.scratch(PLANE)
+
+    def first(self):
+        self.local = pltpu.make_async_copy(
+            self.blocks.at[self.c], self.out.at[self.d * PLANE + self.c], self.local_sem
+        )
+        self.local.start()
+        for off in range(1, PLANE):
+            to = lax.rem(self.c + off, PLANE)
+            copy = remote(
+                self.blocks.at[to],
+                self.out.at[self.d * PLANE + self.c],
+                self.ps.at[off],
+                self.pr.at[self.c],
+                self.d,
+                to,
+            )
+            copy.start()
+            self.sent.append(copy)
+        self.chip.start(self.c, self.blocks.at[self.c])
+
+    def relay(self, off):
+        source = lax.rem(self.c + PLANE - off, PLANE)
+        block = self.out.at[self.d * PLANE + source]
+        remote(
+            block, block, self.ps.at[off], self.pr.at[source], self.d, source
+        ).wait_recv()
+        self.chip.start(source)
+
+    def relay_chip(self):
+        for off in range(PLANE):
+            self.chip.relay(lax.rem(self.c + off, PLANE))
+
+    def last(self):
+        self.chip.last()
+        for copy in self.sent:
+            copy.wait_send()
+        self.local.wait()
+
+
+def add_into(target, sources, rows, step=16):
+    @pl.loop(0, rows, step=step)
+    def _(r):
+        at = pl.ds(pl.multiple_of(r, step), step)
+        total = sources[0][at].astype(jnp.float32)
+        for source in sources[1:]:
+            total = total + source[at].astype(jnp.float32)
+        target[at] = total.astype(target.dtype)
+
+
+class ChipScatter:
+    def __init__(self, parts, cbuf, stage, xbuf, sems, count):
+        self.parts, self.count = parts, count
+        self.cbuf, self.stage, self.xbuf = cbuf, stage, xbuf
+        self.cs, self.cr, self.xs, self.xr = sems
+        self.d, self.c, self.x, self.core, _, _ = place()
+        self.sent = []
+
+    @staticmethod
+    def scratch(count, rows, width):
+        return [
+            pltpu.VMEM((2, count, rows, width), jnp.bfloat16),
+            pltpu.VMEM((count, rows, width), jnp.bfloat16),
+            pltpu.VMEM((count, rows, width), jnp.bfloat16),
+            pltpu.SemaphoreType.DMA((2, count)),
+            pltpu.SemaphoreType.DMA((2, count)),
+            pltpu.SemaphoreType.DMA((count,)),
+            pltpu.SemaphoreType.DMA((count,)),
+        ]
+
+    def to_core(self, far, j):
+        x = 1 - self.x if far else self.x
+        return remote(
+            self.parts.at[(x * 2 + 1 - self.core) * self.count + j],
+            self.cbuf.at[far, j],
+            self.cs.at[far, j],
+            self.cr.at[far, j],
+            self.x * 2 + 1 - self.core,
+            self.c,
+        )
+
+    def to_x(self, j):
+        return remote(
+            self.stage.at[j],
+            self.xbuf.at[j],
+            self.xs.at[j],
+            self.xr.at[j],
+            (1 - self.x) * 2 + self.core,
+            self.c,
+        )
+
+    def start(self, j):
+        for far in (1, 0):
+            copy = self.to_core(far, j)
+            copy.start()
+            self.sent.append(copy)
+
+    def relay(self, j):
+        self.to_core(1, j).wait_recv()
+        own = self.parts.at[((1 - self.x) * 2 + self.core) * self.count + j]
+        add_into(self.stage.at[j], [own, self.cbuf.at[1, j]], own.shape[0])
+        copy = self.to_x(j)
+        copy.start()
+        self.sent.append(copy)
+
+    def total(self, j, target):
+        self.to_core(0, j).wait_recv()
+        self.to_x(j).wait_recv()
+        own = self.parts.at[self.d * self.count + j]
+        add_into(target, [own, self.cbuf.at[0, j], self.xbuf.at[j]], own.shape[0])
+
+    def finish(self):
+        for copy in self.sent:
+            copy.wait_send()
+
+
+class WeightScatter:
+    def __init__(self, parts, out, bufs, sems):
+        self.stage = bufs[0]
+        self.ps, self.pr = sems[:2]
+        self.chip = ChipScatter(parts, *bufs[1:], sems[2:], PLANE)
+        self.out = out
+        self.d, self.c = self.chip.d, self.chip.c
+        self.sent = []
+
+    @staticmethod
+    def scratch(rows, width):
+        chip = ChipScatter.scratch(PLANE, rows, width)
+        return [
+            pltpu.VMEM((PLANE, rows, width), jnp.bfloat16),
+            *chip[:3],
+            pltpu.SemaphoreType.DMA((PLANE,)),
+            pltpu.SemaphoreType.DMA((PLANE,)),
+            *chip[3:],
+        ]
+
+    def first(self):
+        for off in range(1, PLANE + 1):
+            self.chip.start(lax.rem(self.c + off, PLANE))
+
+    def relay(self, off):
+        self.chip.relay(lax.rem(self.c + off, PLANE))
+
+    def send(self, off):
+        to = lax.rem(self.c + off, PLANE)
+        if off == PLANE:
+            self.chip.total(to, self.out.at[self.c])
+            return
+        self.chip.total(to, self.stage.at[to])
+        copy = remote(
+            self.stage.at[to],
+            self.out.at[self.c],
+            self.ps.at[off],
+            self.pr.at[self.c],
+            self.d,
+            to,
+        )
+        copy.start()
+        self.sent.append(copy)
+
+    def last(self):
+        for off in range(1, PLANE):
+            source = lax.rem(self.c + off, PLANE)
+            block = self.out.at[source]
+            remote(
+                block, block, self.ps.at[off], self.pr.at[source], self.d, source
+            ).wait_recv()
+        for copy in self.sent:
+            copy.wait_send()
+        self.chip.finish()
+
+
+def params(collective_id):
+    return pltpu.CompilerParams(
+        collective_id=collective_id, has_side_effects=True, vmem_limit_bytes=56 * 2**20
+    )
+
+
+ANY = pl.BlockSpec(memory_space=pl.ANY)
+VMEM = pl.BlockSpec(memory_space=pltpu.VMEM)
+CHUNKS = 4
+
+
+def opening_kernel(rows_ref, spots_ref, blocks_ref, rows_out, spots_out, blocks_out, *scratch):
+    spot_send, spot_recv, spot_local = scratch[:3]
+    gather = SequenceGather(rows_ref, rows_out, scratch[3:8], CHUNKS)
+    weights = WeightGather(blocks_ref, blocks_out, scratch[8:])
+    d, c, x, core, z, y = place()
+    greet(plane_peers(d, c) + chip_peers(d, c, x, core))
+    weights.first()
+    sent = []
+    local = pltpu.make_async_copy(spots_ref, spots_out.at[c], spot_local)
+    local.start()
+    for off in range(1, PLANE):
+        to = lax.rem(c + off, PLANE)
+        copy = remote(
+            spots_ref, spots_out.at[c], spot_send.at[off], spot_recv.at[c], d, to
+        )
+        copy.start()
+        sent.append(copy)
+    gather.first()
+    for off in range(1, PLANE):
+        weights.relay(off)
+    for k in range(CHUNKS):
+        gather.relay(k)
+    weights.relay_chip()
+    gather.last()
+    weights.last()
+    for off in range(1, PLANE):
+        source = lax.rem(c + off, PLANE)
+        block = spots_out.at[source]
+        remote(block, block, spot_send.at[off], spot_recv.at[source], d, source).wait_recv()
+    for copy in sent:
+        copy.wait_send()
+    local.wait()
+
+
+def opening(rows, spots, blocks):
+    return pl.pallas_call(
+        opening_kernel,
+        out_shape=(
+            jax.ShapeDtypeStruct((PLANE, *rows.shape), rows.dtype),
+            jax.ShapeDtypeStruct((PLANE, *spots.shape), spots.dtype),
+            jax.ShapeDtypeStruct((RANKS, *blocks.shape[1:]), blocks.dtype),
+        ),
+        in_specs=[ANY] * 3,
+        out_specs=(ANY,) * 3,
+        scratch_shapes=[
+            pltpu.SemaphoreType.DMA((PLANE,)),
+            pltpu.SemaphoreType.DMA((PLANE,)),
+            pltpu.SemaphoreType.DMA(()),
+            *SequenceGather.scratch(CHUNKS),
+            *WeightGather.scratch(),
+        ],
+        compiler_params=params(1),
+        name="opening",
+    )(rows, spots, blocks)
+
+
+def gather_kernel(rows_ref, rows_out, *scratch):
+    gather = SequenceGather(rows_ref, rows_out, scratch, CHUNKS)
+    d, c, x, core, z, y = place()
+    greet(
+        [(d, lax.rem(z + off, ZS) * YS + y) for off in range(1, ZS)] + [(d, z * YS + 1 - y)]
+    )
+    gather.first()
+    for k in range(CHUNKS):
+        gather.relay(k)
+    gather.last()
+
+
+def gather_rows(rows, collective_id):
+    return pl.pallas_call(
+        gather_kernel,
+        out_shape=jax.ShapeDtypeStruct((PLANE, *rows.shape), rows.dtype),
+        in_specs=[ANY],
+        out_specs=ANY,
+        scratch_shapes=SequenceGather.scratch(CHUNKS),
+        compiler_params=params(collective_id),
+        name="gather_rows",
+    )(rows)
+
+
+def scatter_kernel(parts_ref, out_ref, *scratch):
+    scatter = SequenceScatter(parts_ref, out_ref, *scratch[:3], scratch[3:], CHUNKS)
+    d, c, x, core, z, y = place()
+    greet(
+        [(d, lax.rem(z + off, ZS) * YS + y) for off in range(1, ZS)] + [(d, z * YS + 1 - y)]
+    )
+    scatter.first()
+    for k in range(CHUNKS):
+        scatter.relay(k)
+    for k in range(CHUNKS):
+        scatter.last(k)
+    scatter.finish()
+
+
+def scatter_rows(parts, collective_id):
+    return pl.pallas_call(
+        scatter_kernel,
+        out_shape=jax.ShapeDtypeStruct(parts.shape[1:], jnp.float32),
+        in_specs=[VMEM],
+        out_specs=VMEM,
+        scratch_shapes=SequenceScatter.scratch(*parts.shape[1:], CHUNKS),
+        compiler_params=params(collective_id),
+        name="scatter_rows",
+    )(parts)
+
+
+DOWN_PARTS = 4
+SCORE_SCALE = 1.0 / math.sqrt(HEAD_SIZE)
+GROUP = QUERY_HEADS // KEY_VALUE_HEADS
+PAIRS = GROUP // 2
+
+
+def times_rows(left, right):
+    return lax.dot_general(
+        left, right, (((1,), (1,)), ((), ())), preferred_element_type=jnp.float32
+    )
+
+
+def down_kernel(rows_ref, down_ref, rows_out, down_out, *scratch):
+    down_local = scratch[0]
+    gather = SequenceGather(rows_ref, rows_out, scratch[1:6], CHUNKS)
+    down = ChipGather(down_out, scratch[6:], DOWN_PARTS)
+    d, c, x, core, z, y = place()
+    greet(plane_peers(d, c) + chip_peers(d, c, x, core))
+    local = pltpu.make_async_copy(
+        down_ref, down_out.at[pl.ds(d * DOWN_PARTS, DOWN_PARTS)], down_local
+    )
+    local.start()
+    gather.first()
+    for j in range(DOWN_PARTS):
+        down.start(j, down_ref.at[j])
+    for k in range(CHUNKS):
+        gather.relay(k)
+    for j in range(DOWN_PARTS):
+        down.relay(j)
+    gather.last()
+    down.last()
+    local.wait()
+
+
+def gather_with_down(rows, down, collective_id):
+    return pl.pallas_call(
+        down_kernel,
+        out_shape=(
+            jax.ShapeDtypeStruct((PLANE, *rows.shape), rows.dtype),
+            jax.ShapeDtypeStruct((4 * DOWN_PARTS, *down.shape[1:]), down.dtype),
+        ),
+        in_specs=[ANY] * 2,
+        out_specs=(ANY,) * 2,
+        scratch_shapes=[
+            pltpu.SemaphoreType.DMA(()),
+            *SequenceGather.scratch(CHUNKS),
+            *ChipGather.scratch(DOWN_PARTS),
+        ],
+        compiler_params=params(collective_id),
+        name="gather_with_down",
+    )(rows, down)
+
+
+class PlaneExchange:
+    def __init__(self, blocks, out, sems):
+        self.blocks, self.out = blocks, out
+        self.ps, self.pr, self.local_sem = sems
+        self.d, self.c = lax.axis_index("dp"), lax.axis_index("ctx")
+        self.sent = []
+
+    @staticmethod
+    def scratch():
+        return [
+            pltpu.SemaphoreType.DMA((PLANE,)),
+            pltpu.SemaphoreType.DMA((PLANE,)),
+            pltpu.SemaphoreType.DMA(()),
+        ]
+
+    def send(self, off):
+        to = lax.rem(self.c + off, PLANE)
+        if off % PLANE == 0:
+            self.local = pltpu.make_async_copy(
+                self.blocks.at[to], self.out.at[self.c], self.local_sem
+            )
+            self.local.start()
+            return
+        copy = remote(
+            self.blocks.at[to],
+            self.out.at[self.c],
+            self.ps.at[off],
+            self.pr.at[self.c],
+            self.d,
+            to,
+        )
+        copy.start()
+        self.sent.append(copy)
+
+    def arrive(self, off):
+        if off % PLANE == 0:
+            self.local.wait()
+            return
+        source = lax.rem(self.c + PLANE - off, PLANE)
+        block = self.out.at[source]
+        remote(
+            block, block, self.ps.at[off], self.pr.at[source], self.d, source
+        ).wait_recv()
+
+    def finish(self):
+        for copy in self.sent:
+            copy.wait_send()
+
+
+def probabilities(query, keys, spot, start, key_spots):
+    scores = times_rows(query, keys) * SCORE_SCALE
+    masked = jnp.where((key_spots <= spot) & (key_spots >= start), scores, masked_score)
+    exponent = jnp.exp(masked - jnp.max(masked, axis=-1, keepdims=True))
+    return exponent * (1.0 / jnp.sum(exponent, axis=-1, keepdims=True))
+
+
+def attention_kernel(
+    query_ref,
+    key_ref,
+    value_ref,
+    spot_ref,
+    start_ref,
+    key_spot_ref,
+    blocks_ref,
+    out_rows_ref,
+    mixed_out,
+    blocks_out,
+    out_rows_out,
+    *scratch,
+):
+    mixed_stage = scratch[0]
+    exchange = PlaneExchange(mixed_stage, mixed_out, scratch[1:4])
+    weights = WeightGather(blocks_ref, blocks_out, scratch[4:11])
+    d, c, x, core, z, y = place()
+    gather = SequenceGather(
+        out_rows_ref, out_rows_out.at[pl.ds(d * PLANE, PLANE)], scratch[11:16], 1
+    )
+    chip = ChipGather(out_rows_out, scratch[16:], PLANE)
+    greet(plane_peers(d, c) + chip_peers(d, c, x, core))
+    gather.first()
+    chip.start(c, out_rows_ref)
+    weights.first()
+    for step in range(1, PLANE + 1):
+        block = lax.rem(c + step, PLANE)
+
+        @pl.loop(0, PAIRS)
+        def _(pair):
+            halves = []
+            for half in range(2):
+                probs = probabilities(
+                    query_ref[block, pair, half],
+                    key_ref[...],
+                    spot_ref[block],
+                    start_ref[block],
+                    key_spot_ref[...],
+                )
+                halves.append(
+                    jnp.dot(
+                        probs.astype(jnp.bfloat16),
+                        value_ref[...],
+                        preferred_element_type=jnp.float32,
+                    ).astype(jnp.bfloat16)
+                )
+            mixed_stage[block, pair] = jnp.concatenate(halves, axis=1)
+
+        exchange.send(step)
+        if step == 1:
+            gather.relay(0)
+            for off in range(1, ZS):
+                chip.start(lax.rem(z + off, ZS) * YS + y)
+        if step < PLANE:
+            weights.relay(step)
+    gather.last()
+    for other in range(ZS):
+        chip.start(other * YS + 1 - y)
+    for off in range(PLANE):
+        chip.relay(lax.rem(c + off, PLANE))
+    weights.relay_chip()
+    for off in range(1, PLANE + 1):
+        exchange.arrive(off)
+    chip.last()
+    weights.last()
+    exchange.finish()
+
+
+def attention(query, keys, values, spots, starts, key_spots, blocks, out_rows):
+    exchanged = jax.ShapeDtypeStruct(
+        (PLANE, PAIRS, query.shape[3], 2 * HEAD_SIZE), jnp.bfloat16
+    )
+    return pl.pallas_call(
+        attention_kernel,
+        out_shape=(
+            exchanged,
+            jax.ShapeDtypeStruct((RANKS, *blocks.shape[1:]), blocks.dtype),
+            jax.ShapeDtypeStruct((RANKS, *out_rows.shape), out_rows.dtype),
+        ),
+        in_specs=[VMEM] * 6 + [ANY] * 2,
+        out_specs=(VMEM, ANY, ANY),
+        scratch_shapes=[
+            pltpu.VMEM(exchanged.shape, jnp.bfloat16),
+            *PlaneExchange.scratch(),
+            *WeightGather.scratch(),
+            *SequenceGather.scratch(1),
+            *ChipGather.scratch(PLANE),
+        ],
+        compiler_params=params(2),
+        name="attention",
+    )(query, keys, values, spots, starts, key_spots, blocks, out_rows)
+
+
+def attention_back_kernel(
+    query_ref,
+    key_ref,
+    value_ref,
+    spot_ref,
+    start_ref,
+    key_spot_ref,
+    mixed_ref,
+    parts_ref,
+    down_ref,
+    query_out,
+    key_out,
+    value_out,
+    out_ref,
+    down_out,
+    *scratch,
+):
+    mixed_all = scratch[0]
+    exchange = PlaneExchange(mixed_ref, mixed_all, scratch[1:4])
+    weights = WeightScatter(parts_ref, out_ref, scratch[4:8], scratch[8:14])
+    down = ChipScatter(down_ref, *scratch[14:17], scratch[17:], DOWN_PARTS)
+    d, c, x, core, z, y = place()
+    greet(plane_peers(d, c) + chip_peers(d, c, x, core))
+    for off in range(1, PLANE + 1):
+        exchange.send(off)
+    weights.first()
+    for j in range(DOWN_PARTS):
+        down.start(j)
+    key_out[...] = jnp.zeros_like(key_out)
+    value_out[...] = jnp.zeros_like(value_out)
+    for step in range(PLANE):
+        block = lax.rem(c + PLANE - step, PLANE)
+        exchange.arrive(step)
+
+        @pl.loop(0, PAIRS)
+        def _(pair):
+            for half in range(2):
+                query = query_ref[block, pair, half]
+                grad = mixed_all[block, pair][:, half * HEAD_SIZE : (half + 1) * HEAD_SIZE]
+                probs = probabilities(
+                    query, key_ref[...], spot_ref[block], start_ref[block], key_spot_ref[...]
+                )
+                grad_probs = times_rows(grad, value_ref[...])
+                delta = jnp.sum(probs * grad_probs, axis=-1, keepdims=True)
+                grad_scores = (probs * (grad_probs - delta) * SCORE_SCALE).astype(jnp.bfloat16)
+                query_out[block, pair, half] = jnp.dot(
+                    grad_scores, key_ref[...], preferred_element_type=jnp.float32
+                )
+                key_out[...] += transposed_times(grad_scores, query)
+                value_out[...] += transposed_times(probs.astype(jnp.bfloat16), grad)
+
+        weights.relay(step + 1)
+        if step >= 2:
+            weights.send(step - 1)
+    for off in (PLANE - 1, PLANE):
+        weights.send(off)
+    for j in range(DOWN_PARTS):
+        down.relay(j)
+    for j in range(DOWN_PARTS):
+        down.total(j, down_out.at[j])
+    weights.last()
+    down.finish()
+    exchange.finish()
+
+
+def attention_back(query, keys, values, spots, starts, key_spots, mixed, parts, down):
+    return pl.pallas_call(
+        attention_back_kernel,
+        out_shape=(
+            jax.ShapeDtypeStruct(query.shape, jnp.float32),
+            jax.ShapeDtypeStruct(keys.shape, jnp.float32),
+            jax.ShapeDtypeStruct(values.shape, jnp.float32),
+            jax.ShapeDtypeStruct((PLANE, *parts.shape[1:]), parts.dtype),
+            jax.ShapeDtypeStruct((DOWN_PARTS, *down.shape[1:]), jnp.float32),
+        ),
+        in_specs=[VMEM] * 9,
+        out_specs=(VMEM,) * 5,
+        scratch_shapes=[
+            pltpu.VMEM(mixed.shape, jnp.bfloat16),
+            *PlaneExchange.scratch(),
+            *WeightScatter.scratch(*parts.shape[1:]),
+            *ChipScatter.scratch(DOWN_PARTS, *down.shape[1:]),
+        ],
+        compiler_params=params(3),
+        name="attention_back",
+    )(query, keys, values, spots, starts, key_spots, mixed, parts, down)
+
+
+def closing_kernel(rows_ref, parts_ref, outs_ref, rows_out, out_ref, outs_out, *scratch):
+    scatter = SequenceScatter(rows_ref, rows_out, *scratch[:3], scratch[3:7], CHUNKS)
+    weights = WeightScatter(parts_ref, out_ref, scratch[7:11], scratch[11:17])
+    outs_sum = scratch[17]
+    chip = ChipScatter(outs_ref, *scratch[18:21], scratch[21:25], PLANE)
+    outs = SequenceScatter(outs_sum, outs_out, *scratch[25:28], scratch[28:], 1)
+    d, c, x, core, z, y = place()
+    greet(plane_peers(d, c) + chip_peers(d, c, x, core))
+    slots = [lax.rem(z + off, ZS) * YS + 1 - y for off in (2, 1, 3, 0)]
+    slots += [lax.rem(z + off, ZS) * YS + y for off in (2, 1, 3, 0)]
+    for j in slots:
+        chip.start(j)
+    weights.first()
+    scatter.first()
+    for j in slots:
+        chip.relay(j)
+    for off in range(1, PLANE + 1):
+        weights.relay(off)
+    for k in range(CHUNKS):
+        scatter.relay(k)
+    for off in range(1, PLANE + 1):
+        weights.send(off)
+    for i, j in enumerate(slots):
+        chip.total(j, outs_sum.at[j])
+        if i < ZS:
+            copy = outs.across(lax.rem(z + (2, 1, 3, 0)[i], ZS), 0)
+            copy.start()
+            outs.sent.append(copy)
+    outs.relay(0)
+    for k in range(CHUNKS):
+        scatter.last(k)
+    weights.last()
+    outs.last(0)
+    scatter.finish()
+    chip.finish()
+    outs.finish()
+
+
+def closing(rows, parts, outs):
+    return pl.pallas_call(
+        closing_kernel,
+        out_shape=(
+            jax.ShapeDtypeStruct(rows.shape[1:], jnp.float32),
+            jax.ShapeDtypeStruct((PLANE, *parts.shape[1:]), parts.dtype),
+            jax.ShapeDtypeStruct(outs.shape[1:], jnp.float32),
+        ),
+        in_specs=[VMEM] * 3,
+        out_specs=(VMEM,) * 3,
+        scratch_shapes=[
+            *SequenceScatter.scratch(*rows.shape[1:], CHUNKS),
+            *WeightScatter.scratch(*parts.shape[1:]),
+            pltpu.VMEM((PLANE, *outs.shape[1:]), jnp.bfloat16),
+            *ChipScatter.scratch(PLANE, *outs.shape[1:]),
+            *SequenceScatter.scratch(*outs.shape[1:], 1),
+        ],
+        compiler_params=params(4),
+        name="closing",
+    )(rows, parts, outs)
 
 
 def body(
@@ -408,9 +1335,231 @@
     )
 
 
+def tensor_parallel(
+    layer_in,
+    positions,
+    doc_starts,
+    out_grad,
+    norm_gains,
+    norm_gains_m,
+    norm_gains_v,
+    w_query,
+    w_query_m,
+    w_query_v,
+    key_value_weight,
+    key_value_first_moment,
+    key_value_second_moment,
+    w_out,
+    w_out_m,
+    w_out_v,
+    w_gate_up,
+    w_gate_up_m,
+    w_gate_up_v,
+    w_down,
+    w_down_m,
+    w_down_v,
+):
+    low = jnp.bfloat16
+    own_tokens, width = layer_in.shape
+    seq_len = own_tokens * PLANE
+    group = GROUP
+    group_width = group * HEAD_SIZE
+    ff_part = FF // PLANE
+    ff_own = FF // RANKS
+    rows = w_query.shape[0]
+
+    gains_low = norm_gains.astype(low)
+    small = jnp.broadcast_to(
+        jnp.pad(gains_low.T, ((0, 0), (0, 126)))[None], (PLANE, rows, 128)
+    )
+    attention_blocks = jnp.concatenate(
+        [
+            w_query.astype(low).reshape(rows, PLANE, group_width).transpose(1, 0, 2),
+            key_value_weight.astype(low)
+            .reshape(rows, 2, PLANE, HEAD_SIZE)
+            .transpose(2, 0, 1, 3)
+            .reshape(PLANE, rows, 2 * HEAD_SIZE),
+            small,
+        ],
+        axis=2,
+    )
+    feed_blocks = (
+        w_gate_up.astype(low)
+        .reshape(rows, 2, 4, PLANE, ff_own)
+        .transpose(3, 0, 1, 2, 4)
+        .reshape(PLANE, rows, 2 * ff_part)
+    )
+    spots = jnp.broadcast_to(positions[None, :], (8, own_tokens))
+    rows_all, spots_all, attention_all = opening(layer_in, spots, attention_blocks)
+    attention_all = attention_all.reshape(width, -1)
+    qkv_width = group_width + 2 * HEAD_SIZE
+    qkv_weight = attention_all[:, :qkv_width]
+    gain_one = attention_all[:, qkv_width].astype(jnp.float32)
+    gain_two = attention_all[:, qkv_width + 1].astype(jnp.float32)
+    places = spots_all[:, 0, :].reshape(seq_len)
+    starts = jnp.max(
+        jnp.where(doc_starts[0][None, :] <= places[:, None], doc_starts[0][None, :], 0), axis=1
+    )
+    normed_all, unused = norm_forward(rows_all.reshape(seq_len, width).astype(jnp.float32))
+    input_one = (normed_all * gain_one).astype(low)
+    projected = jnp.dot(input_one, qkv_weight, preferred_element_type=jnp.float32)
+    cosine_table, sine_table = rope_tables(places, HEAD_SIZE)
+    query_rows = (
+        apply_rotation(
+            projected[:, :group_width].reshape(seq_len, group, HEAD_SIZE),
+            cosine_table,
+            sine_table,
+        )
+        .astype(low)
+        .reshape(PLANE, own_tokens, PAIRS, 2, HEAD_SIZE)
+        .transpose(0, 2, 3, 1, 4)
+    )
+    key_rows = apply_rotation(
+        projected[:, None, group_width : group_width + HEAD_SIZE], cosine_table, sine_table
+    ).astype(low)[:, 0]
+    value_rows = projected[:, group_width + HEAD_SIZE :].astype(low)
+    token_spots = places.reshape(PLANE, own_tokens, 1)
+    token_starts = starts.reshape(PLANE, own_tokens, 1)
+    mixed_parts, feed_all, out_all = attention(
+        query_rows,
+        key_rows,
+        value_rows,
+        token_spots,
+        token_starts,
+        places[None, :],
+        feed_blocks,
+        w_out.astype(low),
+    )
+    mixed = mixed_parts.transpose(2, 0, 1, 3).reshape(own_tokens, width)
+    out_weight = out_all.reshape(width, width)
+    branch = jnp.dot(mixed, out_weight, preferred_element_type=jnp.float32)
+
+    layer_rows = layer_in.astype(jnp.float32)
+    middle = layer_rows + branch
+    normed_two, inverse_two = norm_forward(middle)
+    input_two_all, down_all = gather_with_down(
+        (normed_two * gain_two).astype(low),
+        w_down.astype(low).reshape(DOWN_PARTS, -1, width),
+        6,
+    )
+    input_two = input_two_all.reshape(seq_len, width)
+    grads_all = gather_rows(out_grad, 5)
+    feed_weight = feed_all.reshape(width, 2 * ff_part)
+    down_weight = down_all.reshape(ff_part, width)
+    gate_up = jnp.dot(input_two, feed_weight, preferred_element_type=jnp.float32)
+    gate_part = gate_up[:, :ff_part]
+    up_part = gate_up[:, ff_part:]
+    sigmoid_gate = jax.nn.sigmoid(gate_part)
+    silu_gate = gate_part * sigmoid_gate
+    hidden = (silu_gate * up_part).astype(low)
+    down_parts = jnp.dot(hidden, down_weight, preferred_element_type=jnp.float32).astype(low)
+    down_sum = scatter_rows(down_parts.reshape(PLANE, own_tokens, width), 7)
+    layer_out = (middle + down_sum).astype(low)
+
+    out_grads = grads_all.reshape(seq_len, width)
+    grad_hidden = times_transposed(out_grads, down_weight)
+    grad_gate = grad_hidden * up_part * sigmoid_gate * (1.0 + gate_part * (1.0 - sigmoid_gate))
+    grad_up = grad_hidden * silu_gate
+    grad_gate_up = jnp.concatenate([grad_gate, grad_up], axis=1).astype(low)
+    normed_parts = times_transposed(grad_gate_up, feed_weight).astype(low)
+    grad_normed_two = scatter_rows(normed_parts.reshape(PLANE, own_tokens, width), 8)
+    down_term = transposed_times(hidden, out_grads).astype(low)
+    feed_term = transposed_times(input_two, grad_gate_up).astype(low)
+    grad_norm_two, unused = norm_backward(grad_normed_two, normed_two, inverse_two, gain_two)
+    grad_middle = out_grad.astype(jnp.float32) + grad_norm_two
+    grad_middle_low = grad_middle.astype(low)
+    out_term = transposed_times(mixed, grad_middle_low).astype(low)
+    grad_mixed = (
+        times_transposed(grad_middle_low, out_weight)
+        .astype(low)
+        .reshape(own_tokens, PLANE, PAIRS, 2 * HEAD_SIZE)
+        .transpose(1, 2, 0, 3)
+    )
+    grad_query, grad_key, grad_value, feed_grad, down_grad = attention_back(
+        query_rows,
+        key_rows,
+        value_rows,
+        token_spots,
+        token_starts,
+        places[None, :],
+        grad_mixed,
+        feed_term.reshape(RANKS, rows, 2 * ff_part),
+        down_term.reshape(4 * DOWN_PARTS, -1, width),
+    )
+    gate_up_grad = (
+        feed_grad.reshape(PLANE, rows, 2, 4, ff_own)
+        .transpose(1, 2, 3, 0, 4)
+        .reshape(rows, 2 * FF)
+        .astype(jnp.float32)
+    )
+    down_grad = down_grad.reshape(w_down.shape)
+    grad_query = grad_query.transpose(0, 3, 1, 2, 4).reshape(seq_len, group, HEAD_SIZE)
+    grad_qkv = jnp.concatenate(
+        [
+            reverse_rotation(grad_query, cosine_table, sine_table).reshape(seq_len, group_width),
+            reverse_rotation(grad_key[:, None], cosine_table, sine_table)[:, 0],
+            grad_value,
+        ],
+        axis=1,
+    ).astype(low)
+    one_parts = times_transposed(grad_qkv, qkv_weight).astype(low)
+    qkv_term = transposed_times(input_one, grad_qkv).astype(low)
+    grad_normed_one, qkv_grad, out_weight_grad = closing(
+        one_parts.reshape(PLANE, own_tokens, width),
+        qkv_term.reshape(RANKS, rows, qkv_width),
+        out_term.reshape(RANKS, rows, width),
+    )
+    normed_one, inverse_one = norm_forward(layer_rows)
+    grad_norm_one, unused = norm_backward(grad_normed_one, normed_one, inverse_one, gain_one)
+    in_grad = grad_middle + grad_norm_one
+    qkv_grad = qkv_grad.astype(jnp.float32)
+    query_grad = qkv_grad[:, :, :group_width].transpose(1, 0, 2).reshape(w_query.shape)
+    keyval_grad = (
+        qkv_grad[:, :, group_width:]
+        .reshape(PLANE, rows, 2, HEAD_SIZE)
+        .transpose(1, 2, 0, 3)
+        .reshape(key_value_weight.shape)
+    )
+    def low_times(weight, grad):
+        return jnp.sum(weight.astype(low).astype(jnp.float32) * grad, axis=1)
+
+    gains_grad = jnp.stack(
+        [
+            low_times(w_query, query_grad) + low_times(key_value_weight, keyval_grad),
+            low_times(w_gate_up, gate_up_grad),
+        ]
+    ) / gains_low.astype(jnp.float32)
+
+    rates = rates_for(seq_len)
+    return (
+        layer_out,
+        in_grad,
+        gains_grad,
+        *adamw(norm_gains, gains_grad, norm_gains_m, norm_gains_v, rates[0], 0.0),
+        query_grad,
+        *adamw(w_query, query_grad, w_query_m, w_query_v, rates[1], weight_decay),
+        keyval_grad,
+        *adamw(
+            key_value_weight,
+            keyval_grad,
+            key_value_first_moment,
+            key_value_second_moment,
+            rates[2],
+            weight_decay,
+        ),
+        out_weight_grad,
+        *adamw(w_out, out_weight_grad, w_out_m, w_out_v, rates[3], weight_decay),
+        gate_up_grad,
+        *adamw(w_gate_up, gate_up_grad, w_gate_up_m, w_gate_up_v, rates[4], weight_decay),
+        down_grad,
+        *adamw(w_down, down_grad, w_down_m, w_down_v, rates[5], weight_decay),
+    )
+
+
 def solution(mesh):
+    planned = tensor_parallel if dict(mesh.shape) == {"dp": 2 * XS, "ctx": ZS * YS} else body
     return jax.shard_map(
-        body,
+        planned,
         mesh=mesh,
         in_specs=(
             P(("dp", "ctx"), None),

time: 6380 us -> 827 us (0.13)
  waiting for transfers between devices: 5920 us -> 0 us
  Pallas kernels: 0 us -> 637 us
  matrix products: 270 us -> 92.1 us
  blocking collectives: 85.7 us -> 0 us
    unnamed x19 -> x0, waiting for transfers between devices: 2930 us -> none
    reduce_scatter x4 -> x0, waiting for transfers between devices: 2300 us -> none  [the longest x1 1400 us: body(): lax.psum_scatter(transposed_times(hidden, out_grad), ('dp', 'ctx'), scatt...]
    all_gather x7 -> x0, waiting for transfers between devices: 688 us -> none  [the longest x1 353 us: body(): lax.all_gather(gate_up_low, ('dp', 'ctx'), axis=0, tiled=True)]
    pallas_call x0 -> x8, Pallas kernels: none -> 637 us  [the longest x1 128 us: attention(): pl.pallas_call(attention_kernel, out_shape=(exchanged, jax.ShapeDtypeStru...]
    all_gather x2 -> x0, blocking collectives: 85.7 us -> none  [the longest x1 69.4 us: body(): lax.all_gather(norm_gains.astype(jnp.bfloat16), ('dp', 'ctx'), axis=1, ti...]
    dot_general x19 -> x4, matrix products: 108 us -> 27.5 us  [the longest x1 14.6 us: tensor_parallel(): jnp.dot(input_two, feed_weight, preferred_element_type=jnp.float32)]
  transfers between devices with their start and end apart: 15 -> 0, of which waited for: 14 -> 0; matrix products, arithmetic and copies ran while one was open for 4% -> 0% of each run, Pallas kernels for 0% -> 0%
where the time goes in v1:
time: 827 us; the launch traced here: 821 us
  Pallas kernels  637 us (77%)
  matrix products  92.1 us (11%)
  other arithmetic  52.6 us (6%)
  local copies, waits for them, and re-layouts  37.3 us (5%)
    pallas_call x1, Pallas kernels, attention(): pl.pallas_call(attention_kernel, out_shape=(exchanged, jax.ShapeDtypeStru...  128 us
    pallas_call x2, Pallas kernels, scatter_rows(): pl.pallas_call(scatter_kernel, out_shape=jax.ShapeDtypeStruct(parts.shape...  117 us
    pallas_call x1, Pallas kernels, closing(): pl.pallas_call(closing_kernel, out_shape=(jax.ShapeDtypeStruct(rows.shape...  99.7 us
    pallas_call x1, Pallas kernels, attention_back(): pl.pallas_call(attention_back_kernel, out_shape=(jax.ShapeDtypeStruct(que...  83.5 us
    pallas_call x1, Pallas kernels, gather_with_down(): pl.pallas_call(down_kernel, out_shape=(jax.ShapeDtypeStruct((PLANE, *rows...  73.6 us
    pallas_call x1, Pallas kernels, opening(): pl.pallas_call(opening_kernel, out_shape=(jax.ShapeDtypeStruct((PLANE, *r...  72 us
    pallas_call x1, Pallas kernels, gather_rows(): pl.pallas_call(gather_kernel, out_shape=jax.ShapeDtypeStruct((PLANE, *row...  62.6 us
    dot_general x4, matrix products, transposed_times(): lax.dot_general(left, right, (((0,), (0,)), ((), ())), preferred_element_...  33.5 us

profile of v1, /device:TPU:0, one launch (start us, length us, event | category | flops | bytes accessed | tf_op | source)
XLA Modules:
  0.0 820.7 jit_solution(1687780451547940249)
XLA Ops:
  5.6 72.0 %opening.1 = (bf16[8,128,2048]{2,1,0:T(8,128)(2,1)}, s32[8,8,128]{2,1,0:T(8,128)}, bf16[32,64,512]{2,1,0:T(8,128)(2,1)}) custom-call(bf16[128,2048]{1,0:T(8,128)(2,1)} %rows_ref.2, s32[8,128]{1,0:T(8,128)} %broadcast_in_dim.18.spots_ref, bf16[8,64,512]{2,1,0:T(8,128)(2,1)} %pad_maximum_fusion.4.blocks_ref), custom_call_target="tpu_custom_call" | custom-call | tf_op jit(solution)/shard_map/opening/pallas_call | solution.py:612
  80.3 3.2 multiply_reduce_fusion
  107.6 127.9 %attention.1 = (bf16[8,2,128,128]{3,2,1,0:T(8,128)(2,1)}, bf16[32,64,2048]{2,1,0:T(8,128)(2,1)}, bf16[32,64,2048]{2,1,0:T(8,128)(2,1)}) custom-call(bf16[8,2,2,128,64]{4,3,2,1,0:T(8,128)(2,1)} %maximum_bitcast_fusion.query_ref, bf16[1024,64]{1,0:T(8,128)(2,1)} %pad_maximum_fusion.8.key_ref, bf16[1024,64]{1,0:T(8,128)(2,1)} %copy.139.value_ref, ...), custom_call_target="tpu_custom_call" | custom-call | tf_op jit(solution)/shard_map/attention/pallas_call | solution.py:865
  236.8 4.8 multiply_reduce_fusion.3
  245.7 73.6 %gather_with_down.1 = (bf16[8,128,2048]{2,1,0:T(8,128)(2,1)}, bf16[16,64,2048]{2,1,0:T(8,128)(2,1)}) custom-call(bf16[128,2048]{1,0:T(8,128)(2,1)} %multiply_convert_fusion.1.rows_ref, bf16[4,64,2048]{2,1,0:T(8,128)(2,1)} %bitcast.145), custom_call_target="tpu_custom_call" | custom-call | tf_op jit(solution)/shard_map/gather_with_down/pallas_call | solution.py:718
  319.3 14.6 %fusion.53 = f32[1024,2048]{1,0:T(8,128)} fusion(bf16[1024,2048]{1,0:T(8,128)(2,1)} %bitcast.184, bf16[2048,2048]{1,0:T(8,128)(2,1)} %bitcast.182), kind=kOutput, calls=%fused_computation.122 | convolution fusion | flops 8589934592 | bytes 20971520 | tf_op jit(solution)/shard_map/dot_general | solution.py:1449
  333.8 62.6 %gather_rows.1 = bf16[8,128,2048]{2,1,0:T(8,128)(2,1)} custom-call(bf16[128,2048]{1,0:T(8,128)(2,1)} %rows_ref.3), custom_call_target="tpu_custom_call" | custom-call | tf_op jit(solution)/shard_map/gather_rows/pallas_call | solution.py:646
  396.4 11.2 %fusion.5 = (bf16[1024,1024]{1,0:T(8,128)(2,1)}, bf16[1024,1024]{1,0:T(8,128)(2,1)}, bf16[1024,1024]{1,0:T(8,128)(2,1)S(1)}) fusion(f32[1024,2048]{1,0:T(8,128)} %fusion.53, bf16[1024,2048]{1,0:T(8,128)(2,1)S(1)} %bitcast.186, bf16[1024,2048]{1,0:T(8,128)(2,1)} %bitcast.146), kind=kOutput, calls=%fused_computation.13 | convolution fusion | flops 4310695936 | bytes 23068672 | tf_op jit(solution)/shard_map/dot_general | solution.py:99
  407.6 6.2 convolution_convert_fusion.5
  413.9 62.9 %scatter_rows.2 = f32[128,2048]{1,0:T(8,128)} custom-call(bf16[8,128,2048]{2,1,0:T(8,128)(2,1)} %bitcast.143), custom_call_target="tpu_custom_call" | custom-call | tf_op jit(solution)/shard_map/scatter_rows/pallas_call | solution.py:672
  476.8 12.6 %convolution_convert_fusion.3 = bf16[1024,2048]{1,0:T(8,128)(2,1)} fusion(bf16[2048,2048]{1,0:T(8,128)(2,1)} %bitcast.183, bf16[1024,1024]{1,0:T(8,128)(2,1)S(1)} %copy-done.43, bf16[1024,1024]{1,0:T(8,128)(2,1)S(1)} %copy-done.42), kind=kOutput, calls=%fused_computation.22 | convolution fusion | flops 8600420352 | bytes 16777216 | tf_op jit(solution)/shard_map/dot_general | solution.py:99
  489.4 54.6 %scatter_rows.3 = f32[128,2048]{1,0:T(8,128)} custom-call(bf16[8,128,2048]{2,1,0:T(8,128)(2,1)} %bitcast.144), custom_call_target="tpu_custom_call" | custom-call | tf_op jit(solution)/shard_map/scatter_rows/pallas_call | solution.py:672
  547.9 6.0 convolution_convert_fusion.1
  553.9 12.1 %convolution_convert_fusion = bf16[2048,2048]{1,0:T(8,128)(2,1)} fusion(bf16[1024,2048]{1,0:T(8,128)(2,1)S(1)} %bitcast.185, bf16[1024,1024]{1,0:T(8,128)(2,1)S(1)} %copy-done.44, bf16[1024,1024]{1,0:T(8,128)(2,1)S(1)} %copy-done.42), kind=kOutput, calls=%fused_computation.4 | convolution fusion | flops 8602517504 | bytes 16777216 | tf_op jit(solution)/shard_map/dot_general | solution.py:105
  570.2 9.4 %convolution_convert_fusion.4 = bf16[1024,2048]{1,0:T(8,128)(2,1)} fusion(bf16[1024,1024]{1,0:T(8,128)(2,1)} %copy-done.41, bf16[1024,2048]{1,0:T(8,128)(2,1)} %bitcast.147), kind=kOutput, calls=%fused_computation.23 | convolution fusion | flops 4297064448 | bytes 10485760 | tf_op jit(solution)/shard_map/dot_general | solution.py:105
  579.6 83.5 %attention_back.1 = (f32[8,2,2,128,64]{4,3,2,1,0:T(8,128)}, f32[1024,64]{1,0:T(8,128)}, f32[1024,64]{1,0:T(8,128)}, bf16[8,64,2048]{2,1,0:T(8,128)(2,1)}, f32[4,64,2048]{2,1,0:T(8,128)}) custom-call(bf16[8,2,2,128,64]{4,3,2,1,0:T(8,128)(2,1)} %maximum_bitcast_fusion.query_ref, bf16[1024,64]{1,0:T(8,128)(2,1)} %pad_maximum_fusion.8.key_ref, ...), custom_call_target="tpu_custom_call" | custom-call | tf_op jit(solution)/shard_map/attention_back/pallas_call | solution.py:952
  672.6 6.0 convolution_convert_fusion.6
  678.6 4.4 convolution_convert_fusion.2
  683.1 99.7 %closing.1 = (f32[128,2048]{1,0:T(8,128)}, bf16[8,64,384]{2,1,0:T(8,128)(2,1)}, f32[64,2048]{1,0:T(8,128)}) custom-call(bf16[8,128,2048]{2,1,0:T(8,128)(2,1)} %bitcast.142, bf16[32,64,384]{2,1,0:T(8,128)(2,1)} %bitcast.156, bf16[32,64,2048]{2,1,0:T(8,128)(2,1)} %bitcast.128), custom_call_target="tpu_custom_call" | custom-call | tf_op jit(solution)/shard_map/closing/pallas_call | solution.py:1013
  784.0 3.5 multiply_subtract_fusion.2
  790.7 6.0 reshape.373
  796.7 4.8 copy.133
  805.1 6.4 multiply_subtract_fusion
  814.1 4.0 multiply_subtract_fusion.1
  (176 shorter events, 66.7 us)
Async XLA Ops:
  90.3 7.9 copy-start.38
  106.9 129.9 %copy-start.3 = (bf16[128,2048]{1,0:T(8,128)(2,1)S(1)}, bf16[128,2048]{1,0:T(8,128)(2,1)}, u32[]{:S(2)}) copy-start(bf16[128,2048]{1,0:T(8,128)(2,1)} %rows_ref.2) | copy-start | bytes 1572868
  333.8 62.6 %copy-start.40 = (bf16[16,64,2048]{2,1,0:T(8,128)(2,1)S(1)}, bf16[16,64,2048]{2,1,0:T(8,128)(2,1)}, u32[]{:S(2)}) copy-start(bf16[16,64,2048]{2,1,0:T(8,128)(2,1)} %get-tuple-element.49) | copy-start | bytes 12582916
  413.9 62.9 %copy-start.42 = (bf16[1024,1024]{1,0:T(8,128)(2,1)S(1)}, bf16[1024,1024]{1,0:T(8,128)(2,1)}, u32[]{:S(2)}) copy-start(bf16[1024,1024]{1,0:T(8,128)(2,1)} %get-tuple-element.77) | copy-start | bytes 6291460
  413.9 62.9 %copy-start.43 = (bf16[1024,1024]{1,0:T(8,128)(2,1)S(1)}, bf16[1024,1024]{1,0:T(8,128)(2,1)}, u32[]{:S(2)}) copy-start(bf16[1024,1024]{1,0:T(8,128)(2,1)} %get-tuple-element.78) | copy-start | bytes 6291460
  489.4 56.1 %copy-start.8 = (f32[128,2048]{1,0:T(8,128)S(1)}, f32[128,2048]{1,0:T(8,128)}, u32[]{:S(2)}) copy-start(f32[128,2048]{1,0:T(8,128)} %scatter_rows.2) | copy-start | bytes 3145732
  489.4 56.1 %copy-start.14 = (bf16[128,2048]{1,0:T(8,128)(2,1)S(1)}, bf16[128,2048]{1,0:T(8,128)(2,1)}, u32[]{:S(2)}) copy-start(bf16[128,2048]{1,0:T(8,128)(2,1)} %rows_ref.3) | copy-start | bytes 1572868
  547.9 18.1 %slice-start = ((s8[8388608]{0:T(1024)(128)(4,1)}), s8[4194304]{0:T(1024)(128)(4,1)S(1)}, s32[]{:S(2)}) async-start(s8[8388608]{0:T(1024)(128)(4,1)} %bitcast.125), calls=%async_computation | async-start | bytes 8388608
  553.9 12.1 %slice-start.1 = ((s8[8388608]{0:T(1024)(128)(4,1)}), s8[4194304]{0:T(1024)(128)(4,1)S(1)}, s32[]{:S(2)}) async-start(s8[8388608]{0:T(1024)(128)(4,1)} %bitcast.125), calls=%async_computation.1 | async-start | bytes 8388608
  683.0 101.0 %copy-start.16 = (f32[64,2048]{1,0:T(8,128)S(1)}, f32[64,2048]{1,0:T(8,128)}, u32[]{:S(2)}) copy-start(f32[64,2048]{1,0:T(8,128)} %param.29) | copy-start | bytes 1572868
  683.0 101.0 %copy-start.18 = (f32[64,2048]{1,0:T(8,128)S(1)}, f32[64,2048]{1,0:T(8,128)}, u32[]{:S(2)}) copy-start(f32[64,2048]{1,0:T(8,128)} %param.35) | copy-start | bytes 1572868
  683.0 101.0 %copy-start.28 = (f32[64,2048]{1,0:T(8,128)S(1)}, f32[64,2048]{1,0:T(8,128)}, u32[]{:S(2)}) copy-start(f32[64,2048]{1,0:T(8,128)} %param.37) | copy-start | bytes 1572868
  683.0 101.0 %copy-start.29 = (f32[64,2048]{1,0:T(8,128)S(1)}, f32[64,2048]{1,0:T(8,128)}, u32[]{:S(2)}) copy-start(f32[64,2048]{1,0:T(8,128)} %param.36) | copy-start | bytes 1572868
  683.0 101.0 %copy-start.30 = (f32[64,2048]{1,0:T(8,128)S(1)}, f32[64,2048]{1,0:T(8,128)}, u32[]{:S(2)}) copy-start(f32[64,2048]{1,0:T(8,128)} %param.31) | copy-start | bytes 1572868
  683.0 101.0 %copy-start.31 = (f32[64,2048]{1,0:T(8,128)S(1)}, f32[64,2048]{1,0:T(8,128)}, u32[]{:S(2)}) copy-start(f32[64,2048]{1,0:T(8,128)} %param.30) | copy-start | bytes 1572868
  788.5 13.0 %copy-start.23 = (f32[64,1024]{1,0:T(8,128)}, f32[64,1024]{1,0:T(8,128)S(1)}, u32[]{:S(2)}) copy-start(f32[64,1024]{1,0:T(8,128)S(1)} %reshape.367) | copy-start | bytes 786436
  796.7 7.2 copy-start.11
  803.9 7.6 copy-start.2
  805.0 6.5 copy-start.35
  805.0 6.5 copy-start.36
  805.1 7.3 copy-start.9
  805.1 7.3 copy-start.33
  805.1 9.0 %copy-start.12 = (f32[256,2048]{1,0:T(8,128)S(1)}, f32[256,2048]{1,0:T(8,128)}, u32[]{:S(2)}) copy-start(f32[256,2048]{1,0:T(8,128)} %param.43) | copy-start | bytes 6291460
  805.1 9.0 %copy-start.13 = (f32[256,2048]{1,0:T(8,128)S(1)}, f32[256,2048]{1,0:T(8,128)}, u32[]{:S(2)}) copy-start(f32[256,2048]{1,0:T(8,128)} %param.42) | copy-start | bytes 6291460
  (24 other events, 98.7 us)

commit v2 on v1

--- a/solution.py
+++ b/solution.py
@@ -147,6 +147,16 @@
     return [(x * 2 + 1 - core, c), ((1 - x) * 2 + core, c)]
 
 
+def add_into(target, sources, rows, step=16):
+    @pl.loop(0, rows, step=step)
+    def _(r):
+        at = pl.ds(pl.multiple_of(r, step), step)
+        total = sources[0][at].astype(jnp.float32)
+        for source in sources[1:]:
+            total = total + source[at].astype(jnp.float32)
+        target[at] = total.astype(target.dtype)
+
+
 class SequenceGather:
     def __init__(self, own, out, sems, chunks):
         self.own, self.out, self.chunks = own, out, chunks
@@ -190,44 +200,58 @@
             to * YS + self.y,
         )
 
-    def first(self):
+    def start(self, copy):
+        copy.start()
+        self.sent.append(copy)
+
+    def first(self, by_block=False):
         self.local = pltpu.make_async_copy(self.own, self.out.at[self.c], self.local_sem)
         self.local.start()
+        if by_block:
+            for k in range(self.chunks):
+                self.start(self.across(self.z, k, self.part(self.own, k)))
+            for off in (1, 3, 2):
+                for k in range(self.chunks):
+                    self.start(self.along(off, k))
+            return
         for k in range(self.chunks):
             for off in (2, 1, 3):
-                copy = self.along(off, k)
-                copy.start()
-                self.sent.append(copy)
-            copy = self.across(self.z, k, self.part(self.own, k))
-            copy.start()
-            self.sent.append(copy)
+                self.start(self.along(off, k))
+            self.start(self.across(self.z, k, self.part(self.own, k)))
+
+    def relay_one(self, off, k):
+        source = lax.rem(self.z + off, ZS)
+        slot = source * YS + self.y
+        block = self.part(self.out.at[slot], k)
+        remote(
+            block, block, self.zs.at[off, k], self.zr.at[source, k], self.d, slot
+        ).wait_recv()
+        self.start(self.across(source, k, block))
 
     def relay(self, k):
         for off in (1, 3, 2):
-            source = lax.rem(self.z + off, ZS)
-            slot = source * YS + self.y
-            block = self.part(self.out.at[slot], k)
+            self.relay_one(off, k)
+
+    def arrive_across(self, z):
+        for k in range(self.chunks):
+            block = self.part(self.out.at[z * YS + 1 - self.y], k)
             remote(
-                block, block, self.zs.at[off, k], self.zr.at[source, k], self.d, slot
+                block,
+                block,
+                self.ys.at[z, k],
+                self.yr.at[z, k],
+                self.d,
+                self.z * YS + 1 - self.y,
             ).wait_recv()
-            copy = self.across(source, k, block)
-            copy.start()
-            self.sent.append(copy)
-
-    def last(self):
-        for k in range(self.chunks):
-            for z in range(ZS):
-                block = self.part(self.out.at[z * YS + 1 - self.y], k)
-                remote(
-                    block,
-                    block,
-                    self.ys.at[z, k],
-                    self.yr.at[z, k],
-                    self.d,
-                    self.z * YS + 1 - self.y,
-                ).wait_recv()
+
+    def finish(self):
         for copy in self.sent:
             copy.wait_send()
+
+    def last(self):
+        for z in range(ZS):
+            self.arrive_across(z)
+        self.finish()
         self.local.wait()
 
 
@@ -276,30 +300,35 @@
             to * YS + self.y,
         )
 
+    def start(self, z, k):
+        copy = self.across(z, k)
+        copy.start()
+        self.sent.append(copy)
+
     def first(self):
         for k in range(self.chunks):
             for off in (2, 1, 3, 0):
-                copy = self.across(lax.rem(self.z + off, ZS), k)
-                copy.start()
-                self.sent.append(copy)
+                self.start(lax.rem(self.z + off, ZS), k)
+
+    def relay_one(self, off, k):
+        z = lax.rem(self.z + off, ZS)
+        self.across(z, k).wait_recv()
+        add_into(
+            self.stage.at[off, self.span(k)],
+            [self.parts.at[z * YS + self.y, self.span(k)], self.ybuf.at[z, self.span(k)]],
+            self.rows,
+        )
+        copy = self.along(off, k)
+        copy.start()
+        self.sent.append(copy)
 
     def relay(self, k):
         for off in (2, 1, 3):
-            z = lax.rem(self.z + off, ZS)
-            self.across(z, k).wait_recv()
-            self.stage[off, self.span(k)] = (
-                self.parts[z * YS + self.y, self.span(k)].astype(jnp.float32)
-                + self.ybuf[z, self.span(k)].astype(jnp.float32)
-            ).astype(jnp.bfloat16)
-            copy = self.along(off, k)
-            copy.start()
-            self.sent.append(copy)
+            self.relay_one(off, k)
 
     def last(self, k):
         self.across(self.z, k).wait_recv()
-        total = self.parts[self.c, self.span(k)].astype(jnp.float32) + self.ybuf[
-            self.z, self.span(k)
-        ].astype(jnp.float32)
+        blocks = [self.parts.at[self.c, self.span(k)], self.ybuf.at[self.z, self.span(k)]]
         for off in (1, 3, 2):
             source = lax.rem(self.z + off, ZS)
             block = self.zbuf.at[source, self.span(k)]
@@ -311,8 +340,8 @@
                 self.d,
                 source * YS + self.y,
             ).wait_recv()
-            total = total + block[...].astype(jnp.float32)
-        self.out[self.span(k)] = total
+            blocks.append(block)
+        add_into(self.out.at[self.span(k)], blocks, self.rows)
 
     def finish(self):
         for copy in self.sent:
@@ -429,16 +458,6 @@
         for copy in self.sent:
             copy.wait_send()
         self.local.wait()
-
-
-def add_into(target, sources, rows, step=16):
-    @pl.loop(0, rows, step=step)
-    def _(r):
-        at = pl.ds(pl.multiple_of(r, step), step)
-        total = sources[0][at].astype(jnp.float32)
-        for source in sources[1:]:
-            total = total + source[at].astype(jnp.float32)
-        target[at] = total.astype(target.dtype)
 
 
 class ChipScatter:
@@ -630,56 +649,6 @@
     )(rows, spots, blocks)
 
 
-def gather_kernel(rows_ref, rows_out, *scratch):
-    gather = SequenceGather(rows_ref, rows_out, scratch, CHUNKS)
-    d, c, x, core, z, y = place()
-    greet(
-        [(d, lax.rem(z + off, ZS) * YS + y) for off in range(1, ZS)] + [(d, z * YS + 1 - y)]
-    )
-    gather.first()
-    for k in range(CHUNKS):
-        gather.relay(k)
-    gather.last()
-
-
-def gather_rows(rows, collective_id):
-    return pl.pallas_call(
-        gather_kernel,
-        out_shape=jax.ShapeDtypeStruct((PLANE, *rows.shape), rows.dtype),
-        in_specs=[ANY],
-        out_specs=ANY,
-        scratch_shapes=SequenceGather.scratch(CHUNKS),
-        compiler_params=params(collective_id),
-        name="gather_rows",
-    )(rows)
-
-
-def scatter_kernel(parts_ref, out_ref, *scratch):
-    scatter = SequenceScatter(parts_ref, out_ref, *scratch[:3], scratch[3:], CHUNKS)
-    d, c, x, core, z, y = place()
-    greet(
-        [(d, lax.rem(z + off, ZS) * YS + y) for off in range(1, ZS)] + [(d, z * YS + 1 - y)]
-    )
-    scatter.first()
-    for k in range(CHUNKS):
-        scatter.relay(k)
-    for k in range(CHUNKS):
-        scatter.last(k)
-    scatter.finish()
-
-
-def scatter_rows(parts, collective_id):
-    return pl.pallas_call(
-        scatter_kernel,
-        out_shape=jax.ShapeDtypeStruct(parts.shape[1:], jnp.float32),
-        in_specs=[VMEM],
-        out_specs=VMEM,
-        scratch_shapes=SequenceScatter.scratch(*parts.shape[1:], CHUNKS),
-        compiler_params=params(collective_id),
-        name="scatter_rows",
-    )(parts)
-
-
 DOWN_PARTS = 4
 SCORE_SCALE = 1.0 / math.sqrt(HEAD_SIZE)
 GROUP = QUERY_HEADS // KEY_VALUE_HEADS
@@ -690,47 +659,6 @@
     return lax.dot_general(
         left, right, (((1,), (1,)), ((), ())), preferred_element_type=jnp.float32
     )
-
-
-def down_kernel(rows_ref, down_ref, rows_out, down_out, *scratch):
-    down_local = scratch[0]
-    gather = SequenceGather(rows_ref, rows_out, scratch[1:6], CHUNKS)
-    down = ChipGather(down_out, scratch[6:], DOWN_PARTS)
-    d, c, x, core, z, y = place()
-    greet(plane_peers(d, c) + chip_peers(d, c, x, core))
-    local = pltpu.make_async_copy(
-        down_ref, down_out.at[pl.ds(d * DOWN_PARTS, DOWN_PARTS)], down_local
-    )
-    local.start()
-    gather.first()
-    for j in range(DOWN_PARTS):
-        down.start(j, down_ref.at[j])
-    for k in range(CHUNKS):
-        gather.relay(k)
-    for j in range(DOWN_PARTS):
-        down.relay(j)
-    gather.last()
-    down.last()
-    local.wait()
-
-
-def gather_with_down(rows, down, collective_id):
-    return pl.pallas_call(
-        down_kernel,
-        out_shape=(
-            jax.ShapeDtypeStruct((PLANE, *rows.shape), rows.dtype),
-            jax.ShapeDtypeStruct((4 * DOWN_PARTS, *down.shape[1:]), down.dtype),
-        ),
-        in_specs=[ANY] * 2,
-        out_specs=(ANY,) * 2,
-        scratch_shapes=[
-            pltpu.SemaphoreType.DMA(()),
-            *SequenceGather.scratch(CHUNKS),
-            *ChipGather.scratch(DOWN_PARTS),
-        ],
-        compiler_params=params(collective_id),
-        name="gather_with_down",
-    )(rows, down)
 
 
 class PlaneExchange:
@@ -798,9 +726,13 @@
     key_spot_ref,
     blocks_ref,
     out_rows_ref,
+    down_ref,
+    rows_ref,
     mixed_out,
     blocks_out,
     out_rows_out,
+    down_out,
+    rows_out,
     *scratch,
 ):
     mixed_stage = scratch[0]
@@ -810,11 +742,20 @@
     gather = SequenceGather(
         out_rows_ref, out_rows_out.at[pl.ds(d * PLANE, PLANE)], scratch[11:16], 1
     )
-    chip = ChipGather(out_rows_out, scratch[16:], PLANE)
+    chip = ChipGather(out_rows_out, scratch[16:20], PLANE)
+    rows = SequenceGather(rows_ref, rows_out, scratch[20:25], CHUNKS)
+    down = ChipGather(down_out, scratch[25:29], DOWN_PARTS)
     greet(plane_peers(d, c) + chip_peers(d, c, x, core))
     gather.first()
     chip.start(c, out_rows_ref)
     weights.first()
+    local = pltpu.make_async_copy(
+        down_ref, down_out.at[pl.ds(d * DOWN_PARTS, DOWN_PARTS)], scratch[29]
+    )
+    local.start()
+    for j in range(DOWN_PARTS):
+        down.start(j, down_ref.at[j])
+    rows.first()
     for step in range(1, PLANE + 1):
         block = lax.rem(c + step, PLANE)
 
@@ -848,17 +789,24 @@
     gather.last()
     for other in range(ZS):
         chip.start(other * YS + 1 - y)
+    for k in range(CHUNKS):
+        rows.relay(k)
+    for j in range(DOWN_PARTS):
+        down.relay(j)
     for off in range(PLANE):
         chip.relay(lax.rem(c + off, PLANE))
     weights.relay_chip()
     for off in range(1, PLANE + 1):
         exchange.arrive(off)
+    rows.last()
+    down.last()
     chip.last()
     weights.last()
     exchange.finish()
-
-
-def attention(query, keys, values, spots, starts, key_spots, blocks, out_rows):
+    local.wait()
+
+
+def attention(query, keys, values, spots, starts, key_spots, blocks, out_rows, down, rows):
     exchanged = jax.ShapeDtypeStruct(
         (PLANE, PAIRS, query.shape[3], 2 * HEAD_SIZE), jnp.bfloat16
     )
@@ -868,19 +816,147 @@
             exchanged,
             jax.ShapeDtypeStruct((RANKS, *blocks.shape[1:]), blocks.dtype),
             jax.ShapeDtypeStruct((RANKS, *out_rows.shape), out_rows.dtype),
+            jax.ShapeDtypeStruct((4 * DOWN_PARTS, *down.shape[1:]), down.dtype),
+            jax.ShapeDtypeStruct((PLANE, *rows.shape), rows.dtype),
         ),
-        in_specs=[VMEM] * 6 + [ANY] * 2,
-        out_specs=(VMEM, ANY, ANY),
+        in_specs=[VMEM] * 6 + [ANY] * 4,
+        out_specs=(VMEM, ANY, ANY, ANY, ANY),
         scratch_shapes=[
             pltpu.VMEM(exchanged.shape, jnp.bfloat16),
             *PlaneExchange.scratch(),
             *WeightGather.scratch(),
             *SequenceGather.scratch(1),
             *ChipGather.scratch(PLANE),
+            *SequenceGather.scratch(CHUNKS),
+            *ChipGather.scratch(DOWN_PARTS),
+            pltpu.SemaphoreType.DMA(()),
         ],
         compiler_params=params(2),
         name="attention",
-    )(query, keys, values, spots, starts, key_spots, blocks, out_rows)
+    )(query, keys, values, spots, starts, key_spots, blocks, out_rows, down, rows)
+
+
+def feed_kernel(
+    rows_ref,
+    grads_ref,
+    weight_ref,
+    down_ref,
+    rows_all,
+    hidden_out,
+    grad_out,
+    normed_out,
+    total_out,
+    *scratch,
+):
+    normed_parts, down_parts = scratch[:2]
+    gather = SequenceGather(rows_ref, rows_all, scratch[2:7], 2)
+    normed = SequenceScatter(normed_parts, normed_out, *scratch[7:10], scratch[10:14], 1)
+    total = SequenceScatter(down_parts, total_out, *scratch[14:17], scratch[17:21], 1)
+    d, c, x, core, z, y = place()
+    greet(
+        [(d, lax.rem(z + off, ZS) * YS + y) for off in range(1, ZS)] + [(d, z * YS + 1 - y)]
+    )
+    tokens, width = rows_ref.shape
+    part = hidden_out.shape[2]
+    tile = 256
+
+    def work(pair):
+        both = pl.ds(pair * YS, YS)
+
+        @pl.loop(0, part, step=tile)
+        def _(n):
+            at = pl.ds(pl.multiple_of(n, tile), tile)
+            after = pl.ds(pl.multiple_of(n + part, tile), tile)
+            rows = rows_all[both].reshape(YS * tokens, width)
+            gate = jnp.dot(rows, weight_ref[:, at], preferred_element_type=jnp.float32)
+            up = jnp.dot(rows, weight_ref[:, after], preferred_element_type=jnp.float32)
+            grad = times_rows(grads_ref[both].reshape(YS * tokens, width), down_ref[at, :])
+            sigmoid = jax.nn.sigmoid(gate)
+            silu = gate * sigmoid
+            gate_grad = grad * up * sigmoid * (1.0 + gate * (1.0 - sigmoid))
+
+            def held(value):
+                return value.astype(jnp.bfloat16).reshape(YS, tokens, tile)
+
+            hidden_out[both, :, at] = held(silu * up)
+            grad_out[both, :, at] = held(gate_grad)
+            grad_out[both, :, after] = held(grad * silu)
+
+        @pl.loop(0, width, step=2 * tile)
+        def _(n):
+            at = pl.ds(pl.multiple_of(n, 2 * tile), 2 * tile)
+            grads = grad_out[both].reshape(YS * tokens, 2 * part)
+            hidden = hidden_out[both].reshape(YS * tokens, part)
+            normed_parts[both, :, at] = (
+                times_rows(grads, weight_ref[at, :])
+                .astype(jnp.bfloat16)
+                .reshape(YS, tokens, 2 * tile)
+            )
+            down_parts[both, :, at] = (
+                jnp.dot(hidden, down_ref[:, at], preferred_element_type=jnp.float32)
+                .astype(jnp.bfloat16)
+                .reshape(YS, tokens, 2 * tile)
+            )
+
+    def pair_of(off):
+        return lax.rem(z + off, ZS)
+
+    gather.first(by_block=True)
+    gather.local.wait()
+    gather.arrive_across(z)
+    work(z)
+    order = (1, 3, 2)
+    for k in range(2):
+        gather.relay_one(1, k)
+    for k in range(2):
+        gather.relay_one(3, k)
+    for step, off in enumerate(order):
+        gather.arrive_across(pair_of(off))
+        work(pair_of(off))
+        normed.start(pair_of(off), 0)
+        if step == 0:
+            for k in range(2):
+                gather.relay_one(2, k)
+        else:
+            normed.relay_one(order[step - 1], 0)
+            total.start(pair_of(order[step - 1]), 0)
+    normed.relay_one(2, 0)
+    normed.start(z, 0)
+    total.start(pair_of(2), 0)
+    total.start(z, 0)
+    for off in order:
+        total.relay_one(off, 0)
+    normed.last(0)
+    total.last(0)
+    gather.finish()
+    normed.finish()
+    total.finish()
+
+
+def feed(rows, grads, weight, down):
+    part = down.shape[0]
+    summed = jax.ShapeDtypeStruct(rows.shape, jnp.float32)
+    return pl.pallas_call(
+        feed_kernel,
+        out_shape=(
+            jax.ShapeDtypeStruct((PLANE, *rows.shape), rows.dtype),
+            jax.ShapeDtypeStruct((PLANE, rows.shape[0], part), rows.dtype),
+            jax.ShapeDtypeStruct((PLANE, rows.shape[0], 2 * part), rows.dtype),
+            summed,
+            summed,
+        ),
+        in_specs=[ANY] + [VMEM] * 3,
+        out_specs=(VMEM,) * 5,
+        scratch_shapes=[
+            pltpu.VMEM((PLANE, *rows.shape), rows.dtype),
+            pltpu.VMEM((PLANE, *rows.shape), rows.dtype),
+            *SequenceGather.scratch(2),
+            *SequenceScatter.scratch(*rows.shape, 1),
+            *SequenceScatter.scratch(*rows.shape, 1),
+        ],
+        compiler_params=params(5),
+        name="feed",
+    )(rows, grads, weight, down)
 
 
 def attention_back_kernel(
@@ -1420,7 +1496,7 @@
     value_rows = projected[:, group_width + HEAD_SIZE :].astype(low)
     token_spots = places.reshape(PLANE, own_tokens, 1)
     token_starts = starts.reshape(PLANE, own_tokens, 1)
-    mixed_parts, feed_all, out_all = attention(
+    mixed_parts, feed_all, out_all, down_all, grads_all = attention(
         query_rows,
         key_rows,
         value_rows,
@@ -1429,6 +1505,8 @@
         places[None, :],
         feed_blocks,
         w_out.astype(low),
+        w_down.astype(low).reshape(DOWN_PARTS, -1, width),
+        out_grad,
     )
     mixed = mixed_parts.transpose(2, 0, 1, 3).reshape(own_tokens, width)
     out_weight = out_all.reshape(width, width)
@@ -1437,32 +1515,18 @@
     layer_rows = layer_in.astype(jnp.float32)
     middle = layer_rows + branch
     normed_two, inverse_two = norm_forward(middle)
-    input_two_all, down_all = gather_with_down(
+    input_two_all, hidden_all, grad_gate_up_all, grad_normed_two, down_sum = feed(
         (normed_two * gain_two).astype(low),
-        w_down.astype(low).reshape(DOWN_PARTS, -1, width),
-        6,
+        grads_all,
+        feed_all.reshape(width, 2 * ff_part),
+        down_all.reshape(ff_part, width),
     )
     input_two = input_two_all.reshape(seq_len, width)
-    grads_all = gather_rows(out_grad, 5)
-    feed_weight = feed_all.reshape(width, 2 * ff_part)
-    down_weight = down_all.reshape(ff_part, width)
-    gate_up = jnp.dot(input_two, feed_weight, preferred_element_type=jnp.float32)
-    gate_part = gate_up[:, :ff_part]
-    up_part = gate_up[:, ff_part:]
-    sigmoid_gate = jax.nn.sigmoid(gate_part)
-    silu_gate = gate_part * sigmoid_gate
-    hidden = (silu_gate * up_part).astype(low)
-    down_parts = jnp.dot(hidden, down_weight, preferred_element_type=jnp.float32).astype(low)
-    down_sum = scatter_rows(down_parts.reshape(PLANE, own_tokens, width), 7)
+    hidden = hidden_all.reshape(seq_len, ff_part)
+    grad_gate_up = grad_gate_up_all.reshape(seq_len, 2 * ff_part)
     layer_out = (middle + down_sum).astype(low)
 
     out_grads = grads_all.reshape(seq_len, width)
-    grad_hidden = times_transposed(out_grads, down_weight)
-    grad_gate = grad_hidden * up_part * sigmoid_gate * (1.0 + gate_part * (1.0 - sigmoid_gate))
-    grad_up = grad_hidden * silu_gate
-    grad_gate_up = jnp.concatenate([grad_gate, grad_up], axis=1).astype(low)
-    normed_parts = times_transposed(grad_gate_up, feed_weight).astype(low)
-    grad_normed_two = scatter_rows(normed_parts.reshape(PLANE, own_tokens, width), 8)
     down_term = transposed_times(hidden, out_grads).astype(low)
     feed_term = transposed_times(input_two, grad_gate_up).astype(low)
     grad_norm_two, unused = norm_backward(grad_normed_two, normed_two, inverse_two, gain_two)

time: 827 us -> 749 us (0.906)
  matrix products: 92.1 us -> 43.8 us
  Pallas kernels: 637 us -> 605 us
    pallas_call x4 -> x1, Pallas kernels: 254 us -> 199 us  [feed(): pl.pallas_call(feed_kernel, out_shape=(jax.ShapeDtypeStruct((PLANE, *rows...]
    dot_general x4 -> x2, matrix products: 31.1 us -> 7.31 us  [times_transposed(): lax.dot_general(left, right, (((1,), (1,)), ((), ())), preferred_element_...]
    dot_general x2 -> x0, matrix products: 20.8 us -> none  [the longest x1 14.6 us: tensor_parallel(): jnp.dot(input_two, feed_weight, preferred_element_type=jnp.float32)]
    pallas_call x1, Pallas kernels: 128 us -> 146 us  [attention(): pl.pallas_call(attention_kernel, out_shape=(exchanged, jax.ShapeDtypeStru...]
where the time goes in v2:
time: 749 us; the launch traced here: 743 us
  Pallas kernels  605 us (81%)
  other arithmetic  51.2 us (7%)
  matrix products  43.8 us (6%)
  local copies, waits for them, and re-layouts  40.6 us (5%)
    pallas_call x1, Pallas kernels, feed(): pl.pallas_call(feed_kernel, out_shape=(jax.ShapeDtypeStruct((PLANE, *rows...  199 us
    pallas_call x1, Pallas kernels, attention(): pl.pallas_call(attention_kernel, out_shape=(exchanged, jax.ShapeDtypeStru...  146 us
    pallas_call x1, Pallas kernels, closing(): pl.pallas_call(closing_kernel, out_shape=(jax.ShapeDtypeStruct(rows.shape...  100 us
    pallas_call x1, Pallas kernels, attention_back(): pl.pallas_call(attention_back_kernel, out_shape=(jax.ShapeDtypeStruct(que...  88.1 us
    pallas_call x1, Pallas kernels, opening(): pl.pallas_call(opening_kernel, out_shape=(jax.ShapeDtypeStruct((PLANE, *r...  72 us
    dot_general x4, matrix products, transposed_times(): lax.dot_general(left, right, (((0,), (0,)), ((), ())), preferred_element_...  29.8 us
    sub x5, other arithmetic, adamw(): weight - rate * (first_hat / (jnp.sqrt(second_hat) + eps_adam) + decay *...  16.5 us

profile of v2, /device:TPU:0, one launch (start us, length us, event | category | flops | bytes accessed | tf_op | source)
XLA Modules:
  0.0 742.6 jit_solution(9083239270020045912)
XLA Ops:
  5.6 72.0 %opening.1 = (bf16[8,128,2048]{2,1,0:T(8,128)(2,1)}, s32[8,8,128]{2,1,0:T(8,128)}, bf16[32,64,512]{2,1,0:T(8,128)(2,1)}) custom-call(bf16[128,2048]{1,0:T(8,128)(2,1)} %rows_ref.2, s32[8,128]{1,0:T(8,128)} %broadcast_in_dim.18.spots_ref, bf16[8,64,512]{2,1,0:T(8,128)(2,1)} %pad_maximum_fusion.1.blocks_ref), custom_call_target="tpu_custom_call" | custom-call | tf_op jit(solution)/shard_map/opening/pallas_call | solution.py:631
  77.6 2.4 slice_convert_fusion
  80.3 3.2 multiply_reduce_fusion
  92.6 2.9 fusion.36
  100.3 2.4 convert_element_type.141
  105.3 4.5 reshape.339.blocks_ref
  111.7 146.2 %attention.1 = (bf16[8,2,128,128]{3,2,1,0:T(8,128)(2,1)}, bf16[32,64,2048]{2,1,0:T(8,128)(2,1)}, bf16[32,64,2048]{2,1,0:T(8,128)(2,1)}, bf16[16,64,2048]{2,1,0:T(8,128)(2,1)}, bf16[8,128,2048]{2,1,0:T(8,128)(2,1)}) custom-call(bf16[8,2,2,128,64]{4,3,2,1,0:T(8,128)(2,1)} %maximum_bitcast_fusion.query_ref, bf16[1024,64]{1,0:T(8,128)(2,1)} %pad_maximum_fusion.5.key_ref, ...), custom_call_target="tpu_custom_call" | custom-call | tf_op jit(solution)/shard_map/attention/pallas_call | solution.py:813
  259.2 4.8 multiply_reduce_fusion.3
  265.4 198.5 %feed.1 = (bf16[8,128,2048]{2,1,0:T(8,128)(2,1)}, bf16[8,128,1024]{2,1,0:T(8,128)(2,1)}, bf16[8,128,2048]{2,1,0:T(8,128)(2,1)}, f32[128,2048]{1,0:T(8,128)}, f32[128,2048]{1,0:T(8,128)}) custom-call(bf16[128,2048]{1,0:T(8,128)(2,1)} %multiply_convert_fusion.rows_ref, bf16[8,128,2048]{2,1,0:T(8,128)(2,1)} %get-tuple-element.52.grads_ref, ...), custom_call_target="tpu_custom_call" | custom-call | tf_op jit(solution)/shard_map/feed/pallas_call | solution.py:939
  465.5 2.7 multiply_add_fusion.2
  468.2 5.6 convolution_convert_fusion
  473.8 6.2 bitcast_convert_fusion.1
  480.1 11.9 %bitcast_convert_fusion = bf16[2048,2048]{1,0:T(8,128)(2,1)} fusion(bf16[8,128,2048]{2,1,0:T(8,128)(2,1)S(1)} %copy-done.38, bf16[8,128,2048]{2,1,0:T(8,128)(2,1)S(1)} %copy-done.39), kind=kOutput, calls=%fused_computation | convolution fusion | flops 8594128896 | bytes 16777216 | tf_op jit(solution)/shard_map/dot_general | solution.py:105
  492.0 2.9 convolution_convert_fusion.3
  496.2 88.1 %attention_back.1 = (f32[8,2,2,128,64]{4,3,2,1,0:T(8,128)}, f32[1024,64]{1,0:T(8,128)}, f32[1024,64]{1,0:T(8,128)}, bf16[8,64,2048]{2,1,0:T(8,128)(2,1)}, f32[4,64,2048]{2,1,0:T(8,128)}) custom-call(bf16[8,2,2,128,64]{4,3,2,1,0:T(8,128)(2,1)} %maximum_bitcast_fusion.query_ref, bf16[1024,64]{1,0:T(8,128)(2,1)} %pad_maximum_fusion.5.key_ref, ...), custom_call_target="tpu_custom_call" | custom-call | tf_op jit(solution)/shard_map/attention_back/pallas_call | solution.py:1028
  590.0 2.6 fusion.27
  594.1 6.0 convolution_convert_fusion.2
  600.1 4.4 convolution_convert_fusion.1
  604.6 100.4 %closing.1 = (f32[128,2048]{1,0:T(8,128)}, bf16[8,64,384]{2,1,0:T(8,128)(2,1)}, f32[64,2048]{1,0:T(8,128)}) custom-call(bf16[8,128,2048]{2,1,0:T(8,128)(2,1)} %bitcast.126, bf16[32,64,384]{2,1,0:T(8,128)(2,1)} %bitcast.137, bf16[32,64,2048]{2,1,0:T(8,128)(2,1)} %bitcast.111), custom_call_target="tpu_custom_call" | custom-call | tf_op jit(solution)/shard_map/closing/pallas_call | solution.py:1089
  706.2 3.5 multiply_subtract_fusion.2
  712.9 6.2 reshape.361
  719.1 4.8 copy.137
  727.5 6.2 multiply_subtract_fusion
  736.2 4.0 multiply_subtract_fusion.1
  (161 shorter events, 48.2 us)
Async XLA Ops:
  90.3 7.8 %copy-start.37 = (s32[1,3]{1,0:T(1,128)S(1)}, s32[1,3]{1,0:T(1,128)}, u32[]{:S(2)}) copy-start(s32[1,3]{1,0:T(1,128)} %param.24) | copy-start | bytes 40
  103.2 6.6 copy-start.4
  111.0 148.3 %copy-start.3 = (bf16[128,2048]{1,0:T(8,128)(2,1)S(1)}, bf16[128,2048]{1,0:T(8,128)(2,1)}, u32[]{:S(2)}) copy-start(bf16[128,2048]{1,0:T(8,128)(2,1)} %rows_ref.2) | copy-start | bytes 1572868
  265.4 200.1 %copy-start.16 = (bf16[128,2048]{1,0:T(8,128)(2,1)S(1)}, bf16[128,2048]{1,0:T(8,128)(2,1)}, u32[]{:S(2)}) copy-start(bf16[128,2048]{1,0:T(8,128)(2,1)} %rows_ref.3) | copy-start | bytes 1572868
  473.8 6.3 copy-start.38
  473.8 6.3 copy-start.39
  473.8 18.2 %slice-start = ((s8[8388608]{0:T(1024)(128)(4,1)}), s8[4194304]{0:T(1024)(128)(4,1)S(1)}, s32[]{:S(2)}) async-start(s8[8388608]{0:T(1024)(128)(4,1)} %bitcast.108), calls=%async_computation | async-start | bytes 8388608
  480.1 11.9 %slice-start.1 = ((s8[8388608]{0:T(1024)(128)(4,1)}), s8[4194304]{0:T(1024)(128)(4,1)S(1)}, s32[]{:S(2)}) async-start(s8[8388608]{0:T(1024)(128)(4,1)} %bitcast.108), calls=%async_computation.1 | async-start | bytes 8388608
  594.1 6.0 copy-start.27
  604.5 101.6 %copy-start.17 = (f32[64,2048]{1,0:T(8,128)S(1)}, f32[64,2048]{1,0:T(8,128)}, u32[]{:S(2)}) copy-start(f32[64,2048]{1,0:T(8,128)} %param.29) | copy-start | bytes 1572868
  604.5 101.6 %copy-start.19 = (f32[64,2048]{1,0:T(8,128)S(1)}, f32[64,2048]{1,0:T(8,128)}, u32[]{:S(2)}) copy-start(f32[64,2048]{1,0:T(8,128)} %param.35) | copy-start | bytes 1572868
  604.5 101.7 %copy-start.29 = (f32[64,2048]{1,0:T(8,128)S(1)}, f32[64,2048]{1,0:T(8,128)}, u32[]{:S(2)}) copy-start(f32[64,2048]{1,0:T(8,128)} %param.37) | copy-start | bytes 1572868
  604.5 101.7 %copy-start.30 = (f32[64,2048]{1,0:T(8,128)S(1)}, f32[64,2048]{1,0:T(8,128)}, u32[]{:S(2)}) copy-start(f32[64,2048]{1,0:T(8,128)} %param.36) | copy-start | bytes 1572868
  604.5 101.7 %copy-start.31 = (f32[64,2048]{1,0:T(8,128)S(1)}, f32[64,2048]{1,0:T(8,128)}, u32[]{:S(2)}) copy-start(f32[64,2048]{1,0:T(8,128)} %param.31) | copy-start | bytes 1572868
  604.5 101.7 %copy-start.32 = (f32[64,2048]{1,0:T(8,128)S(1)}, f32[64,2048]{1,0:T(8,128)}, u32[]{:S(2)}) copy-start(f32[64,2048]{1,0:T(8,128)} %param.30) | copy-start | bytes 1572868
  710.6 13.3 %copy-start.24 = (f32[64,1024]{1,0:T(8,128)}, f32[64,1024]{1,0:T(8,128)S(1)}, u32[]{:S(2)}) copy-start(f32[64,1024]{1,0:T(8,128)S(1)} %reshape.355) | copy-start | bytes 786436
  719.1 7.2 copy-start.11
  726.3 7.3 copy-start.2
  727.5 6.2 copy-start.33
  727.5 6.2 copy-start.34
  727.5 6.2 copy-start.35
  727.5 7.0 copy-start.9
  727.5 8.7 %copy-start.13 = (f32[256,2048]{1,0:T(8,128)S(1)}, f32[256,2048]{1,0:T(8,128)}, u32[]{:S(2)}) copy-start(f32[256,2048]{1,0:T(8,128)} %param.43) | copy-start | bytes 6291460
  727.5 8.7 %copy-start.14 = (f32[256,2048]{1,0:T(8,128)S(1)}, f32[256,2048]{1,0:T(8,128)}, u32[]{:S(2)}) copy-start(f32[256,2048]{1,0:T(8,128)} %param.42) | copy-start | bytes 6291460
  (20 other events, 76.7 us)

commit v3 on v2

--- a/solution.py
+++ b/solution.py
@@ -157,6 +157,11 @@
         target[at] = total.astype(target.dtype)
 
 
+def near_first(z):
+    half = lax.div(z, 2)
+    return [half * 4 + 1 - z, 2 - half, 3 - 3 * half]
+
+
 class SequenceGather:
     def __init__(self, own, out, sems, chunks):
         self.own, self.out, self.chunks = own, out, chunks
@@ -189,12 +194,11 @@
             self.z * YS + 1 - self.y,
         )
 
-    def along(self, off, k):
-        to = lax.rem(self.z + off, ZS)
+    def along(self, to, k):
         return remote(
             self.part(self.own, k),
             self.part(self.out.at[self.c], k),
-            self.zs.at[off, k],
+            self.zs.at[to, k],
             self.zr.at[self.z, k],
             self.d,
             to * YS + self.y,
@@ -207,30 +211,34 @@
     def first(self, by_block=False):
         self.local = pltpu.make_async_copy(self.own, self.out.at[self.c], self.local_sem)
         self.local.start()
+        near = near_first(self.z)
         if by_block:
             for k in range(self.chunks):
                 self.start(self.across(self.z, k, self.part(self.own, k)))
-            for off in (1, 3, 2):
+            for to in near:
                 for k in range(self.chunks):
-                    self.start(self.along(off, k))
+                    self.start(self.along(to, k))
             return
         for k in range(self.chunks):
-            for off in (2, 1, 3):
-                self.start(self.along(off, k))
+            for to in near[::-1]:
+                self.start(self.along(to, k))
             self.start(self.across(self.z, k, self.part(self.own, k)))
 
-    def relay_one(self, off, k):
-        source = lax.rem(self.z + off, ZS)
+    def relay_one(self, source, k):
         slot = source * YS + self.y
         block = self.part(self.out.at[slot], k)
         remote(
-            block, block, self.zs.at[off, k], self.zr.at[source, k], self.d, slot
+            block, block, self.zs.at[source, k], self.zr.at[source, k], self.d, slot
         ).wait_recv()
         self.start(self.across(source, k, block))
 
     def relay(self, k):
-        for off in (1, 3, 2):
-            self.relay_one(off, k)
+        for source in near_first(self.z):
+            self.relay_one(source, k)
+
+    def relay_block(self, source):
+        for k in range(self.chunks):
+            self.relay_one(source, k)
 
     def arrive_across(self, z):
         for k in range(self.chunks):
@@ -256,9 +264,9 @@
 
 
 class SequenceScatter:
-    def __init__(self, parts, out, ybuf, stage, zbuf, sems, chunks):
+    def __init__(self, parts, out, ybuf, zbuf, sems, chunks):
         self.parts, self.out, self.chunks = parts, out, chunks
-        self.ybuf, self.stage, self.zbuf = ybuf, stage, zbuf
+        self.ybuf, self.zbuf = ybuf, zbuf
         self.ys, self.yr, self.zs, self.zr = sems
         self.d, self.c, _, _, self.z, self.y = place()
         self.rows = parts.shape[1] // chunks
@@ -267,7 +275,6 @@
     @staticmethod
     def scratch(rows, width, chunks):
         return [
-            pltpu.VMEM((ZS, rows, width), jnp.bfloat16),
             pltpu.VMEM((ZS, rows, width), jnp.bfloat16),
             pltpu.VMEM((ZS, rows, width), jnp.bfloat16),
             pltpu.SemaphoreType.DMA((ZS, chunks)),
@@ -289,12 +296,11 @@
             self.z * YS + 1 - self.y,
         )
 
-    def along(self, off, k):
-        to = lax.rem(self.z + off, ZS)
+    def along(self, to, k):
         return remote(
-            self.stage.at[off, self.span(k)],
+            self.ybuf.at[to, self.span(k)],
             self.zbuf.at[self.z, self.span(k)],
-            self.zs.at[off, k],
+            self.zs.at[to, k],
             self.zr.at[self.z, k],
             self.d,
             to * YS + self.y,
@@ -307,35 +313,30 @@
 
     def first(self):
         for k in range(self.chunks):
-            for off in (2, 1, 3, 0):
-                self.start(lax.rem(self.z + off, ZS), k)
-
-    def relay_one(self, off, k):
-        z = lax.rem(self.z + off, ZS)
+            for z in (*near_first(self.z)[::-1], self.z):
+                self.start(z, k)
+
+    def relay_one(self, z, k):
         self.across(z, k).wait_recv()
-        add_into(
-            self.stage.at[off, self.span(k)],
-            [self.parts.at[z * YS + self.y, self.span(k)], self.ybuf.at[z, self.span(k)]],
-            self.rows,
-        )
-        copy = self.along(off, k)
+        block = self.ybuf.at[z, self.span(k)]
+        add_into(block, [self.parts.at[z * YS + self.y, self.span(k)], block], self.rows)
+        copy = self.along(z, k)
         copy.start()
         self.sent.append(copy)
 
     def relay(self, k):
-        for off in (2, 1, 3):
-            self.relay_one(off, k)
+        for z in near_first(self.z)[::-1]:
+            self.relay_one(z, k)
 
     def last(self, k):
         self.across(self.z, k).wait_recv()
         blocks = [self.parts.at[self.c, self.span(k)], self.ybuf.at[self.z, self.span(k)]]
-        for off in (1, 3, 2):
-            source = lax.rem(self.z + off, ZS)
+        for source in near_first(self.z):
             block = self.zbuf.at[source, self.span(k)]
             remote(
                 block,
                 block,
-                self.zs.at[off, k],
+                self.zs.at[source, k],
                 self.zr.at[source, k],
                 self.d,
                 source * YS + self.y,
@@ -591,62 +592,6 @@
 ANY = pl.BlockSpec(memory_space=pl.ANY)
 VMEM = pl.BlockSpec(memory_space=pltpu.VMEM)
 CHUNKS = 4
-
-
-def opening_kernel(rows_ref, spots_ref, blocks_ref, rows_out, spots_out, blocks_out, *scratch):
-    spot_send, spot_recv, spot_local = scratch[:3]
-    gather = SequenceGather(rows_ref, rows_out, scratch[3:8], CHUNKS)
-    weights = WeightGather(blocks_ref, blocks_out, scratch[8:])
-    d, c, x, core, z, y = place()
-    greet(plane_peers(d, c) + chip_peers(d, c, x, core))
-    weights.first()
-    sent = []
-    local = pltpu.make_async_copy(spots_ref, spots_out.at[c], spot_local)
-    local.start()
-    for off in range(1, PLANE):
-        to = lax.rem(c + off, PLANE)
-        copy = remote(
-            spots_ref, spots_out.at[c], spot_send.at[off], spot_recv.at[c], d, to
-        )
-        copy.start()
-        sent.append(copy)
-    gather.first()
-    for off in range(1, PLANE):
-        weights.relay(off)
-    for k in range(CHUNKS):
-        gather.relay(k)
-    weights.relay_chip()
-    gather.last()
-    weights.last()
-    for off in range(1, PLANE):
-        source = lax.rem(c + off, PLANE)
-        block = spots_out.at[source]
-        remote(block, block, spot_send.at[off], spot_recv.at[source], d, source).wait_recv()
-    for copy in sent:
-        copy.wait_send()
-    local.wait()
-
-
-def opening(rows, spots, blocks):
-    return pl.pallas_call(
-        opening_kernel,
-        out_shape=(
-            jax.ShapeDtypeStruct((PLANE, *rows.shape), rows.dtype),
-            jax.ShapeDtypeStruct((PLANE, *spots.shape), spots.dtype),
-            jax.ShapeDtypeStruct((RANKS, *blocks.shape[1:]), blocks.dtype),
-        ),
-        in_specs=[ANY] * 3,
-        out_specs=(ANY,) * 3,
-        scratch_shapes=[
-            pltpu.SemaphoreType.DMA((PLANE,)),
-            pltpu.SemaphoreType.DMA((PLANE,)),
-            pltpu.SemaphoreType.DMA(()),
-            *SequenceGather.scratch(CHUNKS),
-            *WeightGather.scratch(),
-        ],
-        compiler_params=params(1),
-        name="opening",
-    )(rows, spots, blocks)
 
 
 DOWN_PARTS = 4
@@ -717,123 +662,272 @@
     return exponent * (1.0 / jnp.sum(exponent, axis=-1, keepdims=True))
 
 
+def rotate(value, table, back=False):
+    lane = lax.broadcasted_iota(jnp.int32, value.shape, 1)
+    turned = pltpu.roll(table, HEAD_SIZE, 1)
+    cosine = jnp.where(lane < HEAD_SIZE, table, turned)
+    sine = jnp.where(lane < HEAD_SIZE, turned, table)
+    half = HEAD_SIZE // 2
+    other = jnp.where(
+        lax.rem(lane, HEAD_SIZE) < half,
+        pltpu.roll(value, 2 * HEAD_SIZE - half, 1),
+        pltpu.roll(value, half, 1),
+    )
+    if back:
+        return value * cosine - other * sine
+    return value * cosine + other * sine
+
+
+QKV_WIDTH = (GROUP + 2) * HEAD_SIZE
+
+
 def attention_kernel(
-    query_ref,
-    key_ref,
-    value_ref,
-    spot_ref,
-    start_ref,
-    key_spot_ref,
+    starts_ref,
+    rows_ref,
+    table_ref,
+    spots_ref,
+    qkv_ref,
     blocks_ref,
     out_rows_ref,
     down_ref,
-    rows_ref,
+    grads_ref,
+    input_out,
+    table_out,
+    qkv_out,
+    gains_out,
+    query_out,
+    key_out,
+    value_out,
+    spot_out,
+    start_out,
+    key_spot_out,
     mixed_out,
     blocks_out,
     out_rows_out,
     down_out,
-    rows_out,
+    grads_out,
     *scratch,
 ):
-    mixed_stage = scratch[0]
-    exchange = PlaneExchange(mixed_stage, mixed_out, scratch[1:4])
-    weights = WeightGather(blocks_ref, blocks_out, scratch[4:11])
+    mixed_stage, spots_all, rows_all = scratch[:3]
+    scratch = list(scratch[3:])
+
+    def take(count):
+        taken, scratch[:count] = scratch[:count], []
+        return taken
+
     d, c, x, core, z, y = place()
-    gather = SequenceGather(
-        out_rows_ref, out_rows_out.at[pl.ds(d * PLANE, PLANE)], scratch[11:16], 1
-    )
-    chip = ChipGather(out_rows_out, scratch[16:20], PLANE)
-    rows = SequenceGather(rows_ref, rows_out, scratch[20:25], CHUNKS)
-    down = ChipGather(down_out, scratch[25:29], DOWN_PARTS)
+    exchange = PlaneExchange(mixed_stage, mixed_out, take(3))
+    qkv = WeightGather(qkv_ref, qkv_out, take(7))
+    weights = WeightGather(blocks_ref, blocks_out, take(7))
+    outs = SequenceGather(out_rows_ref, out_rows_out.at[pl.ds(d * PLANE, PLANE)], take(5), 1)
+    outs_chip = ChipGather(out_rows_out, take(4), PLANE)
+    rows = SequenceGather(rows_ref, rows_all, take(5), 2)
+    table = SequenceGather(table_ref, table_out, take(5), 1)
+    grads = SequenceGather(grads_ref, grads_out, take(5), CHUNKS)
+    down = ChipGather(down_out, take(4), DOWN_PARTS)
+    spot_send, spot_recv, spot_local, down_local = take(4)
     greet(plane_peers(d, c) + chip_peers(d, c, x, core))
-    gather.first()
-    chip.start(c, out_rows_ref)
-    weights.first()
-    local = pltpu.make_async_copy(
-        down_ref, down_out.at[pl.ds(d * DOWN_PARTS, DOWN_PARTS)], scratch[29]
-    )
-    local.start()
+    order = near_first(z)
+
+    qkv.first()
+    spots_own = pltpu.make_async_copy(spots_ref, spots_all.at[c], spot_local)
+    spots_own.start()
+    spots_sent = []
+    for off in range(1, PLANE):
+        to = lax.rem(c + off, PLANE)
+        copy = remote(
+            spots_ref, spots_all.at[c], spot_send.at[off], spot_recv.at[c], d, to
+        )
+        copy.start()
+        spots_sent.append(copy)
+    table.first()
+    rows.first(by_block=True)
+    down_own = pltpu.make_async_copy(
+        down_ref, down_out.at[pl.ds(d * DOWN_PARTS, DOWN_PARTS)], down_local
+    )
+    down_own.start()
     for j in range(DOWN_PARTS):
         down.start(j, down_ref.at[j])
-    rows.first()
+    outs.first()
+    outs_chip.start(c, out_rows_ref)
+    for off in range(1, PLANE):
+        qkv.relay(off)
+    table.relay(0)
+    rows.relay_block(order[0])
+    qkv.relay_chip()
+    rows.relay_block(order[1])
+    rows.relay_block(order[2])
+    weights.first()
+    for off in range(1, PLANE):
+        source = lax.rem(c + off, PLANE)
+        block = spots_all.at[source]
+        remote(block, block, spot_send.at[off], spot_recv.at[source], d, source).wait_recv()
+    spots_own.wait()
+    table.last()
+    for slot in range(PLANE):
+        key_spot_out[:, slot * 128 : (slot + 1) * 128] = spots_all[slot]
+        spot = jnp.broadcast_to(spots_all[slot][:1], (128, 128)).T[:, :1]
+        start = jnp.zeros_like(spot)
+        for doc in range(starts_ref.shape[1]):
+            first = starts_ref[0, doc].astype(jnp.float32)
+            start = jnp.maximum(start, jnp.where(spot >= first, first, 0.0))
+        spot_out[slot] = spot
+        start_out[slot] = start
+    qkv.last()
+    for pair in range(RANKS // 2):
+        columns = qkv_out[2 * pair : 2 * pair + 2, :, QKV_WIDTH:]
+        turned = columns.reshape(128, 128).astype(jnp.float32).T
+        gains_out[:, pair * 128 : (pair + 1) * 128] = turned[:8]
+
+    tokens, width = rows_ref.shape
+    wide = 2 * HEAD_SIZE
+
+    def project(pair):
+        for slot in range(YS):
+
+            @pl.loop(0, tokens, step=32)
+            def _(r):
+                at = pl.ds(pl.multiple_of(r, 32), 32)
+                value = rows_all[pair * YS + slot, at].astype(jnp.float32)
+                inverse = lax.rsqrt(
+                    jnp.mean(value * value, axis=-1, keepdims=True) + eps_norm
+                )
+                input_out[pair * YS + slot, at] = (value * inverse * gains_out[:1]).astype(
+                    jnp.bfloat16
+                )
+
+        both = pl.ds(pair * YS, YS)
+        weight = qkv_out[:, :, :QKV_WIDTH].reshape(width, QKV_WIDTH)
+        projected = jnp.dot(
+            input_out[both].reshape(YS * tokens, width),
+            weight,
+            preferred_element_type=jnp.float32,
+        )
+        turns = table_out[both].reshape(YS * tokens, wide)
+        for slot in range(YS):
+            span = slice(slot * tokens, (slot + 1) * tokens)
+            block = pair * YS + slot
+            for heads in range(PAIRS):
+                query = rotate(
+                    projected[span, heads * wide : (heads + 1) * wide], turns[span]
+                ).astype(jnp.bfloat16)
+                query_out[block, heads, 0] = query[:, :HEAD_SIZE]
+                query_out[block, heads, 1] = query[:, HEAD_SIZE:]
+            key = rotate(projected[span, PAIRS * wide :], turns[span])
+            key_out[block] = key[:, :HEAD_SIZE].astype(jnp.bfloat16)
+            value_out[block] = projected[span, PAIRS * wide + HEAD_SIZE :].astype(
+                jnp.bfloat16
+            )
+
+    rows.local.wait()
+    rows.arrive_across(z)
+    project(z)
+    outs.relay(0)
+    for source in order:
+        outs_chip.start(source * YS + y)
+    for pair in order:
+        rows.arrive_across(pair)
+        project(pair)
+    rows.finish()
+    for other in range(ZS):
+        outs.arrive_across(other)
+        outs_chip.start(other * YS + 1 - y)
+    grads.first()
+
     for step in range(1, PLANE + 1):
         block = lax.rem(c + step, PLANE)
 
         @pl.loop(0, PAIRS)
         def _(pair):
             halves = []
+            keys = key_out[...].reshape(PLANE * tokens, HEAD_SIZE)
+            values = value_out[...].reshape(PLANE * tokens, HEAD_SIZE)
             for half in range(2):
                 probs = probabilities(
-                    query_ref[block, pair, half],
-                    key_ref[...],
-                    spot_ref[block],
-                    start_ref[block],
-                    key_spot_ref[...],
+                    query_out[block, pair, half],
+                    keys,
+                    spot_out[block],
+                    start_out[block],
+                    key_spot_out[:1],
                 )
                 halves.append(
                     jnp.dot(
-                        probs.astype(jnp.bfloat16),
-                        value_ref[...],
-                        preferred_element_type=jnp.float32,
+                        probs.astype(jnp.bfloat16), values, preferred_element_type=jnp.float32
                     ).astype(jnp.bfloat16)
                 )
             mixed_stage[block, pair] = jnp.concatenate(halves, axis=1)
 
         exchange.send(step)
-        if step == 1:
-            gather.relay(0)
-            for off in range(1, ZS):
-                chip.start(lax.rem(z + off, ZS) * YS + y)
         if step < PLANE:
             weights.relay(step)
-    gather.last()
-    for other in range(ZS):
-        chip.start(other * YS + 1 - y)
     for k in range(CHUNKS):
-        rows.relay(k)
+        grads.relay(k)
     for j in range(DOWN_PARTS):
         down.relay(j)
     for off in range(PLANE):
-        chip.relay(lax.rem(c + off, PLANE))
+        outs_chip.relay(lax.rem(c + off, PLANE))
     weights.relay_chip()
     for off in range(1, PLANE + 1):
         exchange.arrive(off)
-    rows.last()
+    grads.last()
     down.last()
-    chip.last()
+    outs_chip.last()
     weights.last()
+    outs.finish()
+    outs.local.wait()
     exchange.finish()
-    local.wait()
-
-
-def attention(query, keys, values, spots, starts, key_spots, blocks, out_rows, down, rows):
-    exchanged = jax.ShapeDtypeStruct(
-        (PLANE, PAIRS, query.shape[3], 2 * HEAD_SIZE), jnp.bfloat16
-    )
+    for copy in spots_sent:
+        copy.wait_send()
+    down_own.wait()
+
+
+def attention(starts, rows, table, spots, qkv, blocks, out_rows, down, grads):
+    low, full = jnp.bfloat16, jnp.float32
+    tokens, width = rows.shape
+    mixed = jax.ShapeDtypeStruct((PLANE, PAIRS, tokens, 2 * HEAD_SIZE), low)
+    seq_len = PLANE * tokens
     return pl.pallas_call(
         attention_kernel,
         out_shape=(
-            exchanged,
-            jax.ShapeDtypeStruct((RANKS, *blocks.shape[1:]), blocks.dtype),
-            jax.ShapeDtypeStruct((RANKS, *out_rows.shape), out_rows.dtype),
-            jax.ShapeDtypeStruct((4 * DOWN_PARTS, *down.shape[1:]), down.dtype),
-            jax.ShapeDtypeStruct((PLANE, *rows.shape), rows.dtype),
+            jax.ShapeDtypeStruct((PLANE, tokens, width), low),
+            jax.ShapeDtypeStruct((PLANE, *table.shape), full),
+            jax.ShapeDtypeStruct((RANKS, *qkv.shape[1:]), low),
+            jax.ShapeDtypeStruct((8, width), full),
+            jax.ShapeDtypeStruct((PLANE, PAIRS, 2, tokens, HEAD_SIZE), low),
+            jax.ShapeDtypeStruct((PLANE, tokens, HEAD_SIZE), low),
+            jax.ShapeDtypeStruct((PLANE, tokens, HEAD_SIZE), low),
+            jax.ShapeDtypeStruct((PLANE, tokens, 1), full),
+            jax.ShapeDtypeStruct((PLANE, tokens, 1), full),
+            jax.ShapeDtypeStruct((8, seq_len), full),
+            mixed,
+            jax.ShapeDtypeStruct((RANKS, *blocks.shape[1:]), low),
+            jax.ShapeDtypeStruct((RANKS, *out_rows.shape), low),
+            jax.ShapeDtypeStruct((4 * DOWN_PARTS, *down.shape[1:]), low),
+            jax.ShapeDtypeStruct((PLANE, *grads.shape), low),
         ),
-        in_specs=[VMEM] * 6 + [ANY] * 4,
-        out_specs=(VMEM, ANY, ANY, ANY, ANY),
+        in_specs=[pl.BlockSpec(memory_space=pltpu.SMEM)] + [ANY] * 8,
+        out_specs=(VMEM,) * 11 + (ANY,) * 4,
         scratch_shapes=[
-            pltpu.VMEM(exchanged.shape, jnp.bfloat16),
+            pltpu.VMEM(mixed.shape, low),
+            pltpu.VMEM((PLANE, *spots.shape), full),
+            pltpu.VMEM((PLANE, tokens, width), low),
             *PlaneExchange.scratch(),
+            *WeightGather.scratch(),
             *WeightGather.scratch(),
             *SequenceGather.scratch(1),
             *ChipGather.scratch(PLANE),
+            *SequenceGather.scratch(2),
+            *SequenceGather.scratch(1),
             *SequenceGather.scratch(CHUNKS),
             *ChipGather.scratch(DOWN_PARTS),
+            pltpu.SemaphoreType.DMA((PLANE,)),
+            pltpu.SemaphoreType.DMA((PLANE,)),
+            pltpu.SemaphoreType.DMA(()),
             pltpu.SemaphoreType.DMA(()),
         ],
         compiler_params=params(2),
         name="attention",
-    )(query, keys, values, spots, starts, key_spots, blocks, out_rows, down, rows)
+    )(starts, rows, table, spots, qkv, blocks, out_rows, down, grads)
 
 
 def feed_kernel(
@@ -850,8 +944,8 @@
 ):
     normed_parts, down_parts = scratch[:2]
     gather = SequenceGather(rows_ref, rows_all, scratch[2:7], 2)
-    normed = SequenceScatter(normed_parts, normed_out, *scratch[7:10], scratch[10:14], 1)
-    total = SequenceScatter(down_parts, total_out, *scratch[14:17], scratch[17:21], 1)
+    normed = SequenceScatter(normed_parts, normed_out, *scratch[7:9], scratch[9:13], 1)
+    total = SequenceScatter(down_parts, total_out, *scratch[13:15], scratch[15:19], 1)
     d, c, x, core, z, y = place()
     greet(
         [(d, lax.rem(z + off, ZS) * YS + y) for off in range(1, ZS)] + [(d, z * YS + 1 - y)]
@@ -898,34 +992,28 @@
                 .reshape(YS, tokens, 2 * tile)
             )
 
-    def pair_of(off):
-        return lax.rem(z + off, ZS)
-
+    order = near_first(z)
     gather.first(by_block=True)
     gather.local.wait()
     gather.arrive_across(z)
     work(z)
-    order = (1, 3, 2)
-    for k in range(2):
-        gather.relay_one(1, k)
-    for k in range(2):
-        gather.relay_one(3, k)
-    for step, off in enumerate(order):
-        gather.arrive_across(pair_of(off))
-        work(pair_of(off))
-        normed.start(pair_of(off), 0)
+    gather.relay_block(order[0])
+    gather.relay_block(order[1])
+    for step, pair in enumerate(order):
+        gather.arrive_across(pair)
+        work(pair)
+        normed.start(pair, 0)
         if step == 0:
-            for k in range(2):
-                gather.relay_one(2, k)
+            gather.relay_block(order[2])
         else:
             normed.relay_one(order[step - 1], 0)
-            total.start(pair_of(order[step - 1]), 0)
-    normed.relay_one(2, 0)
+            total.start(order[step - 1], 0)
+    normed.relay_one(order[2], 0)
     normed.start(z, 0)
-    total.start(pair_of(2), 0)
+    total.start(order[2], 0)
     total.start(z, 0)
-    for off in order:
-        total.relay_one(off, 0)
+    for pair in order:
+        total.relay_one(pair, 0)
     normed.last(0)
     total.last(0)
     gather.finish()
@@ -995,17 +1083,19 @@
 
         @pl.loop(0, PAIRS)
         def _(pair):
+            keys = key_ref[...].reshape(key_out.shape)
+            values = value_ref[...].reshape(value_out.shape)
             for half in range(2):
                 query = query_ref[block, pair, half]
                 grad = mixed_all[block, pair][:, half * HEAD_SIZE : (half + 1) * HEAD_SIZE]
                 probs = probabilities(
-                    query, key_ref[...], spot_ref[block], start_ref[block], key_spot_ref[...]
+                    query, keys, spot_ref[block], start_ref[block], key_spot_ref[:1]
                 )
-                grad_probs = times_rows(grad, value_ref[...])
+                grad_probs = times_rows(grad, values)
                 delta = jnp.sum(probs * grad_probs, axis=-1, keepdims=True)
                 grad_scores = (probs * (grad_probs - delta) * SCORE_SCALE).astype(jnp.bfloat16)
                 query_out[block, pair, half] = jnp.dot(
-                    grad_scores, key_ref[...], preferred_element_type=jnp.float32
+                    grad_scores, keys, preferred_element_type=jnp.float32
                 )
                 key_out[...] += transposed_times(grad_scores, query)
                 value_out[...] += transposed_times(probs.astype(jnp.bfloat16), grad)
@@ -1029,8 +1119,8 @@
         attention_back_kernel,
         out_shape=(
             jax.ShapeDtypeStruct(query.shape, jnp.float32),
-            jax.ShapeDtypeStruct(keys.shape, jnp.float32),
-            jax.ShapeDtypeStruct(values.shape, jnp.float32),
+            jax.ShapeDtypeStruct((PLANE * keys.shape[1], HEAD_SIZE), jnp.float32),
+            jax.ShapeDtypeStruct((PLANE * values.shape[1], HEAD_SIZE), jnp.float32),
             jax.ShapeDtypeStruct((PLANE, *parts.shape[1:]), parts.dtype),
             jax.ShapeDtypeStruct((DOWN_PARTS, *down.shape[1:]), jnp.float32),
         ),
@@ -1048,15 +1138,15 @@
 
 
 def closing_kernel(rows_ref, parts_ref, outs_ref, rows_out, out_ref, outs_out, *scratch):
-    scatter = SequenceScatter(rows_ref, rows_out, *scratch[:3], scratch[3:7], CHUNKS)
-    weights = WeightScatter(parts_ref, out_ref, scratch[7:11], scratch[11:17])
-    outs_sum = scratch[17]
-    chip = ChipScatter(outs_ref, *scratch[18:21], scratch[21:25], PLANE)
-    outs = SequenceScatter(outs_sum, outs_out, *scratch[25:28], scratch[28:], 1)
+    scatter = SequenceScatter(rows_ref, rows_out, *scratch[:2], scratch[2:6], CHUNKS)
+    weights = WeightScatter(parts_ref, out_ref, scratch[6:10], scratch[10:16])
+    outs_sum = scratch[16]
+    chip = ChipScatter(outs_ref, *scratch[17:20], scratch[20:24], PLANE)
+    outs = SequenceScatter(outs_sum, outs_out, *scratch[24:26], scratch[26:], 1)
     d, c, x, core, z, y = place()
     greet(plane_peers(d, c) + chip_peers(d, c, x, core))
-    slots = [lax.rem(z + off, ZS) * YS + 1 - y for off in (2, 1, 3, 0)]
-    slots += [lax.rem(z + off, ZS) * YS + y for off in (2, 1, 3, 0)]
+    places = (*near_first(z)[::-1], z)
+    slots = [place * YS + 1 - y for place in places] + [place * YS + y for place in places]
     for j in slots:
         chip.start(j)
     weights.first()
@@ -1072,9 +1162,7 @@
     for i, j in enumerate(slots):
         chip.total(j, outs_sum.at[j])
         if i < ZS:
-            copy = outs.across(lax.rem(z + (2, 1, 3, 0)[i], ZS), 0)
-            copy.start()
-            outs.sent.append(copy)
+            outs.start(places[i], 0)
     outs.relay(0)
     for k in range(CHUNKS):
         scatter.last(k)
@@ -1465,49 +1553,43 @@
         .transpose(3, 0, 1, 2, 4)
         .reshape(PLANE, rows, 2 * ff_part)
     )
-    spots = jnp.broadcast_to(positions[None, :], (8, own_tokens))
-    rows_all, spots_all, attention_all = opening(layer_in, spots, attention_blocks)
-    attention_all = attention_all.reshape(width, -1)
-    qkv_width = group_width + 2 * HEAD_SIZE
-    qkv_weight = attention_all[:, :qkv_width]
-    gain_one = attention_all[:, qkv_width].astype(jnp.float32)
-    gain_two = attention_all[:, qkv_width + 1].astype(jnp.float32)
-    places = spots_all[:, 0, :].reshape(seq_len)
-    starts = jnp.max(
-        jnp.where(doc_starts[0][None, :] <= places[:, None], doc_starts[0][None, :], 0), axis=1
-    )
-    normed_all, unused = norm_forward(rows_all.reshape(seq_len, width).astype(jnp.float32))
-    input_one = (normed_all * gain_one).astype(low)
-    projected = jnp.dot(input_one, qkv_weight, preferred_element_type=jnp.float32)
-    cosine_table, sine_table = rope_tables(places, HEAD_SIZE)
-    query_rows = (
-        apply_rotation(
-            projected[:, :group_width].reshape(seq_len, group, HEAD_SIZE),
-            cosine_table,
-            sine_table,
-        )
-        .astype(low)
-        .reshape(PLANE, own_tokens, PAIRS, 2, HEAD_SIZE)
-        .transpose(0, 2, 3, 1, 4)
-    )
-    key_rows = apply_rotation(
-        projected[:, None, group_width : group_width + HEAD_SIZE], cosine_table, sine_table
-    ).astype(low)[:, 0]
-    value_rows = projected[:, group_width + HEAD_SIZE :].astype(low)
-    token_spots = places.reshape(PLANE, own_tokens, 1)
-    token_starts = starts.reshape(PLANE, own_tokens, 1)
-    mixed_parts, feed_all, out_all, down_all, grads_all = attention(
+    spots = jnp.broadcast_to(positions[None, :].astype(jnp.float32), (8, own_tokens))
+    cosine_own, sine_own = rope_tables(positions, HEAD_SIZE)
+    cosine_own, sine_own = cosine_own[:, 0], sine_own[:, 0]
+    table = jnp.concatenate([cosine_own, cosine_own, -sine_own, sine_own], axis=1)
+    qkv_width = QKV_WIDTH
+    (
+        input_one_all,
+        table_all,
+        attention_all,
+        gain_rows,
         query_rows,
         key_rows,
         value_rows,
         token_spots,
         token_starts,
-        places[None, :],
+        key_spots,
+        mixed_parts,
+        feed_all,
+        out_all,
+        down_all,
+        grads_all,
+    ) = attention(
+        doc_starts,
+        layer_in,
+        table,
+        spots,
+        attention_blocks,
         feed_blocks,
         w_out.astype(low),
         w_down.astype(low).reshape(DOWN_PARTS, -1, width),
         out_grad,
     )
+    gain_one, gain_two = gain_rows[0], gain_rows[1]
+    input_one = input_one_all.reshape(seq_len, width)
+    qkv_weight = attention_all.reshape(width, -1)[:, :qkv_width]
+    cosine_table = table_all[:, :, : HEAD_SIZE // 2].reshape(seq_len, 1, -1)
+    sine_table = table_all[:, :, 3 * HEAD_SIZE // 2 :].reshape(seq_len, 1, -1)
     mixed = mixed_parts.transpose(2, 0, 1, 3).reshape(own_tokens, width)
     out_weight = out_all.reshape(width, width)
     branch = jnp.dot(mixed, out_weight, preferred_element_type=jnp.float32)
@@ -1545,7 +1627,7 @@
         value_rows,
         token_spots,
         token_starts,
-        places[None, :],
+        key_spots,
         grad_mixed,
         feed_term.reshape(RANKS, rows, 2 * ff_part),
         down_term.reshape(4 * DOWN_PARTS, -1, width),

time: 749 us -> 702 us (0.937)
  Pallas kernels: 605 us -> 577 us
  other arithmetic: 51.2 us -> 35.3 us
    pallas_call x2 -> x1, Pallas kernels: 218 us -> 205 us  [attention(): pl.pallas_call(attention_kernel, out_shape=(jax.ShapeDtypeStruct((PLANE,...]
    pallas_call x1, Pallas kernels: 199 us -> 189 us  [feed(): pl.pallas_call(feed_kernel, out_shape=(jax.ShapeDtypeStruct((PLANE, *rows...]
where the time goes in v3:
time: 702 us; the launch traced here: 691 us
  Pallas kernels  577 us (82%)
  matrix products  41.7 us (6%)
  local copies, waits for them, and re-layouts  35.4 us (5%)
  other arithmetic  35.3 us (5%)
    pallas_call x1, Pallas kernels, attention(): pl.pallas_call(attention_kernel, out_shape=(jax.ShapeDtypeStruct((PLANE,...  205 us
    pallas_call x1, Pallas kernels, feed(): pl.pallas_call(feed_kernel, out_shape=(jax.ShapeDtypeStruct((PLANE, *rows...  189 us
    pallas_call x1, Pallas kernels, closing(): pl.pallas_call(closing_kernel, out_shape=(jax.ShapeDtypeStruct(rows.shape...  99 us
    pallas_call x1, Pallas kernels, attention_back(): pl.pallas_call(attention_back_kernel, out_shape=(jax.ShapeDtypeStruct(que...  83.9 us
    dot_general x4, matrix products, transposed_times(): lax.dot_general(left, right, (((0,), (0,)), ((), ())), preferred_element_...  29.7 us
    sub x5, other arithmetic, adamw(): weight - rate * (first_hat / (jnp.sqrt(second_hat) + eps_adam) + decay *...  16.7 us

profile of v3, /device:TPU:0, one launch (start us, length us, event | category | flops | bytes accessed | tf_op | source)
XLA Modules:
  0.0 691.5 jit_solution(2592437340018166959)
XLA Ops:
  3.0 2.4 convert_element_type.94
  6.0 2.1 copy.102
  8.1 4.6 reshape.192.blocks_ref
  17.9 205.1 %attention.1 = (bf16[8,128,2048]{2,1,0:T(8,128)(2,1)}, f32[8,128,128]{2,1,0:T(8,128)}, bf16[32,64,512]{2,1,0:T(8,128)(2,1)}, f32[8,2048]{1,0:T(8,128)}, bf16[8,2...) custom-call(s32[1,3]{1,0:T(1,128)} %starts_ref.1, ...), custom_call_target="tpu_custom_call" | custom-call | tf_op jit(solution)/shard_map/attention/pallas_call | solution.py:889
  224.3 4.7 multiply_reduce_fusion.2
  231.0 189.4 %feed.1 = (bf16[8,128,2048]{2,1,0:T(8,128)(2,1)}, bf16[8,128,1024]{2,1,0:T(8,128)(2,1)}, bf16[8,128,2048]{2,1,0:T(8,128)(2,1)}, f32[128,2048]{1,0:T(8,128)}, f32[128,2048]{1,0:T(8,128)}) custom-call(bf16[128,2048]{1,0:T(8,128)(2,1)} %multiply_convert_fusion.rows_ref, bf16[8,128,2048]{2,1,0:T(8,128)(2,1)} %get-tuple-element.57.grads_ref, ...), custom_call_target="tpu_custom_call" | custom-call | tf_op jit(solution)/shard_map/feed/pallas_call | solution.py:1027
  420.3 1.5 multiply_reduce_fusion.1
  421.9 2.7 multiply_add_fusion.2
  424.6 5.6 convolution_convert_fusion
  430.2 6.2 bitcast_convert_fusion.1
  436.4 11.9 %bitcast_convert_fusion = bf16[2048,2048]{1,0:T(8,128)(2,1)} fusion(bf16[8,128,2048]{2,1,0:T(8,128)(2,1)S(1)} %copy-done.33, bf16[8,128,2048]{2,1,0:T(8,128)(2,1)S(1)} %copy-done.34), kind=kOutput, calls=%fused_computation | convolution fusion | flops 8594128896 | bytes 16777216 | tf_op jit(solution)/shard_map/dot_general | solution.py:105
  448.3 2.9 convolution_convert_fusion.3
  452.5 83.9 %attention_back.1 = (f32[8,2,2,128,64]{4,3,2,1,0:T(8,128)}, f32[1024,64]{1,0:T(8,128)}, f32[1024,64]{1,0:T(8,128)}, bf16[8,64,2048]{2,1,0:T(8,128)(2,1)}, f32[4,64,2048]{2,1,0:T(8,128)}) custom-call(bf16[8,2,2,128,64]{4,3,2,1,0:T(8,128)(2,1)} %get-tuple-element.62.query_ref, bf16[8,128,64]{2,1,0:T(8,128)(2,1)} %get-tuple-element.63.key_ref, ...), custom_call_target="tpu_custom_call" | custom-call | tf_op jit(solution)/shard_map/attention_back/pallas_call | solution.py:1118
  536.4 2.3 copy.84
  544.3 6.0 convolution_convert_fusion.2
  550.3 4.4 convolution_convert_fusion.1
  554.8 99.0 %closing.1 = (f32[128,2048]{1,0:T(8,128)}, bf16[8,64,384]{2,1,0:T(8,128)(2,1)}, f32[64,2048]{1,0:T(8,128)}) custom-call(bf16[8,128,2048]{2,1,0:T(8,128)(2,1)} %bitcast.112, bf16[32,64,384]{2,1,0:T(8,128)(2,1)} %bitcast.123, bf16[32,64,2048]{2,1,0:T(8,128)(2,1)} %bitcast.97), custom_call_target="tpu_custom_call" | custom-call | tf_op jit(solution)/shard_map/closing/pallas_call | solution.py:1177
  655.0 3.5 multiply_subtract_fusion.2
  659.4 2.2 multiply_subtract_fusion.4
  661.7 6.0 reshape.215
  667.7 4.8 copy.91
  672.5 2.4 copy.98
  676.0 6.4 multiply_subtract_fusion
  684.9 4.0 multiply_subtract_fusion.1
  (132 shorter events, 25.8 us)
Async XLA Ops:
  5.9 6.8 copy-start.23
  6.0 9.0 %copy-start.15 = (f32[64,2048]{1,0:T(8,128)S(1)}, f32[64,2048]{1,0:T(8,128)}, u32[]{:S(2)}) copy-start(f32[64,2048]{1,0:T(8,128)} %param.29) | copy-start | bytes 1572868
  8.1 6.9 %copy-start.30 = (f32[2,64]{1,0:T(2,128)S(1)}, f32[2,64]{1,0:T(2,128)}, u32[]{:S(2)}) copy-start(f32[2,64]{1,0:T(2,128)} %param.26) | copy-start | bytes 1540
  8.1 7.9 %copy-start.3 = (f32[256,2048]{1,0:T(8,128)S(1)}, f32[256,2048]{1,0:T(8,128)}, u32[]{:S(2)}) copy-start(f32[256,2048]{1,0:T(8,128)} %param.41) | copy-start | bytes 6291460
  17.2 207.2 %copy-start.2 = (bf16[128,2048]{1,0:T(8,128)(2,1)S(1)}, bf16[128,2048]{1,0:T(8,128)(2,1)}, u32[]{:S(2)}) copy-start(bf16[128,2048]{1,0:T(8,128)(2,1)} %rows_ref.1) | copy-start | bytes 1572868
  231.0 190.9 %copy-start.12 = (bf16[128,2048]{1,0:T(8,128)(2,1)S(1)}, bf16[128,2048]{1,0:T(8,128)(2,1)}, u32[]{:S(2)}) copy-start(bf16[128,2048]{1,0:T(8,128)(2,1)} %grads_ref.1) | copy-start | bytes 1572868
  430.2 6.3 copy-start.33
  430.2 6.3 copy-start.34
  430.2 18.1 %slice-start = ((s8[8388608]{0:T(1024)(128)(4,1)}), s8[4194304]{0:T(1024)(128)(4,1)S(1)}, s32[]{:S(2)}) async-start(s8[8388608]{0:T(1024)(128)(4,1)} %bitcast.94), calls=%async_computation | async-start | bytes 8388608
  436.4 11.9 %slice-start.1 = ((s8[8388608]{0:T(1024)(128)(4,1)}), s8[4194304]{0:T(1024)(128)(4,1)S(1)}, s32[]{:S(2)}) async-start(s8[8388608]{0:T(1024)(128)(4,1)} %bitcast.94), calls=%async_computation.1 | async-start | bytes 8388608
  554.7 100.2 %copy-start.16 = (f32[64,2048]{1,0:T(8,128)S(1)}, f32[64,2048]{1,0:T(8,128)}, u32[]{:S(2)}) copy-start(f32[64,2048]{1,0:T(8,128)} %param.29) | copy-start | bytes 1572868
  554.7 100.2 %copy-start.18 = (f32[64,2048]{1,0:T(8,128)S(1)}, f32[64,2048]{1,0:T(8,128)}, u32[]{:S(2)}) copy-start(f32[64,2048]{1,0:T(8,128)} %param.35) | copy-start | bytes 1572868
  554.7 100.2 %copy-start.26 = (f32[64,2048]{1,0:T(8,128)S(1)}, f32[64,2048]{1,0:T(8,128)}, u32[]{:S(2)}) copy-start(f32[64,2048]{1,0:T(8,128)} %param.37) | copy-start | bytes 1572868
  554.7 100.2 %copy-start.27 = (f32[64,2048]{1,0:T(8,128)S(1)}, f32[64,2048]{1,0:T(8,128)}, u32[]{:S(2)}) copy-start(f32[64,2048]{1,0:T(8,128)} %param.36) | copy-start | bytes 1572868
  554.7 100.2 %copy-start.28 = (f32[64,2048]{1,0:T(8,128)S(1)}, f32[64,2048]{1,0:T(8,128)}, u32[]{:S(2)}) copy-start(f32[64,2048]{1,0:T(8,128)} %param.31) | copy-start | bytes 1572868
  554.8 100.2 %copy-start.29 = (f32[64,2048]{1,0:T(8,128)S(1)}, f32[64,2048]{1,0:T(8,128)}, u32[]{:S(2)}) copy-start(f32[64,2048]{1,0:T(8,128)} %param.30) | copy-start | bytes 1572868
  659.4 13.0 %copy-start.22 = (f32[64,1024]{1,0:T(8,128)}, f32[64,1024]{1,0:T(8,128)S(1)}, u32[]{:S(2)}) copy-start(f32[64,1024]{1,0:T(8,128)S(1)} %reshape.212) | copy-start | bytes 786436
  667.7 7.2 %copy-start.8 = (f32[64,16384]{1,0:T(8,128)S(1)}, f32[64,16384]{1,0:T(8,128)}, u32[]{:S(2)}) copy-start(f32[64,16384]{1,0:T(8,128)} %param.39) | copy-start | bytes 12582916
  674.9 7.5 %copy-start.1 = (f32[8,8,64,256]{3,1,2,0:T(8,128)}, f32[8,8,64,256]{3,1,2,0:T(8,128)S(1)}, u32[]{:S(2)}) copy-start(f32[8,8,64,256]{3,1,2,0:T(8,128)S(1)} %copy.98) | copy-start | bytes 12582916
  676.0 6.4 copy-start.31
  676.0 6.4 copy-start.32
  676.0 7.2 %copy-start.6 = (f32[128,2048]{1,0:T(8,128)S(1)}, f32[128,2048]{1,0:T(8,128)}, u32[]{:S(2)}) copy-start(f32[128,2048]{1,0:T(8,128)} %get-tuple-element.77) | copy-start | bytes 3145732
  676.0 8.9 %copy-start.10 = (f32[256,2048]{1,0:T(8,128)S(1)}, f32[256,2048]{1,0:T(8,128)}, u32[]{:S(2)}) copy-start(f32[256,2048]{1,0:T(8,128)} %param.43) | copy-start | bytes 6291460
  676.0 8.9 %copy-start.11 = (f32[256,2048]{1,0:T(8,128)S(1)}, f32[256,2048]{1,0:T(8,128)}, u32[]{:S(2)}) copy-start(f32[256,2048]{1,0:T(8,128)} %param.42) | copy-start | bytes 6291460
  (15 other events, 60.7 us)

commit v4 on v3

--- a/solution.py
+++ b/solution.py
@@ -583,9 +583,9 @@
         self.chip.finish()
 
 
-def params(collective_id):
+def params(collective_id, mebibytes=56):
     return pltpu.CompilerParams(
-        collective_id=collective_id, has_side_effects=True, vmem_limit_bytes=56 * 2**20
+        collective_id=collective_id, has_side_effects=True, vmem_limit_bytes=mebibytes * 2**20
     )
 
 
@@ -690,7 +690,6 @@
     blocks_ref,
     out_rows_ref,
     down_ref,
-    grads_ref,
     input_out,
     table_out,
     qkv_out,
@@ -705,7 +704,6 @@
     blocks_out,
     out_rows_out,
     down_out,
-    grads_out,
     *scratch,
 ):
     mixed_stage, spots_all, rows_all = scratch[:3]
@@ -723,7 +721,6 @@
     outs_chip = ChipGather(out_rows_out, take(4), PLANE)
     rows = SequenceGather(rows_ref, rows_all, take(5), 2)
     table = SequenceGather(table_ref, table_out, take(5), 1)
-    grads = SequenceGather(grads_ref, grads_out, take(5), CHUNKS)
     down = ChipGather(down_out, take(4), DOWN_PARTS)
     spot_send, spot_recv, spot_local, down_local = take(4)
     greet(plane_peers(d, c) + chip_peers(d, c, x, core))
@@ -832,7 +829,6 @@
     for other in range(ZS):
         outs.arrive_across(other)
         outs_chip.start(other * YS + 1 - y)
-    grads.first()
 
     for step in range(1, PLANE + 1):
         block = lax.rem(c + step, PLANE)
@@ -860,8 +856,6 @@
         exchange.send(step)
         if step < PLANE:
             weights.relay(step)
-    for k in range(CHUNKS):
-        grads.relay(k)
     for j in range(DOWN_PARTS):
         down.relay(j)
     for off in range(PLANE):
@@ -869,7 +863,6 @@
     weights.relay_chip()
     for off in range(1, PLANE + 1):
         exchange.arrive(off)
-    grads.last()
     down.last()
     outs_chip.last()
     weights.last()
@@ -881,7 +874,7 @@
     down_own.wait()
 
 
-def attention(starts, rows, table, spots, qkv, blocks, out_rows, down, grads):
+def attention(starts, rows, table, spots, qkv, blocks, out_rows, down):
     low, full = jnp.bfloat16, jnp.float32
     tokens, width = rows.shape
     mixed = jax.ShapeDtypeStruct((PLANE, PAIRS, tokens, 2 * HEAD_SIZE), low)
@@ -903,10 +896,9 @@
             jax.ShapeDtypeStruct((RANKS, *blocks.shape[1:]), low),
             jax.ShapeDtypeStruct((RANKS, *out_rows.shape), low),
             jax.ShapeDtypeStruct((4 * DOWN_PARTS, *down.shape[1:]), low),
-            jax.ShapeDtypeStruct((PLANE, *grads.shape), low),
         ),
-        in_specs=[pl.BlockSpec(memory_space=pltpu.SMEM)] + [ANY] * 8,
-        out_specs=(VMEM,) * 11 + (ANY,) * 4,
+        in_specs=[pl.BlockSpec(memory_space=pltpu.SMEM)] + [ANY] * 7,
+        out_specs=(VMEM,) * 11 + (ANY,) * 3,
         scratch_shapes=[
             pltpu.VMEM(mixed.shape, low),
             pltpu.VMEM((PLANE, *spots.shape), full),
@@ -918,7 +910,6 @@
             *ChipGather.scratch(PLANE),
             *SequenceGather.scratch(2),
             *SequenceGather.scratch(1),
-            *SequenceGather.scratch(CHUNKS),
             *ChipGather.scratch(DOWN_PARTS),
             pltpu.SemaphoreType.DMA((PLANE,)),
             pltpu.SemaphoreType.DMA((PLANE,)),
@@ -927,7 +918,7 @@
         ],
         compiler_params=params(2),
         name="attention",
-    )(starts, rows, table, spots, qkv, blocks, out_rows, down, grads)
+    )(starts, rows, table, spots, qkv, blocks, out_rows, down)
 
 
 def feed_kernel(
@@ -935,114 +926,207 @@
     grads_ref,
     weight_ref,
     down_ref,
-    rows_all,
-    hidden_out,
-    grad_out,
     normed_out,
     total_out,
+    weight_grad_out,
+    down_grad_out,
     *scratch,
 ):
-    normed_parts, down_parts = scratch[:2]
-    gather = SequenceGather(rows_ref, rows_all, scratch[2:7], 2)
-    normed = SequenceScatter(normed_parts, normed_out, *scratch[7:9], scratch[9:13], 1)
-    total = SequenceScatter(down_parts, total_out, *scratch[13:15], scratch[15:19], 1)
+    rows_all, grads_all, slope_gate, slope_up, hidden_all, gate_grads = scratch[:6]
+    normed_parts, down_parts, turned, stage, stage_sem = scratch[6:11]
+    scratch = list(scratch[11:])
+
+    def take(count):
+        taken, scratch[:count] = scratch[:count], []
+        return taken
+
+    rows = SequenceGather(rows_ref, rows_all, take(5), 2)
+    grads = SequenceGather(grads_ref, grads_all, take(5), 2)
+    normed = SequenceScatter(normed_parts, normed_out, *take(2), take(4), 1)
+    total = SequenceScatter(down_parts, total_out, *take(2), take(4), 1)
     d, c, x, core, z, y = place()
     greet(
         [(d, lax.rem(z + off, ZS) * YS + y) for off in range(1, ZS)] + [(d, z * YS + 1 - y)]
     )
     tokens, width = rows_ref.shape
-    part = hidden_out.shape[2]
+    part = down_ref.shape[0]
     tile = 256
-
-    def work(pair):
-        both = pl.ds(pair * YS, YS)
-
+    blocks = PLANE // 2
+    half = lax.div(z, 2)
+    near, mid, far = near_first(z)
+
+    def slots(side):
+        return pl.ds(side * blocks, blocks)
+
+    def columns(n, start=0, size=tile):
+        return pl.ds(pl.multiple_of(n + start, size), size)
+
+    def flat(ref, side):
+        value = ref[slots(side)]
+        return value.reshape(blocks * tokens, value.shape[2])
+
+    def held(value, dtype=jnp.bfloat16):
+        return value.astype(dtype).reshape(blocks, tokens, value.shape[1])
+
+    def forward(side):
         @pl.loop(0, part, step=tile)
         def _(n):
-            at = pl.ds(pl.multiple_of(n, tile), tile)
-            after = pl.ds(pl.multiple_of(n + part, tile), tile)
-            rows = rows_all[both].reshape(YS * tokens, width)
-            gate = jnp.dot(rows, weight_ref[:, at], preferred_element_type=jnp.float32)
-            up = jnp.dot(rows, weight_ref[:, after], preferred_element_type=jnp.float32)
-            grad = times_rows(grads_ref[both].reshape(YS * tokens, width), down_ref[at, :])
+            at, after = columns(n), columns(n, part)
+            value = flat(rows_all, side)
+            gate = jnp.dot(value, weight_ref[:, at], preferred_element_type=jnp.float32)
+            up = jnp.dot(value, weight_ref[:, after], preferred_element_type=jnp.float32)
             sigmoid = jax.nn.sigmoid(gate)
             silu = gate * sigmoid
-            gate_grad = grad * up * sigmoid * (1.0 + gate * (1.0 - sigmoid))
-
-            def held(value):
-                return value.astype(jnp.bfloat16).reshape(YS, tokens, tile)
-
-            hidden_out[both, :, at] = held(silu * up)
-            grad_out[both, :, at] = held(gate_grad)
-            grad_out[both, :, after] = held(grad * silu)
-
+            hidden_all[slots(side), :, at] = held(silu * up)
+            slope_up[slots(side), :, at] = held(silu, jnp.float32)
+            slope_gate[slots(side), :, at] = held(
+                up * sigmoid * (1.0 + gate * (1.0 - sigmoid)), jnp.float32
+            )
+
+    def downward(side):
         @pl.loop(0, width, step=2 * tile)
         def _(n):
-            at = pl.ds(pl.multiple_of(n, 2 * tile), 2 * tile)
-            grads = grad_out[both].reshape(YS * tokens, 2 * part)
-            hidden = hidden_out[both].reshape(YS * tokens, part)
-            normed_parts[both, :, at] = (
-                times_rows(grads, weight_ref[at, :])
-                .astype(jnp.bfloat16)
-                .reshape(YS, tokens, 2 * tile)
+            at = columns(n, 0, 2 * tile)
+            down_parts[slots(side), :, at] = held(
+                jnp.dot(
+                    flat(hidden_all, side), down_ref[:, at], preferred_element_type=jnp.float32
+                )
             )
-            down_parts[both, :, at] = (
-                jnp.dot(hidden, down_ref[:, at], preferred_element_type=jnp.float32)
-                .astype(jnp.bfloat16)
-                .reshape(YS, tokens, 2 * tile)
+
+    def backward(side):
+        @pl.loop(0, part, step=tile)
+        def _(n):
+            at, after = columns(n), columns(n, part)
+            grad = held(times_rows(flat(grads_all, side), down_ref[at, :]), jnp.float32)
+            gate_grads[slots(side), :, at] = (grad * slope_gate[slots(side), :, at]).astype(
+                jnp.bfloat16
             )
-
-    order = near_first(z)
-    gather.first(by_block=True)
-    gather.local.wait()
-    gather.arrive_across(z)
-    work(z)
-    gather.relay_block(order[0])
-    gather.relay_block(order[1])
-    for step, pair in enumerate(order):
-        gather.arrive_across(pair)
-        work(pair)
-        normed.start(pair, 0)
-        if step == 0:
-            gather.relay_block(order[2])
-        else:
-            normed.relay_one(order[step - 1], 0)
-            total.start(order[step - 1], 0)
-    normed.relay_one(order[2], 0)
+            gate_grads[slots(side), :, after] = (grad * slope_up[slots(side), :, at]).astype(
+                jnp.bfloat16
+            )
+
+    def inward(side):
+        @pl.loop(0, width, step=2 * tile)
+        def _(n):
+            at = columns(n, 0, 2 * tile)
+            normed_parts[slots(side), :, at] = held(
+                times_rows(flat(gate_grads, side), weight_ref[at, :])
+            )
+
+    tiles = [(hidden_all, grads_all, down_grad_out, n) for n in range(part // tile)]
+    tiles += [(rows_all, gate_grads, weight_grad_out, n) for n in range(width // tile)]
+    copies = []
+
+    def weight_grad(i):
+        left, right, out, n = tiles[i]
+        if i >= 2:
+            copies[i - 2].wait()
+        value = left[:, :, n * tile : (n + 1) * tile].reshape(PLANE * tokens, tile)
+        turned[...] = value.T
+
+        @pl.loop(0, width, step=2 * tile)
+        def _(m):
+            at = columns(m, 0, 2 * tile)
+            stage[i % 2, :, at] = jnp.dot(
+                turned[...],
+                right[:, :, at].reshape(PLANE * tokens, 2 * tile),
+                preferred_element_type=jnp.float32,
+            ).astype(jnp.bfloat16)
+
+        copy = pltpu.make_async_copy(
+            stage.at[i % 2], out.at[pl.ds(n * tile, tile)], stage_sem.at[i % 2]
+        )
+        copy.start()
+        copies.append(copy)
+
+    rows.first(by_block=True)
+    rows.local.wait()
+    rows.relay_block(near)
+    rows.arrive_across(z)
+    rows.arrive_across(near)
+    forward(half)
+    rows.relay_block(mid)
+    rows.relay_block(far)
+    grads.first(by_block=True)
+    downward(half)
+    total.start(near, 0)
+    total.start(z, 0)
+    rows.arrive_across(mid)
+    rows.arrive_across(far)
+    forward(1 - half)
+    grads.local.wait()
+    grads.relay_block(near)
+    downward(1 - half)
+    total.start(mid, 0)
+    total.start(far, 0)
+    total.relay_one(near, 0)
+    grads.arrive_across(z)
+    grads.arrive_across(near)
+    backward(half)
+    total.relay_one(mid, 0)
+    total.relay_one(far, 0)
+    grads.relay_block(mid)
+    grads.relay_block(far)
+    inward(half)
+    normed.start(near, 0)
     normed.start(z, 0)
-    total.start(order[2], 0)
-    total.start(z, 0)
-    for pair in order:
-        total.relay_one(pair, 0)
+    grads.arrive_across(mid)
+    grads.arrive_across(far)
+    backward(1 - half)
+    inward(1 - half)
+    normed.start(far, 0)
+    normed.start(mid, 0)
+    normed.relay_one(near, 0)
+    for i in range(2):
+        weight_grad(i)
+    normed.relay_one(far, 0)
+    weight_grad(2)
+    normed.relay_one(mid, 0)
+    for i in range(3, len(tiles)):
+        weight_grad(i)
+    total.last(0)
     normed.last(0)
-    total.last(0)
-    gather.finish()
+    for copy in copies[-2:]:
+        copy.wait()
+    rows.finish()
+    grads.finish()
     normed.finish()
     total.finish()
 
 
 def feed(rows, grads, weight, down):
-    part = down.shape[0]
+    part, width = down.shape
+    low = rows.dtype
+    tokens = rows.shape[0]
     summed = jax.ShapeDtypeStruct(rows.shape, jnp.float32)
     return pl.pallas_call(
         feed_kernel,
         out_shape=(
-            jax.ShapeDtypeStruct((PLANE, *rows.shape), rows.dtype),
-            jax.ShapeDtypeStruct((PLANE, rows.shape[0], part), rows.dtype),
-            jax.ShapeDtypeStruct((PLANE, rows.shape[0], 2 * part), rows.dtype),
             summed,
             summed,
+            jax.ShapeDtypeStruct(weight.shape, low),
+            jax.ShapeDtypeStruct(down.shape, low),
         ),
-        in_specs=[ANY] + [VMEM] * 3,
-        out_specs=(VMEM,) * 5,
+        in_specs=[ANY] * 2 + [VMEM] * 2,
+        out_specs=(VMEM,) * 2 + (ANY,) * 2,
         scratch_shapes=[
-            pltpu.VMEM((PLANE, *rows.shape), rows.dtype),
-            pltpu.VMEM((PLANE, *rows.shape), rows.dtype),
+            pltpu.VMEM((PLANE, tokens, width), low),
+            pltpu.VMEM((PLANE, tokens, width), low),
+            pltpu.VMEM((PLANE, tokens, part), jnp.float32),
+            pltpu.VMEM((PLANE, tokens, part), jnp.float32),
+            pltpu.VMEM((PLANE, tokens, part), low),
+            pltpu.VMEM((PLANE, tokens, 2 * part), low),
+            pltpu.VMEM((PLANE, tokens, width), low),
+            pltpu.VMEM((PLANE, tokens, width), low),
+            pltpu.VMEM((256, PLANE * tokens), low),
+            pltpu.VMEM((2, 256, width), low),
+            pltpu.SemaphoreType.DMA((2,)),
             *SequenceGather.scratch(2),
-            *SequenceScatter.scratch(*rows.shape, 1),
-            *SequenceScatter.scratch(*rows.shape, 1),
+            *SequenceGather.scratch(2),
+            *SequenceScatter.scratch(tokens, width, 1),
+            *SequenceScatter.scratch(tokens, width, 1),
         ],
-        compiler_params=params(5),
+        compiler_params=params(5, 60),
         name="feed",
     )(rows, grads, weight, down)
 
@@ -1573,7 +1657,6 @@
         feed_all,
         out_all,
         down_all,
-        grads_all,
     ) = attention(
         doc_starts,
         layer_in,
@@ -1583,7 +1666,6 @@
         feed_blocks,
         w_out.astype(low),
         w_down.astype(low).reshape(DOWN_PARTS, -1, width),
-        out_grad,
     )
     gain_one, gain_two = gain_rows[0], gain_rows[1]
     input_one = input_one_all.reshape(seq_len, width)
@@ -1597,20 +1679,14 @@
     layer_rows = layer_in.astype(jnp.float32)
     middle = layer_rows + branch
     normed_two, inverse_two = norm_forward(middle)
-    input_two_all, hidden_all, grad_gate_up_all, grad_normed_two, down_sum = feed(
+    grad_normed_two, down_sum, feed_term, down_term = feed(
         (normed_two * gain_two).astype(low),
-        grads_all,
+        out_grad,
         feed_all.reshape(width, 2 * ff_part),
         down_all.reshape(ff_part, width),
     )
-    input_two = input_two_all.reshape(seq_len, width)
-    hidden = hidden_all.reshape(seq_len, ff_part)
-    grad_gate_up = grad_gate_up_all.reshape(seq_len, 2 * ff_part)
     layer_out = (middle + down_sum).astype(low)
 
-    out_grads = grads_all.reshape(seq_len, width)
-    down_term = transposed_times(hidden, out_grads).astype(low)
-    feed_term = transposed_times(input_two, grad_gate_up).astype(low)
     grad_norm_two, unused = norm_backward(grad_normed_two, normed_two, inverse_two, gain_two)
     grad_middle = out_grad.astype(jnp.float32) + grad_norm_two
     grad_middle_low = grad_middle.astype(low)

time: 702 us -> 727 us (1.036)
  Pallas kernels: 577 us -> 626 us
  matrix products: 41.7 us -> 23.6 us
    pallas_call x1, Pallas kernels: 189 us -> 238 us  [feed(): pl.pallas_call(feed_kernel, out_shape=(summed, summed, jax.ShapeDtypeStru...]
    dot_general x4 -> x2, matrix products: 29.7 us -> 11.6 us  [transposed_times(): lax.dot_general(left, right, (((0,), (0,)), ((), ())), preferred_element_...]
where the time goes in v4:
time: 727 us; the launch traced here: 716 us
  Pallas kernels  626 us (86%)
  other arithmetic  34.1 us (5%)
  local copies, waits for them, and re-layouts  31.4 us (4%)
  matrix products  23.6 us (3%)
    pallas_call x1, Pallas kernels, feed(): pl.pallas_call(feed_kernel, out_shape=(summed, summed, jax.ShapeDtypeStru...  238 us
    pallas_call x1, Pallas kernels, attention(): pl.pallas_call(attention_kernel, out_shape=(jax.ShapeDtypeStruct((PLANE,...  202 us
    pallas_call x1, Pallas kernels, closing(): pl.pallas_call(closing_kernel, out_shape=(jax.ShapeDtypeStruct(rows.shape...  97.4 us
    pallas_call x1, Pallas kernels, attention_back(): pl.pallas_call(attention_back_kernel, out_shape=(jax.ShapeDtypeStruct(que...  88.4 us
    sub x5, other arithmetic, adamw(): weight - rate * (first_hat / (jnp.sqrt(second_hat) + eps_adam) + decay *...  15.2 us

profile of v4, /device:TPU:0, one launch (start us, length us, event | category | flops | bytes accessed | tf_op | source)
XLA Modules:
  0.0 716.5 jit_solution(10658622832723670935)
XLA Ops:
  3.0 2.4 convert_element_type.88
  6.8 2.8 reshape.188.blocks_ref
  13.1 201.6 %attention.1 = (bf16[8,128,2048]{2,1,0:T(8,128)(2,1)}, f32[8,128,128]{2,1,0:T(8,128)}, bf16[32,64,512]{2,1,0:T(8,128)(2,1)}, f32[8,2048]{1,0:T(8,128)}, bf16[8,2...) custom-call(s32[1,3]{1,0:T(1,128)} %starts_ref.1, ...), custom_call_target="tpu_custom_call" | custom-call | tf_op jit(solution)/shard_map/attention/pallas_call | solution.py:882
  216.0 4.7 multiply_reduce_fusion.2
  222.7 238.4 %feed.1 = (f32[128,2048]{1,0:T(8,128)}, f32[128,2048]{1,0:T(8,128)}, bf16[2048,2048]{1,0:T(8,128)(2,1)}, bf16[1024,2048]{1,0:T(8,128)(2,1)}) custom-call(bf16[128,2048]{1,0:T(8,128)(2,1)} %multiply_convert_fusion.rows_ref, bf16[128,2048]{1,0:T(8,128)(2,1)} %grads_ref.1, bf16[2048,2048]{1,0:T(8,128)(2,1)} %bitcast.101, bf16[1024,2048]{1,0:T(8,128)(2,1)} %bitcast.105), custom_call_target="tpu_custom_call" | custom-call | tf_op jit(solution)/shard_map/feed/pallas_call | solution.py:1102
  461.1 1.5 multiply_reduce_fusion.1
  462.6 2.8 multiply_add_fusion.2
  465.4 5.6 convolution_convert_fusion
  471.1 2.9 convolution_convert_fusion.3
  475.2 88.4 %attention_back.1 = (f32[8,2,2,128,64]{4,3,2,1,0:T(8,128)}, f32[1024,64]{1,0:T(8,128)}, f32[1024,64]{1,0:T(8,128)}, bf16[8,64,2048]{2,1,0:T(8,128)(2,1)}, f32[4,64,2048]{2,1,0:T(8,128)}) custom-call(bf16[8,2,2,128,64]{4,3,2,1,0:T(8,128)(2,1)} %get-tuple-element.59.query_ref, bf16[8,128,64]{2,1,0:T(8,128)(2,1)} %get-tuple-element.60.key_ref, ...), custom_call_target="tpu_custom_call" | custom-call | tf_op jit(solution)/shard_map/attention_back/pallas_call | solution.py:1202
  563.7 2.3 copy.78
  567.7 1.4 add_convert_fusion.1
  571.6 6.0 convolution_convert_fusion.2
  577.6 4.4 convolution_convert_fusion.1
  582.0 97.4 %closing.1 = (f32[128,2048]{1,0:T(8,128)}, bf16[8,64,384]{2,1,0:T(8,128)(2,1)}, f32[64,2048]{1,0:T(8,128)}) custom-call(bf16[8,128,2048]{2,1,0:T(8,128)(2,1)} %bitcast.104, bf16[32,64,384]{2,1,0:T(8,128)(2,1)} %bitcast.115, bf16[32,64,2048]{2,1,0:T(8,128)(2,1)} %bitcast.89), custom_call_target="tpu_custom_call" | custom-call | tf_op jit(solution)/shard_map/closing/pallas_call | solution.py:1261
  681.4 2.3 multiply_subtract_fusion.2
  684.8 2.2 multiply_subtract_fusion.4
  687.0 6.2 reshape.211
  693.2 4.8 copy.85
  698.0 2.4 copy.90
  701.5 6.2 multiply_subtract_fusion
  708.8 1.3 fusion.8
  710.2 4.0 multiply_subtract_fusion.1
  715.0 1.3 copy.100
  (126 shorter events, 21.8 us)
Async XLA Ops:
  6.8 2.8 copy-start.23
  6.8 3.4 copy-start.13
  6.8 3.4 copy-start.31
  12.4 203.6 %copy-start.2 = (bf16[128,2048]{1,0:T(8,128)(2,1)S(1)}, bf16[128,2048]{1,0:T(8,128)(2,1)}, u32[]{:S(2)}) copy-start(bf16[128,2048]{1,0:T(8,128)(2,1)} %rows_ref.1) | copy-start | bytes 1572868
  222.6 239.9 %copy-start.20 = (bf16[128,2048]{1,0:T(8,128)(2,1)S(1)}, bf16[128,2048]{1,0:T(8,128)(2,1)}, u32[]{:S(2)}) copy-start(bf16[128,2048]{1,0:T(8,128)(2,1)} %grads_ref.1) | copy-start | bytes 1572868
  462.6 8.5 %slice-start = ((s8[8388608]{0:T(1024)(128)(4,1)}), s8[4194304]{0:T(1024)(128)(4,1)S(1)}, s32[]{:S(2)}) async-start(s8[8388608]{0:T(1024)(128)(4,1)} %bitcast.86), calls=%async_computation | async-start | bytes 8388608
  465.4 5.6 slice-start.1
  563.7 3.4 copy-start.11
  567.3 2.5 copy-start.12
  571.6 6.0 copy-start.25
  571.6 6.0 copy-start.34
  582.0 98.8 %copy-start.29 = (f32[64,2048]{1,0:T(8,128)S(1)}, f32[64,2048]{1,0:T(8,128)}, u32[]{:S(2)}) copy-start(f32[64,2048]{1,0:T(8,128)} %param.30) | copy-start | bytes 1572868
  680.8 2.9 copy-start.17
  684.8 8.4 %copy-start.22 = (f32[64,1024]{1,0:T(8,128)}, f32[64,1024]{1,0:T(8,128)S(1)}, u32[]{:S(2)}) copy-start(f32[64,1024]{1,0:T(8,128)S(1)} %reshape.208) | copy-start | bytes 786436
  693.2 7.2 %copy-start.8 = (f32[64,16384]{1,0:T(8,128)S(1)}, f32[64,16384]{1,0:T(8,128)}, u32[]{:S(2)}) copy-start(f32[64,16384]{1,0:T(8,128)} %param.39) | copy-start | bytes 12582916
  697.9 3.5 copy-start.7
  700.3 7.3 %copy-start.1 = (f32[8,8,64,256]{3,1,2,0:T(8,128)}, f32[8,8,64,256]{3,1,2,0:T(8,128)S(1)}, u32[]{:S(2)}) copy-start(f32[8,8,64,256]{3,1,2,0:T(8,128)S(1)} %copy.90) | copy-start | bytes 12582916
  701.5 6.2 copy-start.32
  701.5 6.2 copy-start.33
  701.5 7.0 copy-start.6
  701.5 8.7 %copy-start.9 = (f32[256,2048]{1,0:T(8,128)S(1)}, f32[256,2048]{1,0:T(8,128)}, u32[]{:S(2)}) copy-start(f32[256,2048]{1,0:T(8,128)} %param.43) | copy-start | bytes 6291460
  701.5 8.7 %copy-start.10 = (f32[256,2048]{1,0:T(8,128)S(1)}, f32[256,2048]{1,0:T(8,128)}, u32[]{:S(2)}) copy-start(f32[256,2048]{1,0:T(8,128)} %param.42) | copy-start | bytes 6291460
  707.7 2.5 copy-start.4
  710.2 4.0 copy-start.19
  (13 other events, 22.8 us)

commit v5 on v4

--- a/solution.py
+++ b/solution.py
@@ -423,26 +423,32 @@
             pltpu.SemaphoreType.DMA(()),
         ] + ChipGather.scratch(PLANE)
 
-    def first(self):
+    def send(self, off):
+        to = lax.rem(self.c + off, PLANE)
+        copy = remote(
+            self.blocks.at[to],
+            self.out.at[self.d * PLANE + self.c],
+            self.ps.at[off],
+            self.pr.at[self.c],
+            self.d,
+            to,
+        )
+        copy.start()
+        self.sent.append(copy)
+
+    def first(self, ahead=PLANE - 1):
+        self.ahead = ahead
         self.local = pltpu.make_async_copy(
             self.blocks.at[self.c], self.out.at[self.d * PLANE + self.c], self.local_sem
         )
         self.local.start()
-        for off in range(1, PLANE):
-            to = lax.rem(self.c + off, PLANE)
-            copy = remote(
-                self.blocks.at[to],
-                self.out.at[self.d * PLANE + self.c],
-                self.ps.at[off],
-                self.pr.at[self.c],
-                self.d,
-                to,
-            )
-            copy.start()
-            self.sent.append(copy)
+        for off in range(1, 1 + ahead):
+            self.send(off)
         self.chip.start(self.c, self.blocks.at[self.c])
 
     def relay(self, off):
+        if off + self.ahead < PLANE:
+            self.send(off + self.ahead)
         source = lax.rem(self.c + PLANE - off, PLANE)
         block = self.out.at[self.d * PLANE + source]
         remote(
@@ -690,6 +696,7 @@
     blocks_ref,
     out_rows_ref,
     down_ref,
+    grads_ref,
     input_out,
     table_out,
     qkv_out,
@@ -704,6 +711,7 @@
     blocks_out,
     out_rows_out,
     down_out,
+    grads_out,
     *scratch,
 ):
     mixed_stage, spots_all, rows_all = scratch[:3]
@@ -721,6 +729,7 @@
     outs_chip = ChipGather(out_rows_out, take(4), PLANE)
     rows = SequenceGather(rows_ref, rows_all, take(5), 2)
     table = SequenceGather(table_ref, table_out, take(5), 1)
+    grads = SequenceGather(grads_ref, grads_out, take(5), CHUNKS)
     down = ChipGather(down_out, take(4), DOWN_PARTS)
     spot_send, spot_recv, spot_local, down_local = take(4)
     greet(plane_peers(d, c) + chip_peers(d, c, x, core))
@@ -751,10 +760,10 @@
         qkv.relay(off)
     table.relay(0)
     rows.relay_block(order[0])
+    weights.first(2)
     qkv.relay_chip()
     rows.relay_block(order[1])
     rows.relay_block(order[2])
-    weights.first()
     for off in range(1, PLANE):
         source = lax.rem(c + off, PLANE)
         block = spots_all.at[source]
@@ -822,9 +831,12 @@
     outs.relay(0)
     for source in order:
         outs_chip.start(source * YS + y)
-    for pair in order:
+    weights.relay(1)
+    grads.first()
+    for step, pair in enumerate(order):
         rows.arrive_across(pair)
         project(pair)
+        weights.relay(step + 2)
     rows.finish()
     for other in range(ZS):
         outs.arrive_across(other)
@@ -854,15 +866,25 @@
             mixed_stage[block, pair] = jnp.concatenate(halves, axis=1)
 
         exchange.send(step)
-        if step < PLANE:
-            weights.relay(step)
-    for j in range(DOWN_PARTS):
-        down.relay(j)
-    for off in range(PLANE):
-        outs_chip.relay(lax.rem(c + off, PLANE))
-    weights.relay_chip()
+        if step < 4:
+            weights.relay(step + 4)
+        if step == 4:
+            for j in range(DOWN_PARTS):
+                down.relay(j)
+        if step == 5:
+            for off in range(PLANE):
+                outs_chip.relay(lax.rem(c + off, PLANE))
+        if step > 5:
+            grads.relay(step - 6)
+    for off in range(4):
+        weights.chip.relay(lax.rem(c + PLANE - off, PLANE))
+    for k in (3,):
+        grads.relay(k)
+    for off in range(4, PLANE):
+        weights.chip.relay(lax.rem(c + PLANE - off, PLANE))
     for off in range(1, PLANE + 1):
         exchange.arrive(off)
+    grads.last()
     down.last()
     outs_chip.last()
     weights.last()
@@ -874,7 +896,7 @@
     down_own.wait()
 
 
-def attention(starts, rows, table, spots, qkv, blocks, out_rows, down):
+def attention(starts, rows, table, spots, qkv, blocks, out_rows, down, grads):
     low, full = jnp.bfloat16, jnp.float32
     tokens, width = rows.shape
     mixed = jax.ShapeDtypeStruct((PLANE, PAIRS, tokens, 2 * HEAD_SIZE), low)
@@ -896,9 +918,10 @@
             jax.ShapeDtypeStruct((RANKS, *blocks.shape[1:]), low),
             jax.ShapeDtypeStruct((RANKS, *out_rows.shape), low),
             jax.ShapeDtypeStruct((4 * DOWN_PARTS, *down.shape[1:]), low),
+            jax.ShapeDtypeStruct((PLANE, *grads.shape), low),
         ),
-        in_specs=[pl.BlockSpec(memory_space=pltpu.SMEM)] + [ANY] * 7,
-        out_specs=(VMEM,) * 11 + (ANY,) * 3,
+        in_specs=[pl.BlockSpec(memory_space=pltpu.SMEM)] + [ANY] * 8,
+        out_specs=(VMEM,) * 11 + (ANY,) * 4,
         scratch_shapes=[
             pltpu.VMEM(mixed.shape, low),
             pltpu.VMEM((PLANE, *spots.shape), full),
@@ -910,6 +933,7 @@
             *ChipGather.scratch(PLANE),
             *SequenceGather.scratch(2),
             *SequenceGather.scratch(1),
+            *SequenceGather.scratch(CHUNKS),
             *ChipGather.scratch(DOWN_PARTS),
             pltpu.SemaphoreType.DMA((PLANE,)),
             pltpu.SemaphoreType.DMA((PLANE,)),
@@ -918,12 +942,12 @@
         ],
         compiler_params=params(2),
         name="attention",
-    )(starts, rows, table, spots, qkv, blocks, out_rows, down)
+    )(starts, rows, table, spots, qkv, blocks, out_rows, down, grads)
 
 
 def feed_kernel(
     rows_ref,
-    grads_ref,
+    grads_all,
     weight_ref,
     down_ref,
     normed_out,
@@ -932,16 +956,15 @@
     down_grad_out,
     *scratch,
 ):
-    rows_all, grads_all, slope_gate, slope_up, hidden_all, gate_grads = scratch[:6]
-    normed_parts, down_parts, turned, stage, stage_sem = scratch[6:11]
-    scratch = list(scratch[11:])
+    rows_all, slope_gate, slope_up, hidden_all, gate_grads = scratch[:5]
+    normed_parts, down_parts, turned, stage, stage_sem = scratch[5:10]
+    scratch = list(scratch[10:])
 
     def take(count):
         taken, scratch[:count] = scratch[:count], []
         return taken
 
     rows = SequenceGather(rows_ref, rows_all, take(5), 2)
-    grads = SequenceGather(grads_ref, grads_all, take(5), 2)
     normed = SequenceScatter(normed_parts, normed_out, *take(2), take(4), 1)
     total = SequenceScatter(down_parts, total_out, *take(2), take(4), 1)
     d, c, x, core, z, y = place()
@@ -1047,49 +1070,38 @@
     forward(half)
     rows.relay_block(mid)
     rows.relay_block(far)
-    grads.first(by_block=True)
-    downward(half)
-    total.start(near, 0)
-    total.start(z, 0)
+    backward(half)
+    inward(half)
+    normed.start(near, 0)
+    normed.start(z, 0)
     rows.arrive_across(mid)
     rows.arrive_across(far)
     forward(1 - half)
-    grads.local.wait()
-    grads.relay_block(near)
-    downward(1 - half)
-    total.start(mid, 0)
-    total.start(far, 0)
-    total.relay_one(near, 0)
-    grads.arrive_across(z)
-    grads.arrive_across(near)
-    backward(half)
-    total.relay_one(mid, 0)
-    total.relay_one(far, 0)
-    grads.relay_block(mid)
-    grads.relay_block(far)
-    inward(half)
-    normed.start(near, 0)
-    normed.start(z, 0)
-    grads.arrive_across(mid)
-    grads.arrive_across(far)
     backward(1 - half)
     inward(1 - half)
     normed.start(far, 0)
     normed.start(mid, 0)
     normed.relay_one(near, 0)
+    downward(1 - half)
+    total.start(far, 0)
+    total.start(mid, 0)
+    normed.relay_one(far, 0)
+    downward(half)
+    total.start(near, 0)
+    total.start(z, 0)
+    normed.relay_one(mid, 0)
     for i in range(2):
         weight_grad(i)
-    normed.relay_one(far, 0)
-    weight_grad(2)
-    normed.relay_one(mid, 0)
-    for i in range(3, len(tiles)):
+    for pair in (far, mid, near):
+        total.relay_one(pair, 0)
+        weight_grad(len(copies))
+    for i in range(len(copies), len(tiles)):
         weight_grad(i)
+    normed.last(0)
     total.last(0)
-    normed.last(0)
     for copy in copies[-2:]:
         copy.wait()
     rows.finish()
-    grads.finish()
     normed.finish()
     total.finish()
 
@@ -1107,10 +1119,9 @@
             jax.ShapeDtypeStruct(weight.shape, low),
             jax.ShapeDtypeStruct(down.shape, low),
         ),
-        in_specs=[ANY] * 2 + [VMEM] * 2,
+        in_specs=[ANY] + [VMEM] * 3,
         out_specs=(VMEM,) * 2 + (ANY,) * 2,
         scratch_shapes=[
-            pltpu.VMEM((PLANE, tokens, width), low),
             pltpu.VMEM((PLANE, tokens, width), low),
             pltpu.VMEM((PLANE, tokens, part), jnp.float32),
             pltpu.VMEM((PLANE, tokens, part), jnp.float32),
@@ -1121,7 +1132,6 @@
             pltpu.VMEM((256, PLANE * tokens), low),
             pltpu.VMEM((2, 256, width), low),
             pltpu.SemaphoreType.DMA((2,)),
-            *SequenceGather.scratch(2),
             *SequenceGather.scratch(2),
             *SequenceScatter.scratch(tokens, width, 1),
             *SequenceScatter.scratch(tokens, width, 1),
@@ -1657,6 +1667,7 @@
         feed_all,
         out_all,
         down_all,
+        grads_all,
     ) = attention(
         doc_starts,
         layer_in,
@@ -1666,6 +1677,7 @@
         feed_blocks,
         w_out.astype(low),
         w_down.astype(low).reshape(DOWN_PARTS, -1, width),
+        out_grad,
     )
     gain_one, gain_two = gain_rows[0], gain_rows[1]
     input_one = input_one_all.reshape(seq_len, width)
@@ -1681,7 +1693,7 @@
     normed_two, inverse_two = norm_forward(middle)
     grad_normed_two, down_sum, feed_term, down_term = feed(
         (normed_two * gain_two).astype(low),
-        out_grad,
+        grads_all,
         feed_all.reshape(width, 2 * ff_part),
         down_all.reshape(ff_part, width),
     )

time: 727 us -> 754 us (1.037)
  Pallas kernels: 626 us -> 648 us
    pallas_call x1, Pallas kernels: 202 us -> 249 us  [attention(): pl.pallas_call(attention_kernel, out_shape=(jax.ShapeDtypeStruct((PLANE,...]
    pallas_call x1, Pallas kernels: 238 us -> 211 us  [feed(): pl.pallas_call(feed_kernel, out_shape=(summed, summed, jax.ShapeDtypeStru...]
where the time goes in v5:
time: 754 us; the launch traced here: 744 us
  Pallas kernels  648 us (86%)
  local copies, waits for them, and re-layouts  35.6 us (5%)
  other arithmetic  35.2 us (5%)
  matrix products  23.6 us (3%)
    pallas_call x1, Pallas kernels, attention(): pl.pallas_call(attention_kernel, out_shape=(jax.ShapeDtypeStruct((PLANE,...  249 us
    pallas_call x1, Pallas kernels, feed(): pl.pallas_call(feed_kernel, out_shape=(summed, summed, jax.ShapeDtypeStru...  211 us
    pallas_call x1, Pallas kernels, closing(): pl.pallas_call(closing_kernel, out_shape=(jax.ShapeDtypeStruct(rows.shape...  99.5 us
    pallas_call x1, Pallas kernels, attention_back(): pl.pallas_call(attention_back_kernel, out_shape=(jax.ShapeDtypeStruct(que...  89 us
    sub x5, other arithmetic, adamw(): weight - rate * (first_hat / (jnp.sqrt(second_hat) + eps_adam) + decay *...  16.5 us

profile of v5, /device:TPU:0, one launch (start us, length us, event | category | flops | bytes accessed | tf_op | source)
XLA Modules:
  0.0 744.2 jit_solution(12839423166901348106)
XLA Ops:
  3.0 2.4 convert_element_type.88
  6.0 2.1 copy.94
  8.1 4.6 reshape.188.blocks_ref
  17.9 249.1 %attention.1 = (bf16[8,128,2048]{2,1,0:T(8,128)(2,1)}, f32[8,128,128]{2,1,0:T(8,128)}, bf16[32,64,512]{2,1,0:T(8,128)(2,1)}, f32[8,2048]{1,0:T(8,128)}, bf16[8,2...) custom-call(s32[1,3]{1,0:T(1,128)} %starts_ref.1, ...), custom_call_target="tpu_custom_call" | custom-call | tf_op jit(solution)/shard_map/attention/pallas_call | solution.py:904
  268.3 4.7 multiply_reduce_fusion.2
  274.9 210.9 %feed.1 = (f32[128,2048]{1,0:T(8,128)}, f32[128,2048]{1,0:T(8,128)}, bf16[2048,2048]{1,0:T(8,128)(2,1)}, bf16[1024,2048]{1,0:T(8,128)(2,1)}) custom-call(bf16[128,2048]{1,0:T(8,128)(2,1)} %multiply_convert_fusion.rows_ref, bf16[8,128,2048]{2,1,0:T(8,128)(2,1)} %get-tuple-element.56.grads_all, bf16[2048,2048]{1,0:T(8,128)(2,1)} %bitcast.98, ...), custom_call_target="tpu_custom_call" | custom-call | tf_op jit(solution)/shard_map/feed/pallas_call | solution.py:1114
  485.8 1.5 multiply_reduce_fusion.1
  487.3 2.8 multiply_add_fusion.2
  490.2 5.6 convolution_convert_fusion
  495.8 2.9 convolution_convert_fusion.3
  500.0 89.0 %attention_back.1 = (f32[8,2,2,128,64]{4,3,2,1,0:T(8,128)}, f32[1024,64]{1,0:T(8,128)}, f32[1024,64]{1,0:T(8,128)}, bf16[8,64,2048]{2,1,0:T(8,128)(2,1)}, f32[4,64,2048]{2,1,0:T(8,128)}) custom-call(bf16[8,2,2,128,64]{4,3,2,1,0:T(8,128)(2,1)} %get-tuple-element.61.query_ref, bf16[8,128,64]{2,1,0:T(8,128)(2,1)} %get-tuple-element.62.key_ref, ...), custom_call_target="tpu_custom_call" | custom-call | tf_op jit(solution)/shard_map/attention_back/pallas_call | solution.py:1212
  589.0 2.3 copy.78
  593.0 1.4 add_convert_fusion.1
  596.9 6.0 convolution_convert_fusion.2
  602.9 4.4 convolution_convert_fusion.1
  607.4 99.5 %closing.1 = (f32[128,2048]{1,0:T(8,128)}, bf16[8,64,384]{2,1,0:T(8,128)(2,1)}, f32[64,2048]{1,0:T(8,128)}) custom-call(bf16[8,128,2048]{2,1,0:T(8,128)(2,1)} %bitcast.104, bf16[32,64,384]{2,1,0:T(8,128)(2,1)} %bitcast.115, bf16[32,64,2048]{2,1,0:T(8,128)(2,1)} %bitcast.89), custom_call_target="tpu_custom_call" | custom-call | tf_op jit(solution)/shard_map/closing/pallas_call | solution.py:1271
  708.1 3.5 multiply_subtract_fusion.2
  712.5 2.2 multiply_subtract_fusion.4
  714.8 6.2 reshape.211
  720.9 4.8 copy.85
  725.7 2.4 copy.90
  729.3 6.2 multiply_subtract_fusion
  736.6 1.3 fusion.8
  738.0 4.0 multiply_subtract_fusion.1
  (122 shorter events, 23.1 us)
Async XLA Ops:
  5.9 6.8 copy-start.22
  6.0 9.0 %copy-start.14 = (f32[64,2048]{1,0:T(8,128)S(1)}, f32[64,2048]{1,0:T(8,128)}, u32[]{:S(2)}) copy-start(f32[64,2048]{1,0:T(8,128)} %param.29) | copy-start | bytes 1572868
  8.1 6.9 copy-start.29
  8.1 7.9 %copy-start.3 = (f32[256,2048]{1,0:T(8,128)S(1)}, f32[256,2048]{1,0:T(8,128)}, u32[]{:S(2)}) copy-start(f32[256,2048]{1,0:T(8,128)} %param.41) | copy-start | bytes 6291460
  17.2 251.1 %copy-start.2 = (bf16[128,2048]{1,0:T(8,128)(2,1)S(1)}, bf16[128,2048]{1,0:T(8,128)(2,1)}, u32[]{:S(2)}) copy-start(bf16[128,2048]{1,0:T(8,128)(2,1)} %rows_ref.1) | copy-start | bytes 1572868
  274.9 212.4 %copy-start.11 = (bf16[128,2048]{1,0:T(8,128)(2,1)S(1)}, bf16[128,2048]{1,0:T(8,128)(2,1)}, u32[]{:S(2)}) copy-start(bf16[128,2048]{1,0:T(8,128)(2,1)} %grads_ref.1) | copy-start | bytes 1572868
  487.3 8.5 %slice-start = ((s8[8388608]{0:T(1024)(128)(4,1)}), s8[4194304]{0:T(1024)(128)(4,1)S(1)}, s32[]{:S(2)}) async-start(s8[8388608]{0:T(1024)(128)(4,1)} %bitcast.86), calls=%async_computation | async-start | bytes 8388608
  490.2 5.6 slice-start.1
  596.9 6.0 copy-start.24
  596.9 6.0 copy-start.32
  607.3 100.7 %copy-start.15 = (f32[64,2048]{1,0:T(8,128)S(1)}, f32[64,2048]{1,0:T(8,128)}, u32[]{:S(2)}) copy-start(f32[64,2048]{1,0:T(8,128)} %param.29) | copy-start | bytes 1572868
  607.3 100.7 %copy-start.17 = (f32[64,2048]{1,0:T(8,128)S(1)}, f32[64,2048]{1,0:T(8,128)}, u32[]{:S(2)}) copy-start(f32[64,2048]{1,0:T(8,128)} %param.35) | copy-start | bytes 1572868
  607.3 100.7 %copy-start.25 = (f32[64,2048]{1,0:T(8,128)S(1)}, f32[64,2048]{1,0:T(8,128)}, u32[]{:S(2)}) copy-start(f32[64,2048]{1,0:T(8,128)} %param.37) | copy-start | bytes 1572868
  607.4 100.7 %copy-start.26 = (f32[64,2048]{1,0:T(8,128)S(1)}, f32[64,2048]{1,0:T(8,128)}, u32[]{:S(2)}) copy-start(f32[64,2048]{1,0:T(8,128)} %param.36) | copy-start | bytes 1572868
  607.4 100.7 %copy-start.27 = (f32[64,2048]{1,0:T(8,128)S(1)}, f32[64,2048]{1,0:T(8,128)}, u32[]{:S(2)}) copy-start(f32[64,2048]{1,0:T(8,128)} %param.31) | copy-start | bytes 1572868
  607.4 100.7 %copy-start.28 = (f32[64,2048]{1,0:T(8,128)S(1)}, f32[64,2048]{1,0:T(8,128)}, u32[]{:S(2)}) copy-start(f32[64,2048]{1,0:T(8,128)} %param.30) | copy-start | bytes 1572868
  712.5 13.2 %copy-start.21 = (f32[64,1024]{1,0:T(8,128)}, f32[64,1024]{1,0:T(8,128)S(1)}, u32[]{:S(2)}) copy-start(f32[64,1024]{1,0:T(8,128)S(1)} %reshape.208) | copy-start | bytes 786436
  720.9 7.2 copy-start.8
  728.1 7.3 copy-start.1
  729.3 6.2 copy-start.30
  729.3 6.2 copy-start.31
  729.3 7.0 copy-start.6
  729.3 8.7 %copy-start.9 = (f32[256,2048]{1,0:T(8,128)S(1)}, f32[256,2048]{1,0:T(8,128)}, u32[]{:S(2)}) copy-start(f32[256,2048]{1,0:T(8,128)} %param.43) | copy-start | bytes 6291460
  729.3 8.7 %copy-start.10 = (f32[256,2048]{1,0:T(8,128)S(1)}, f32[256,2048]{1,0:T(8,128)}, u32[]{:S(2)}) copy-start(f32[256,2048]{1,0:T(8,128)} %param.42) | copy-start | bytes 6291460
  (11 other events, 37.5 us)

commit v6 on v5

--- a/solution.py
+++ b/solution.py
@@ -350,8 +350,8 @@
 
 
 class ChipGather:
-    def __init__(self, out, sems, count):
-        self.out, self.count = out, count
+    def __init__(self, out, sems, count, rows=None):
+        self.out, self.count, self.rows = out, count, rows
         self.cs, self.cr, self.xs, self.xr = sems
         self.d, self.c, self.x, self.core, _, _ = place()
         self.sent = []
@@ -365,9 +365,14 @@
             pltpu.SemaphoreType.DMA((count,)),
         ]
 
+    def block(self, slot):
+        if self.rows is None:
+            return self.out.at[slot]
+        return self.out.at[pl.ds(slot * self.rows, self.rows)]
+
     def to_core(self, far, j, src=None):
         x = 1 - self.x if far else self.x
-        block = self.out.at[(x * 2 + self.core) * self.count + j]
+        block = self.block((x * 2 + self.core) * self.count + j)
         return remote(
             block if src is None else src,
             block,
@@ -378,7 +383,7 @@
         )
 
     def to_x(self, j, src=None):
-        block = self.out.at[self.d * self.count + j]
+        block = self.block(self.d * self.count + j)
         return remote(
             block if src is None else src,
             block,
@@ -685,6 +690,13 @@
 
 
 QKV_WIDTH = (GROUP + 2) * HEAD_SIZE
+
+
+def wide_columns(width):
+    run = width // (8 * PLANE)
+    for to in range(PLANE):
+        for part in range(8):
+            yield to, part * run, (part * PLANE + to) * run
 
 
 def attention_kernel(
@@ -714,8 +726,9 @@
     grads_out,
     *scratch,
 ):
-    mixed_stage, spots_all, rows_all = scratch[:3]
-    scratch = list(scratch[3:])
+    mixed_stage, spots_all, rows_all, wide_full, wide_blocks = scratch[:5]
+    down_full, down_blocks, out_full, out_block, load_sem = scratch[5:10]
+    scratch = list(scratch[10:])
 
     def take(count):
         taken, scratch[:count] = scratch[:count], []
@@ -724,17 +737,26 @@
     d, c, x, core, z, y = place()
     exchange = PlaneExchange(mixed_stage, mixed_out, take(3))
     qkv = WeightGather(qkv_ref, qkv_out, take(7))
-    weights = WeightGather(blocks_ref, blocks_out, take(7))
-    outs = SequenceGather(out_rows_ref, out_rows_out.at[pl.ds(d * PLANE, PLANE)], take(5), 1)
+    weights = WeightGather(wide_blocks, blocks_out, take(7))
+    outs = SequenceGather(out_block, out_rows_out.at[pl.ds(d * PLANE, PLANE)], take(5), 1)
     outs_chip = ChipGather(out_rows_out, take(4), PLANE)
     rows = SequenceGather(rows_ref, rows_all, take(5), 2)
     table = SequenceGather(table_ref, table_out, take(5), 1)
     grads = SequenceGather(grads_ref, grads_out, take(5), CHUNKS)
-    down = ChipGather(down_out, take(4), DOWN_PARTS)
+    down_rows = down_ref.shape[0] // DOWN_PARTS
+    down = ChipGather(down_out, take(4), DOWN_PARTS, down_rows)
     spot_send, spot_recv, spot_local, down_local = take(4)
     greet(plane_peers(d, c) + chip_peers(d, c, x, core))
     order = near_first(z)
 
+    loads = [
+        pltpu.make_async_copy(source, target, load_sem.at[i])
+        for i, (source, target) in enumerate(
+            [(out_rows_ref, out_full), (down_ref, down_full), (blocks_ref, wide_full)]
+        )
+    ]
+    for load in loads:
+        load.start()
     qkv.first()
     spots_own = pltpu.make_async_copy(spots_ref, spots_all.at[c], spot_local)
     spots_own.start()
@@ -748,22 +770,42 @@
         spots_sent.append(copy)
     table.first()
     rows.first(by_block=True)
+    loads[1].wait()
+
+    @pl.loop(0, down_full.shape[0], step=16)
+    def _(r):
+        at = pl.ds(pl.multiple_of(r, 16), 16)
+        down_blocks[at] = down_full[at].astype(jnp.bfloat16)
+
     down_own = pltpu.make_async_copy(
-        down_ref, down_out.at[pl.ds(d * DOWN_PARTS, DOWN_PARTS)], down_local
+        down_blocks, down_out.at[pl.ds(d * down_full.shape[0], down_full.shape[0])], down_local
     )
     down_own.start()
     for j in range(DOWN_PARTS):
-        down.start(j, down_ref.at[j])
+        down.start(j, down_blocks.at[pl.ds(j * down_rows, down_rows)])
+    loads[0].wait()
+    out_block[...] = out_full[...].astype(jnp.bfloat16)
     outs.first()
-    outs_chip.start(c, out_rows_ref)
+    outs_chip.start(c, out_block)
+    loads[2].wait()
+
+    @pl.loop(0, wide_full.shape[0], step=16)
+    def _(r):
+        at = pl.ds(pl.multiple_of(r, 16), 16)
+        for to, start, after in wide_columns(wide_full.shape[1]):
+            size = wide_full.shape[1] // (8 * PLANE)
+            wide_blocks[to, at, start : start + size] = wide_full[
+                at, after : after + size
+            ].astype(jnp.bfloat16)
+
     for off in range(1, PLANE):
         qkv.relay(off)
     table.relay(0)
     rows.relay_block(order[0])
-    weights.first(2)
     qkv.relay_chip()
     rows.relay_block(order[1])
     rows.relay_block(order[2])
+    weights.first()
     for off in range(1, PLANE):
         source = lax.rem(c + off, PLANE)
         block = spots_all.at[source]
@@ -831,16 +873,14 @@
     outs.relay(0)
     for source in order:
         outs_chip.start(source * YS + y)
-    weights.relay(1)
-    grads.first()
-    for step, pair in enumerate(order):
+    for pair in order:
         rows.arrive_across(pair)
         project(pair)
-        weights.relay(step + 2)
     rows.finish()
     for other in range(ZS):
         outs.arrive_across(other)
         outs_chip.start(other * YS + 1 - y)
+    grads.first()
 
     for step in range(1, PLANE + 1):
         block = lax.rem(c + step, PLANE)
@@ -866,22 +906,15 @@
             mixed_stage[block, pair] = jnp.concatenate(halves, axis=1)
 
         exchange.send(step)
-        if step < 4:
-            weights.relay(step + 4)
-        if step == 4:
-            for j in range(DOWN_PARTS):
-                down.relay(j)
-        if step == 5:
-            for off in range(PLANE):
-                outs_chip.relay(lax.rem(c + off, PLANE))
-        if step > 5:
-            grads.relay(step - 6)
-    for off in range(4):
-        weights.chip.relay(lax.rem(c + PLANE - off, PLANE))
-    for k in (3,):
+        if step < PLANE:
+            weights.relay(step)
+    for k in range(CHUNKS):
         grads.relay(k)
-    for off in range(4, PLANE):
-        weights.chip.relay(lax.rem(c + PLANE - off, PLANE))
+    for j in range(DOWN_PARTS):
+        down.relay(j)
+    for off in range(PLANE):
+        outs_chip.relay(lax.rem(c + off, PLANE))
+    weights.relay_chip()
     for off in range(1, PLANE + 1):
         exchange.arrive(off)
     grads.last()
@@ -901,6 +934,7 @@
     tokens, width = rows.shape
     mixed = jax.ShapeDtypeStruct((PLANE, PAIRS, tokens, 2 * HEAD_SIZE), low)
     seq_len = PLANE * tokens
+    wide_block = (blocks.shape[0], blocks.shape[1] // PLANE)
     return pl.pallas_call(
         attention_kernel,
         out_shape=(
@@ -915,9 +949,9 @@
             jax.ShapeDtypeStruct((PLANE, tokens, 1), full),
             jax.ShapeDtypeStruct((8, seq_len), full),
             mixed,
-            jax.ShapeDtypeStruct((RANKS, *blocks.shape[1:]), low),
+            jax.ShapeDtypeStruct((RANKS, *wide_block), low),
             jax.ShapeDtypeStruct((RANKS, *out_rows.shape), low),
-            jax.ShapeDtypeStruct((4 * DOWN_PARTS, *down.shape[1:]), low),
+            jax.ShapeDtypeStruct((4 * down.shape[0], down.shape[1]), low),
             jax.ShapeDtypeStruct((PLANE, *grads.shape), low),
         ),
         in_specs=[pl.BlockSpec(memory_space=pltpu.SMEM)] + [ANY] * 8,
@@ -926,6 +960,13 @@
             pltpu.VMEM(mixed.shape, low),
             pltpu.VMEM((PLANE, *spots.shape), full),
             pltpu.VMEM((PLANE, tokens, width), low),
+            pltpu.VMEM(blocks.shape, full),
+            pltpu.VMEM((PLANE, *wide_block), low),
+            pltpu.VMEM(down.shape, full),
+            pltpu.VMEM(down.shape, low),
+            pltpu.VMEM(out_rows.shape, full),
+            pltpu.VMEM(out_rows.shape, low),
+            pltpu.SemaphoreType.DMA((3,)),
             *PlaneExchange.scratch(),
             *WeightGather.scratch(),
             *WeightGather.scratch(),
@@ -1154,14 +1195,15 @@
     query_out,
     key_out,
     value_out,
-    out_ref,
+    wide_out,
     down_out,
     *scratch,
 ):
-    mixed_all = scratch[0]
-    exchange = PlaneExchange(mixed_ref, mixed_all, scratch[1:4])
-    weights = WeightScatter(parts_ref, out_ref, scratch[4:8], scratch[8:14])
-    down = ChipScatter(down_ref, *scratch[14:17], scratch[17:], DOWN_PARTS)
+    mixed_all, out_ref = scratch[:2]
+    scratch = scratch[2:]
+    exchange = PlaneExchange(mixed_ref, mixed_all, scratch[:3])
+    weights = WeightScatter(parts_ref, out_ref, scratch[3:7], scratch[7:13])
+    down = ChipScatter(down_ref, *scratch[13:16], scratch[16:], DOWN_PARTS)
     d, c, x, core, z, y = place()
     greet(plane_peers(d, c) + chip_peers(d, c, x, core))
     for off in range(1, PLANE + 1):
@@ -1204,6 +1246,9 @@
     for j in range(DOWN_PARTS):
         down.total(j, down_out.at[j])
     weights.last()
+    for source, start, after in wide_columns(wide_out.shape[1]):
+        size = wide_out.shape[1] // (8 * PLANE)
+        wide_out[:, after : after + size] = out_ref[source, :, start : start + size]
     down.finish()
     exchange.finish()
 
@@ -1215,13 +1260,14 @@
             jax.ShapeDtypeStruct(query.shape, jnp.float32),
             jax.ShapeDtypeStruct((PLANE * keys.shape[1], HEAD_SIZE), jnp.float32),
             jax.ShapeDtypeStruct((PLANE * values.shape[1], HEAD_SIZE), jnp.float32),
-            jax.ShapeDtypeStruct((PLANE, *parts.shape[1:]), parts.dtype),
+            jax.ShapeDtypeStruct((parts.shape[1], PLANE * parts.shape[2]), parts.dtype),
             jax.ShapeDtypeStruct((DOWN_PARTS, *down.shape[1:]), jnp.float32),
         ),
         in_specs=[VMEM] * 9,
         out_specs=(VMEM,) * 5,
         scratch_shapes=[
             pltpu.VMEM(mixed.shape, jnp.bfloat16),
+            pltpu.VMEM((PLANE, *parts.shape[1:]), parts.dtype),
             *PlaneExchange.scratch(),
             *WeightScatter.scratch(*parts.shape[1:]),
             *ChipScatter.scratch(DOWN_PARTS, *down.shape[1:]),
@@ -1231,7 +1277,9 @@
     )(query, keys, values, spots, starts, key_spots, mixed, parts, down)
 
 
-def closing_kernel(rows_ref, parts_ref, outs_ref, rows_out, out_ref, outs_out, *scratch):
+def closing_kernel(
+    rows_ref, parts_ref, outs_ref, rows_out, query_out, keyval_out, outs_out, out_ref, *scratch
+):
     scatter = SequenceScatter(rows_ref, rows_out, *scratch[:2], scratch[2:6], CHUNKS)
     weights = WeightScatter(parts_ref, out_ref, scratch[6:10], scratch[10:16])
     outs_sum = scratch[16]
@@ -1261,6 +1309,18 @@
     for k in range(CHUNKS):
         scatter.last(k)
     weights.last()
+    group_width = GROUP * HEAD_SIZE
+    for source in range(PLANE):
+        query_out[:, source * group_width : (source + 1) * group_width] = out_ref[
+            source, :, :group_width
+        ]
+    for kind in range(2):
+        start = group_width + kind * HEAD_SIZE
+        for source in range(0, PLANE, 2):
+            after = (kind * PLANE + source) * HEAD_SIZE
+            keyval_out[:, after : after + 2 * HEAD_SIZE] = jnp.concatenate(
+                [out_ref[source + i, :, start : start + HEAD_SIZE] for i in range(2)], axis=1
+            )
     outs.last(0)
     scatter.finish()
     chip.finish()
@@ -1272,12 +1332,14 @@
         closing_kernel,
         out_shape=(
             jax.ShapeDtypeStruct(rows.shape[1:], jnp.float32),
-            jax.ShapeDtypeStruct((PLANE, *parts.shape[1:]), parts.dtype),
+            jax.ShapeDtypeStruct((parts.shape[1], QUERY_HEADS * HEAD_SIZE), parts.dtype),
+            jax.ShapeDtypeStruct((parts.shape[1], 2 * PLANE * HEAD_SIZE), parts.dtype),
             jax.ShapeDtypeStruct(outs.shape[1:], jnp.float32),
         ),
         in_specs=[VMEM] * 3,
-        out_specs=(VMEM,) * 3,
+        out_specs=(VMEM,) * 4,
         scratch_shapes=[
+            pltpu.VMEM((PLANE, *parts.shape[1:]), parts.dtype),
             *SequenceScatter.scratch(*rows.shape[1:], CHUNKS),
             *WeightScatter.scratch(*parts.shape[1:]),
             pltpu.VMEM((PLANE, *outs.shape[1:]), jnp.bfloat16),
@@ -1623,7 +1685,6 @@
     group = GROUP
     group_width = group * HEAD_SIZE
     ff_part = FF // PLANE
-    ff_own = FF // RANKS
     rows = w_query.shape[0]
 
     gains_low = norm_gains.astype(low)
@@ -1640,12 +1701,6 @@
             small,
         ],
         axis=2,
-    )
-    feed_blocks = (
-        w_gate_up.astype(low)
-        .reshape(rows, 2, 4, PLANE, ff_own)
-        .transpose(3, 0, 1, 2, 4)
-        .reshape(PLANE, rows, 2 * ff_part)
     )
     spots = jnp.broadcast_to(positions[None, :].astype(jnp.float32), (8, own_tokens))
     cosine_own, sine_own = rope_tables(positions, HEAD_SIZE)
@@ -1674,9 +1729,9 @@
         table,
         spots,
         attention_blocks,
-        feed_blocks,
-        w_out.astype(low),
-        w_down.astype(low).reshape(DOWN_PARTS, -1, width),
+        w_gate_up,
+        w_out,
+        w_down,
         out_grad,
     )
     gain_one, gain_two = gain_rows[0], gain_rows[1]
@@ -1695,7 +1750,7 @@
         (normed_two * gain_two).astype(low),
         grads_all,
         feed_all.reshape(width, 2 * ff_part),
-        down_all.reshape(ff_part, width),
+        down_all,
     )
     layer_out = (middle + down_sum).astype(low)
 
@@ -1720,12 +1775,7 @@
         feed_term.reshape(RANKS, rows, 2 * ff_part),
         down_term.reshape(4 * DOWN_PARTS, -1, width),
     )
-    gate_up_grad = (
-        feed_grad.reshape(PLANE, rows, 2, 4, ff_own)
-        .transpose(1, 2, 3, 0, 4)
-        .reshape(rows, 2 * FF)
-        .astype(jnp.float32)
-    )
+    gate_up_grad = feed_grad.astype(jnp.float32)
     down_grad = down_grad.reshape(w_down.shape)
     grad_query = grad_query.transpose(0, 3, 1, 2, 4).reshape(seq_len, group, HEAD_SIZE)
     grad_qkv = jnp.concatenate(
@@ -1738,7 +1788,7 @@
     ).astype(low)
     one_parts = times_transposed(grad_qkv, qkv_weight).astype(low)
     qkv_term = transposed_times(input_one, grad_qkv).astype(low)
-    grad_normed_one, qkv_grad, out_weight_grad = closing(
+    grad_normed_one, query_grad, keyval_grad, out_weight_grad = closing(
         one_parts.reshape(PLANE, own_tokens, width),
         qkv_term.reshape(RANKS, rows, qkv_width),
         out_term.reshape(RANKS, rows, width),
@@ -1746,14 +1796,9 @@
     normed_one, inverse_one = norm_forward(layer_rows)
     grad_norm_one, unused = norm_backward(grad_normed_one, normed_one, inverse_one, gain_one)
     in_grad = grad_middle + grad_norm_one
-    qkv_grad = qkv_grad.astype(jnp.float32)
-    query_grad = qkv_grad[:, :, :group_width].transpose(1, 0, 2).reshape(w_query.shape)
-    keyval_grad = (
-        qkv_grad[:, :, group_width:]
-        .reshape(PLANE, rows, 2, HEAD_SIZE)
-        .transpose(1, 2, 0, 3)
-        .reshape(key_value_weight.shape)
-    )
+    query_grad = query_grad.astype(jnp.float32)
+    keyval_grad = keyval_grad.astype(jnp.float32)
+
     def low_times(weight, grad):
         return jnp.sum(weight.astype(low).astype(jnp.float32) * grad, axis=1)
 

time: 754 us -> 664 us (0.88)
  Pallas kernels: 648 us -> 581 us
  local copies, waits for them, and re-layouts: 35.6 us -> 14 us
    pallas_call x1, Pallas kernels: 249 us -> 205 us  [attention(): pl.pallas_call(attention_kernel, out_shape=(jax.ShapeDtypeStruct((PLANE,...]
    pallas_call x1, Pallas kernels: 211 us -> 186 us  [feed(): pl.pallas_call(feed_kernel, out_shape=(summed, summed, jax.ShapeDtypeStru...]
    convert_element_type x2 -> x0, local copies, waits for them, and re-layouts: 10.9 us -> none  [tensor_parallel(): gate_up_grad = feed_grad.reshape(PLANE, rows, 2, 4, ff_own).transpose(1,...]
where the time goes in v6:
time: 664 us; the launch traced here: 654 us
  Pallas kernels  581 us (88%)
  other arithmetic  34.1 us (5%)
  matrix products  23.6 us (4%)
  local copies, waits for them, and re-layouts  14 us (2%)
    pallas_call x1, Pallas kernels, attention(): pl.pallas_call(attention_kernel, out_shape=(jax.ShapeDtypeStruct((PLANE,...  205 us
    pallas_call x1, Pallas kernels, feed(): pl.pallas_call(feed_kernel, out_shape=(summed, summed, jax.ShapeDtypeStru...  186 us
    pallas_call x1, Pallas kernels, closing(): pl.pallas_call(closing_kernel, out_shape=(jax.ShapeDtypeStruct(rows.shape...  98.4 us
    pallas_call x1, Pallas kernels, attention_back(): pl.pallas_call(attention_back_kernel, out_shape=(jax.ShapeDtypeStruct(que...  91.2 us
    sub x5, other arithmetic, adamw(): weight - rate * (first_hat / (jnp.sqrt(second_hat) + eps_adam) + decay *...  17.2 us

profile of v6, /device:TPU:0, one launch (start us, length us, event | category | flops | bytes accessed | tf_op | source)
XLA Modules:
  0.0 653.7 jit_solution(7110730962406207700)
XLA Ops:
  4.5 1.1 convert_element_type.72
  7.3 205.2 %attention.1 = (bf16[8,128,2048]{2,1,0:T(8,128)(2,1)}, f32[8,128,128]{2,1,0:T(8,128)}, bf16[32,64,512]{2,1,0:T(8,128)(2,1)}, f32[8,2048]{1,0:T(8,128)}, bf16[8,2...) custom-call(s32[1,3]{1,0:T(1,128)} %starts_ref.1, ...), custom_call_target="tpu_custom_call" | custom-call | tf_op jit(solution)/shard_map/attention/pallas_call | solution.py:938
  212.5 1.3 copy.66
  213.8 4.7 multiply_reduce_fusion.2
  220.4 185.9 %feed.1 = (f32[128,2048]{1,0:T(8,128)}, f32[128,2048]{1,0:T(8,128)}, bf16[2048,2048]{1,0:T(8,128)(2,1)}, bf16[1024,2048]{1,0:T(8,128)(2,1)}) custom-call(bf16[128,2048]{1,0:T(8,128)(2,1)} %multiply_convert_fusion.rows_ref, bf16[8,128,2048]{2,1,0:T(8,128)(2,1)} %get-tuple-element.57.grads_all, bf16[2048,2048]{1,0:T(8,128)(2,1)} %bitcast.72, ...), custom_call_target="tpu_custom_call" | custom-call | tf_op jit(solution)/shard_map/feed/pallas_call | solution.py:1155
  406.3 1.5 multiply_reduce_fusion.1
  407.9 2.8 multiply_add_fusion.2
  410.7 5.6 convolution_convert_fusion
  416.3 2.9 convolution_convert_fusion.3
  420.5 91.2 %attention_back.1 = (f32[8,2,2,128,64]{4,3,2,1,0:T(8,128)}, f32[1024,64]{1,0:T(8,128)}, f32[1024,64]{1,0:T(8,128)}, bf16[64,16384]{1,0:T(8,128)(2,1)}, f32[4,64,2048]{2,1,0:T(8,128)}) custom-call(bf16[8,2,2,128,64]{4,3,2,1,0:T(8,128)(2,1)} %get-tuple-element.62.query_ref, bf16[8,128,64]{2,1,0:T(8,128)(2,1)} %get-tuple-element.63.key_ref, ...), custom_call_target="tpu_custom_call" | custom-call | tf_op jit(solution)/shard_map/attention_back/pallas_call | solution.py:1257
  511.7 2.3 copy.69
  514.0 1.1 reshape.166
  515.7 1.4 add_convert_fusion.1
  518.4 1.1 convert.23
  519.6 6.0 convolution_convert_fusion.2
  525.6 4.4 convolution_convert_fusion.1
  530.1 98.4 %closing.1 = (f32[128,2048]{1,0:T(8,128)}, bf16[64,2048]{1,0:T(8,128)(2,1)}, bf16[64,1024]{1,0:T(8,128)(2,1)}, f32[64,2048]{1,0:T(8,128)}) custom-call(bf16[8,128,2048]{2,1,0:T(8,128)(2,1)} %bitcast.76, bf16[32,64,384]{2,1,0:T(8,128)(2,1)} %bitcast.82, bf16[32,64,2048]{2,1,0:T(8,128)(2,1)} %bitcast.68), custom_call_target="tpu_custom_call" | custom-call | tf_op jit(solution)/shard_map/closing/pallas_call | solution.py:1331
  628.6 3.8 multiply_subtract_fusion.2
  632.6 2.9 multiply_subtract_fusion.4
  635.6 6.0 multiply_subtract_fusion
  642.1 1.6 copy-done.1
  644.9 1.4 fusion.8
  647.4 4.0 multiply_subtract_fusion.1
  652.1 1.3 copy.81
  (99 shorter events, 14.6 us)
Async XLA Ops:
  7.3 206.5 %copy-start.2 = (bf16[128,2048]{1,0:T(8,128)(2,1)S(1)}, bf16[128,2048]{1,0:T(8,128)(2,1)}, u32[]{:S(2)}) copy-start(bf16[128,2048]{1,0:T(8,128)(2,1)} %rows_ref.1) | copy-start | bytes 1572868
  220.4 187.4 %copy-start.14 = (bf16[128,2048]{1,0:T(8,128)(2,1)S(1)}, bf16[128,2048]{1,0:T(8,128)(2,1)}, u32[]{:S(2)}) copy-start(bf16[128,2048]{1,0:T(8,128)(2,1)} %grads_ref.1) | copy-start | bytes 1572868
  407.9 8.5 %slice-start = ((s8[8388608]{0:T(1024)(128)(4,1)}), s8[4194304]{0:T(1024)(128)(4,1)S(1)}, s32[]{:S(2)}) async-start(s8[8388608]{0:T(1024)(128)(4,1)} %bitcast.65), calls=%async_computation | async-start | bytes 8388608
  410.7 5.6 slice-start.1
  511.7 3.4 copy-start.12
  519.6 6.0 copy-start.20
  519.6 6.0 copy-start.27
  530.0 98.5 %copy-start.5 = (f32[64,2048]{1,0:T(8,128)S(1)}, f32[64,2048]{1,0:T(8,128)}, u32[]{:S(2)}) copy-start(f32[64,2048]{1,0:T(8,128)} %param.29) | copy-start | bytes 1572868
  530.0 98.5 %copy-start.18 = (f32[64,2048]{1,0:T(8,128)S(1)}, f32[64,2048]{1,0:T(8,128)}, u32[]{:S(2)}) copy-start(f32[64,2048]{1,0:T(8,128)} %out_rows_ref.1) | copy-start | bytes 1572868
  530.0 98.5 %copy-start.21 = (f32[64,2048]{1,0:T(8,128)S(1)}, f32[64,2048]{1,0:T(8,128)}, u32[]{:S(2)}) copy-start(f32[64,2048]{1,0:T(8,128)} %param.37) | copy-start | bytes 1572868
  530.0 98.5 %copy-start.22 = (f32[64,2048]{1,0:T(8,128)S(1)}, f32[64,2048]{1,0:T(8,128)}, u32[]{:S(2)}) copy-start(f32[64,2048]{1,0:T(8,128)} %param.36) | copy-start | bytes 1572868
  530.0 102.5 %copy-start.23 = (f32[64,1024]{1,0:T(8,128)S(1)}, f32[64,1024]{1,0:T(8,128)}, u32[]{:S(2)}) copy-start(f32[64,1024]{1,0:T(8,128)} %param.34) | copy-start | bytes 786436
  530.1 105.5 %copy-start.7 = (f32[64,16384]{1,0:T(8,128)S(1)}, f32[64,16384]{1,0:T(8,128)}, u32[]{:S(2)}) copy-start(f32[64,16384]{1,0:T(8,128)} %param.39) | copy-start | bytes 12582916
  628.5 4.0 copy-start.9
  628.6 7.0 %copy-start = (f32[64,16384]{1,0:T(8,128)S(1)}, f32[64,16384]{1,0:T(8,128)}, u32[]{:S(2)}) copy-start(f32[64,16384]{1,0:T(8,128)} %blocks_ref.1) | copy-start | bytes 12582916
  628.6 7.0 %copy-start.6 = (f32[64,16384]{1,0:T(8,128)S(1)}, f32[64,16384]{1,0:T(8,128)}, u32[]{:S(2)}) copy-start(f32[64,16384]{1,0:T(8,128)} %param.40) | copy-start | bytes 12582916
  628.6 7.0 %copy-start.17 = (bf16[64,16384]{1,0:T(8,128)(2,1)S(1)}, bf16[64,16384]{1,0:T(8,128)(2,1)}, u32[]{:S(2)}) copy-start(bf16[64,16384]{1,0:T(8,128)(2,1)} %get-tuple-element.79) | copy-start | bytes 6291460
  632.4 9.2 %copy-start.16 = (f32[64,2048]{1,0:T(8,128)}, f32[64,2048]{1,0:T(8,128)S(1)}, u32[]{:S(2)}) copy-start(f32[64,2048]{1,0:T(8,128)S(1)} %get-tuple-element.155) | copy-start | bytes 1572868
  635.4 6.2 copy-start.19
  641.6 2.9 copy-start.8
  641.6 4.6 copy-start.10
  641.6 4.6 copy-start.11
  643.7 3.6 copy-start.4
  647.4 4.0 copy-start.15
  (6 other events, 13.9 us)

commit v7 on v6

--- a/solution.py
+++ b/solution.py
@@ -1189,38 +1189,37 @@
     spot_ref,
     start_ref,
     key_spot_ref,
+    table_ref,
+    input_ref,
+    qkv_ref,
     mixed_ref,
     parts_ref,
-    down_ref,
-    query_out,
-    key_out,
-    value_out,
+    rows_out,
+    qkv_out,
     wide_out,
-    down_out,
     *scratch,
 ):
-    mixed_all, out_ref = scratch[:2]
-    scratch = scratch[2:]
+    mixed_all, out_ref, grads, key_grad, value_grad, turned = scratch[:6]
+    scratch = scratch[6:]
     exchange = PlaneExchange(mixed_ref, mixed_all, scratch[:3])
     weights = WeightScatter(parts_ref, out_ref, scratch[3:7], scratch[7:13])
-    down = ChipScatter(down_ref, *scratch[13:16], scratch[16:], DOWN_PARTS)
     d, c, x, core, z, y = place()
     greet(plane_peers(d, c) + chip_peers(d, c, x, core))
     for off in range(1, PLANE + 1):
         exchange.send(off)
     weights.first()
-    for j in range(DOWN_PARTS):
-        down.start(j)
-    key_out[...] = jnp.zeros_like(key_out)
-    value_out[...] = jnp.zeros_like(value_out)
+    key_grad[...] = jnp.zeros_like(key_grad)
+    value_grad[...] = jnp.zeros_like(value_grad)
+    wide = 2 * HEAD_SIZE
     for step in range(PLANE):
         block = lax.rem(c + PLANE - step, PLANE)
         exchange.arrive(step)
 
         @pl.loop(0, PAIRS)
         def _(pair):
-            keys = key_ref[...].reshape(key_out.shape)
-            values = value_ref[...].reshape(value_out.shape)
+            keys = key_ref[...].reshape(key_grad.shape)
+            values = value_ref[...].reshape(value_grad.shape)
+            halves = []
             for half in range(2):
                 query = query_ref[block, pair, half]
                 grad = mixed_all[block, pair][:, half * HEAD_SIZE : (half + 1) * HEAD_SIZE]
@@ -1230,82 +1229,149 @@
                 grad_probs = times_rows(grad, values)
                 delta = jnp.sum(probs * grad_probs, axis=-1, keepdims=True)
                 grad_scores = (probs * (grad_probs - delta) * SCORE_SCALE).astype(jnp.bfloat16)
-                query_out[block, pair, half] = jnp.dot(
-                    grad_scores, keys, preferred_element_type=jnp.float32
+                halves.append(
+                    jnp.dot(grad_scores, keys, preferred_element_type=jnp.float32)
                 )
-                key_out[...] += transposed_times(grad_scores, query)
-                value_out[...] += transposed_times(probs.astype(jnp.bfloat16), grad)
+                key_grad[...] += transposed_times(grad_scores, query)
+                value_grad[...] += transposed_times(probs.astype(jnp.bfloat16), grad)
+            at = pl.ds(pl.multiple_of(pair * wide, wide), wide)
+            grads[block, :, at] = rotate(
+                jnp.concatenate(halves, axis=1), table_ref[block], back=True
+            ).astype(jnp.bfloat16)
 
         weights.relay(step + 1)
         if step >= 2:
             weights.send(step - 1)
-    for off in (PLANE - 1, PLANE):
-        weights.send(off)
-    for j in range(DOWN_PARTS):
-        down.relay(j)
-    for j in range(DOWN_PARTS):
-        down.total(j, down_out.at[j])
+    tokens = grads.shape[1]
+    for block in range(PLANE):
+        span = slice(block * tokens, (block + 1) * tokens)
+        both = jnp.concatenate([key_grad[span], value_grad[span]], axis=1)
+        lane = lax.broadcasted_iota(jnp.int32, both.shape, 1)
+        grads[block, :, PAIRS * wide :] = jnp.where(
+            lane < HEAD_SIZE, rotate(both, table_ref[block], back=True), both
+        ).astype(jnp.bfloat16)
+    weights.send(PLANE - 1)
+    width = input_ref.shape[2]
+    rows = qkv_ref.shape[1]
+    tile = 512
+
+    @pl.loop(0, width // tile)
+    def _(n):
+        weight = qkv_ref[pl.ds(n * (tile // rows), tile // rows), :, :QKV_WIDTH]
+        product = times_rows(
+            grads[...].reshape(PLANE * tokens, QKV_WIDTH), weight.reshape(tile, QKV_WIDTH)
+        )
+        rows_out[:, :, pl.ds(pl.multiple_of(n * tile, tile), tile)] = product.astype(
+            jnp.bfloat16
+        ).reshape(PLANE, tokens, tile)
+
+    weights.send(PLANE)
+
+    @pl.loop(0, width // tile)
+    def _(n):
+        turned[...] = (
+            input_ref[:, :, pl.ds(pl.multiple_of(n * tile, tile), tile)]
+            .reshape(PLANE * tokens, tile)
+            .T
+        )
+        product = jnp.dot(
+            turned[...],
+            grads[...].reshape(PLANE * tokens, QKV_WIDTH),
+            preferred_element_type=jnp.float32,
+        )
+        qkv_out[pl.ds(n * (tile // rows), tile // rows)] = product.astype(
+            jnp.bfloat16
+        ).reshape(tile // rows, rows, QKV_WIDTH)
+
     weights.last()
     for source, start, after in wide_columns(wide_out.shape[1]):
         size = wide_out.shape[1] // (8 * PLANE)
         wide_out[:, after : after + size] = out_ref[source, :, start : start + size]
-    down.finish()
     exchange.finish()
 
 
-def attention_back(query, keys, values, spots, starts, key_spots, mixed, parts, down):
+def attention_back(
+    query, keys, values, spots, starts, key_spots, table, inputs, qkv, mixed, parts
+):
+    low = jnp.bfloat16
+    tokens = inputs.shape[1]
+    sums = pltpu.VMEM((PLANE * tokens, HEAD_SIZE), jnp.float32)
     return pl.pallas_call(
         attention_back_kernel,
         out_shape=(
-            jax.ShapeDtypeStruct(query.shape, jnp.float32),
-            jax.ShapeDtypeStruct((PLANE * keys.shape[1], HEAD_SIZE), jnp.float32),
-            jax.ShapeDtypeStruct((PLANE * values.shape[1], HEAD_SIZE), jnp.float32),
-            jax.ShapeDtypeStruct((parts.shape[1], PLANE * parts.shape[2]), parts.dtype),
-            jax.ShapeDtypeStruct((DOWN_PARTS, *down.shape[1:]), jnp.float32),
+            jax.ShapeDtypeStruct(inputs.shape, low),
+            jax.ShapeDtypeStruct((*qkv.shape[:2], QKV_WIDTH), low),
+            jax.ShapeDtypeStruct((parts.shape[1], PLANE * parts.shape[2]), low),
         ),
-        in_specs=[VMEM] * 9,
-        out_specs=(VMEM,) * 5,
+        in_specs=[VMEM] * 11,
+        out_specs=(VMEM,) * 3,
         scratch_shapes=[
-            pltpu.VMEM(mixed.shape, jnp.bfloat16),
-            pltpu.VMEM((PLANE, *parts.shape[1:]), parts.dtype),
+            pltpu.VMEM(mixed.shape, low),
+            pltpu.VMEM((PLANE, *parts.shape[1:]), low),
+            pltpu.VMEM((PLANE, tokens, QKV_WIDTH), low),
+            sums,
+            sums,
+            pltpu.VMEM((512, PLANE * tokens), low),
             *PlaneExchange.scratch(),
             *WeightScatter.scratch(*parts.shape[1:]),
-            *ChipScatter.scratch(DOWN_PARTS, *down.shape[1:]),
         ],
         compiler_params=params(3),
         name="attention_back",
-    )(query, keys, values, spots, starts, key_spots, mixed, parts, down)
+    )(query, keys, values, spots, starts, key_spots, table, inputs, qkv, mixed, parts)
 
 
 def closing_kernel(
-    rows_ref, parts_ref, outs_ref, rows_out, query_out, keyval_out, outs_out, out_ref, *scratch
+    rows_ref,
+    parts_ref,
+    outs_ref,
+    down_ref,
+    rows_out,
+    query_out,
+    keyval_out,
+    outs_out,
+    down_out,
+    *scratch,
 ):
-    scatter = SequenceScatter(rows_ref, rows_out, *scratch[:2], scratch[2:6], CHUNKS)
-    weights = WeightScatter(parts_ref, out_ref, scratch[6:10], scratch[10:16])
-    outs_sum = scratch[16]
-    chip = ChipScatter(outs_ref, *scratch[17:20], scratch[20:24], PLANE)
-    outs = SequenceScatter(outs_sum, outs_out, *scratch[24:26], scratch[26:], 1)
+    out_ref, outs_sum = scratch[:2]
+    scratch = list(scratch[2:])
+
+    def take(count):
+        taken, scratch[:count] = scratch[:count], []
+        return taken
+
+    scatter = SequenceScatter(rows_ref, rows_out, *take(2), take(4), CHUNKS)
+    weights = WeightScatter(parts_ref, out_ref, take(4), take(6))
+    chip = ChipScatter(outs_ref, *take(3), take(4), PLANE)
+    outs = SequenceScatter(outs_sum, outs_out, *take(2), take(4), 1)
+    down = ChipScatter(down_ref, *take(3), take(4), DOWN_PARTS)
     d, c, x, core, z, y = place()
     greet(plane_peers(d, c) + chip_peers(d, c, x, core))
     places = (*near_first(z)[::-1], z)
     slots = [place * YS + 1 - y for place in places] + [place * YS + y for place in places]
-    for j in slots:
-        chip.start(j)
     weights.first()
     scatter.first()
     for j in slots:
-        chip.relay(j)
+        chip.start(j)
+    for j in range(DOWN_PARTS):
+        down.start(j)
     for off in range(1, PLANE + 1):
         weights.relay(off)
     for k in range(CHUNKS):
         scatter.relay(k)
+        chip.relay(slots[2 * k])
+        chip.relay(slots[2 * k + 1])
+    for j in range(DOWN_PARTS):
+        down.relay(j)
     for off in range(1, PLANE + 1):
         weights.send(off)
     for i, j in enumerate(slots):
         chip.total(j, outs_sum.at[j])
         if i < ZS:
             outs.start(places[i], 0)
-    outs.relay(0)
+        if i >= ZS and i < 2 * ZS - 1:
+            outs.relay_one(places[i - ZS], 0)
+    for j in range(DOWN_PARTS):
+        down.total(j, down_out.at[j])
     for k in range(CHUNKS):
         scatter.last(k)
     weights.last()
@@ -1325,9 +1391,10 @@
     scatter.finish()
     chip.finish()
     outs.finish()
-
-
-def closing(rows, parts, outs):
+    down.finish()
+
+
+def closing(rows, parts, outs, down):
     return pl.pallas_call(
         closing_kernel,
         out_shape=(
@@ -1335,20 +1402,22 @@
             jax.ShapeDtypeStruct((parts.shape[1], QUERY_HEADS * HEAD_SIZE), parts.dtype),
             jax.ShapeDtypeStruct((parts.shape[1], 2 * PLANE * HEAD_SIZE), parts.dtype),
             jax.ShapeDtypeStruct(outs.shape[1:], jnp.float32),
+            jax.ShapeDtypeStruct((DOWN_PARTS, *down.shape[1:]), jnp.float32),
         ),
-        in_specs=[VMEM] * 3,
-        out_specs=(VMEM,) * 4,
+        in_specs=[VMEM] * 4,
+        out_specs=(VMEM,) * 5,
         scratch_shapes=[
             pltpu.VMEM((PLANE, *parts.shape[1:]), parts.dtype),
+            pltpu.VMEM((PLANE, *outs.shape[1:]), jnp.bfloat16),
             *SequenceScatter.scratch(*rows.shape[1:], CHUNKS),
             *WeightScatter.scratch(*parts.shape[1:]),
-            pltpu.VMEM((PLANE, *outs.shape[1:]), jnp.bfloat16),
             *ChipScatter.scratch(PLANE, *outs.shape[1:]),
             *SequenceScatter.scratch(*outs.shape[1:], 1),
+            *ChipScatter.scratch(DOWN_PARTS, *down.shape[1:]),
         ],
         compiler_params=params(4),
         name="closing",
-    )(rows, parts, outs)
+    )(rows, parts, outs, down)
 
 
 def body(
@@ -1706,7 +1775,6 @@
     cosine_own, sine_own = rope_tables(positions, HEAD_SIZE)
     cosine_own, sine_own = cosine_own[:, 0], sine_own[:, 0]
     table = jnp.concatenate([cosine_own, cosine_own, -sine_own, sine_own], axis=1)
-    qkv_width = QKV_WIDTH
     (
         input_one_all,
         table_all,
@@ -1735,10 +1803,6 @@
         out_grad,
     )
     gain_one, gain_two = gain_rows[0], gain_rows[1]
-    input_one = input_one_all.reshape(seq_len, width)
-    qkv_weight = attention_all.reshape(width, -1)[:, :qkv_width]
-    cosine_table = table_all[:, :, : HEAD_SIZE // 2].reshape(seq_len, 1, -1)
-    sine_table = table_all[:, :, 3 * HEAD_SIZE // 2 :].reshape(seq_len, 1, -1)
     mixed = mixed_parts.transpose(2, 0, 1, 3).reshape(own_tokens, width)
     out_weight = out_all.reshape(width, width)
     branch = jnp.dot(mixed, out_weight, preferred_element_type=jnp.float32)
@@ -1764,35 +1828,27 @@
         .reshape(own_tokens, PLANE, PAIRS, 2 * HEAD_SIZE)
         .transpose(1, 2, 0, 3)
     )
-    grad_query, grad_key, grad_value, feed_grad, down_grad = attention_back(
+    one_parts, qkv_term, feed_grad = attention_back(
         query_rows,
         key_rows,
         value_rows,
         token_spots,
         token_starts,
         key_spots,
+        table_all,
+        input_one_all,
+        attention_all,
         grad_mixed,
         feed_term.reshape(RANKS, rows, 2 * ff_part),
+    )
+    gate_up_grad = feed_grad.astype(jnp.float32)
+    grad_normed_one, query_grad, keyval_grad, out_weight_grad, down_grad = closing(
+        one_parts,
+        qkv_term,
+        out_term.reshape(RANKS, rows, width),
         down_term.reshape(4 * DOWN_PARTS, -1, width),
     )
-    gate_up_grad = feed_grad.astype(jnp.float32)
     down_grad = down_grad.reshape(w_down.shape)
-    grad_query = grad_query.transpose(0, 3, 1, 2, 4).reshape(seq_len, group, HEAD_SIZE)
-    grad_qkv = jnp.concatenate(
-        [
-            reverse_rotation(grad_query, cosine_table, sine_table).reshape(seq_len, group_width),
-            reverse_rotation(grad_key[:, None], cosine_table, sine_table)[:, 0],
-            grad_value,
-        ],
-        axis=1,
-    ).astype(low)
-    one_parts = times_transposed(grad_qkv, qkv_weight).astype(low)
-    qkv_term = transposed_times(input_one, grad_qkv).astype(low)
-    grad_normed_one, query_grad, keyval_grad, out_weight_grad = closing(
-        one_parts.reshape(PLANE, own_tokens, width),
-        qkv_term.reshape(RANKS, rows, qkv_width),
-        out_term.reshape(RANKS, rows, width),
-    )
     normed_one, inverse_one = norm_forward(layer_rows)
     grad_norm_one, unused = norm_backward(grad_normed_one, normed_one, inverse_one, gain_one)
     in_grad = grad_middle + grad_norm_one

time: 664 us -> 632 us (0.952)
  Pallas kernels: 581 us -> 567 us
  matrix products: 23.6 us -> 13.2 us
    pallas_call x1, Pallas kernels: 91.2 us -> 76.7 us  [attention_back(): pl.pallas_call(attention_back_kernel, out_shape=(jax.ShapeDtypeStruct(inp...]
where the time goes in v7:
time: 632 us; the launch traced here: 623 us
  Pallas kernels  567 us (90%)
  other arithmetic  30.2 us (5%)
  matrix products  13.2 us (2%)
  local copies, waits for them, and re-layouts  10.9 us (2%)
    pallas_call x1, Pallas kernels, attention(): pl.pallas_call(attention_kernel, out_shape=(jax.ShapeDtypeStruct((PLANE,...  205 us
    pallas_call x1, Pallas kernels, feed(): pl.pallas_call(feed_kernel, out_shape=(summed, summed, jax.ShapeDtypeStru...  186 us
    pallas_call x1, Pallas kernels, closing(): pl.pallas_call(closing_kernel, out_shape=(jax.ShapeDtypeStruct(rows.shape...  99 us
    pallas_call x1, Pallas kernels, attention_back(): pl.pallas_call(attention_back_kernel, out_shape=(jax.ShapeDtypeStruct(inp...  76.7 us
    sub x5, other arithmetic, adamw(): weight - rate * (first_hat / (jnp.sqrt(second_hat) + eps_adam) + decay *...  17 us

profile of v7, /device:TPU:0, one launch (start us, length us, event | category | flops | bytes accessed | tf_op | source)
XLA Modules:
  0.0 622.5 jit_solution(14367907125976011001)
XLA Ops:
  3.0 1.0 convert_element_type.66
  4.5 1.1 convert_element_type.65
  6.5 0.8 pad_maximum_fusion.qkv_ref
  7.3 205.1 %attention.1 = (bf16[8,128,2048]{2,1,0:T(8,128)(2,1)}, f32[8,128,128]{2,1,0:T(8,128)}, bf16[32,64,512]{2,1,0:T(8,128)(2,1)}, f32[8,2048]{1,0:T(8,128)}, bf16[8,2...) custom-call(s32[1,3]{1,0:T(1,128)} %starts_ref.1, ...), custom_call_target="tpu_custom_call" | custom-call | tf_op jit(solution)/shard_map/attention/pallas_call | solution.py:938
  212.4 1.3 copy.61
  213.8 4.7 multiply_reduce_fusion.2
  218.5 0.9 fusion.22
  219.5 0.9 multiply_convert_fusion.rows_ref
  220.4 185.9 %feed.1 = (f32[128,2048]{1,0:T(8,128)}, f32[128,2048]{1,0:T(8,128)}, bf16[2048,2048]{1,0:T(8,128)(2,1)}, bf16[1024,2048]{1,0:T(8,128)(2,1)}) custom-call(bf16[128,2048]{1,0:T(8,128)(2,1)} %multiply_convert_fusion.rows_ref, bf16[8,128,2048]{2,1,0:T(8,128)(2,1)} %get-tuple-element.56.grads_all, bf16[2048,2048]{1,0:T(8,128)(2,1)} %bitcast.39, ...), custom_call_target="tpu_custom_call" | custom-call | tf_op jit(solution)/shard_map/feed/pallas_call | solution.py:1155
  406.3 1.5 multiply_reduce_fusion.1
  407.8 2.8 multiply_add_fusion.2
  410.7 5.6 convolution_convert_fusion
  416.2 2.9 convolution_convert_fusion.1
  419.4 1.0 copy.63
  420.4 76.7 %attention_back.1 = (bf16[8,128,2048]{2,1,0:T(8,128)(2,1)}, bf16[32,64,384]{2,1,0:T(8,128)(2,1)}, bf16[64,16384]{1,0:T(8,128)(2,1)}) custom-call(bf16[8,2,2,128,64]{4,3,2,1,0:T(8,128)(2,1)} %get-tuple-element.61.query_ref, bf16[8,128,64]{2,1,0:T(8,128)(2,1)} %get-tuple-element.62.key_ref, bf16[8,128,64]{2,1,0:T(8,128)(2,1)} %get-tuple-element.63.value_ref, ...), custom_call_target="tpu_custom_call" | custom-call | tf_op jit(solution)/shard_map/attention_back/pallas_call | solution.py:1299
  497.2 99.0 %closing.1 = (f32[128,2048]{1,0:T(8,128)}, bf16[64,2048]{1,0:T(8,128)(2,1)}, bf16[64,1024]{1,0:T(8,128)(2,1)}, f32[64,2048]{1,0:T(8,128)}, f32[4,64,2048]{2,1,0:T(8,128)}) custom-call(bf16[8,128,2048]{2,1,0:T(8,128)(2,1)} %get-tuple-element.71.rows_ref, bf16[32,64,384]{2,1,0:T(8,128)(2,1)} %get-tuple-element.72.parts_ref, bf16[32,64,2048]{2,1,0:T(8,128)(2,1)} %bitcast.34, ...), custom_call_target="tpu_custom_call" | custom-call | tf_op jit(solution)/shard_map/closing/pallas_call | solution.py:1398
  596.3 3.8 multiply_subtract_fusion.2
  600.2 2.9 multiply_subtract_fusion.4
  603.3 5.8 multiply_subtract_fusion
  609.6 1.6 copy-done.1
  614.1 4.0 multiply_subtract_fusion.1
  618.6 1.3 fusion.7
  620.0 0.8 copy.70
  620.8 1.3 copy.71
  (77 shorter events, 8.2 us)
Async XLA Ops:
  7.3 206.5 %copy-start.2 = (bf16[128,2048]{1,0:T(8,128)(2,1)S(1)}, bf16[128,2048]{1,0:T(8,128)(2,1)}, u32[]{:S(2)}) copy-start(bf16[128,2048]{1,0:T(8,128)(2,1)} %rows_ref.1) | copy-start | bytes 1572868
  220.4 187.4 %copy-start.12 = (bf16[128,2048]{1,0:T(8,128)(2,1)S(1)}, bf16[128,2048]{1,0:T(8,128)(2,1)}, u32[]{:S(2)}) copy-start(bf16[128,2048]{1,0:T(8,128)(2,1)} %grads_ref.1) | copy-start | bytes 1572868
  407.8 8.4 %slice-start = ((s8[8388608]{0:T(1024)(128)(4,1)}), s8[4194304]{0:T(1024)(128)(4,1)S(1)}, s32[]{:S(2)}) async-start(s8[8388608]{0:T(1024)(128)(4,1)} %bitcast.31), calls=%async_computation | async-start | bytes 8388608
  410.7 5.6 slice-start.1
  497.2 99.0 %copy-start.5 = (f32[64,2048]{1,0:T(8,128)S(1)}, f32[64,2048]{1,0:T(8,128)}, u32[]{:S(2)}) copy-start(f32[64,2048]{1,0:T(8,128)} %param.29) | copy-start | bytes 1572868
  497.2 99.0 %copy-start.16 = (f32[64,2048]{1,0:T(8,128)S(1)}, f32[64,2048]{1,0:T(8,128)}, u32[]{:S(2)}) copy-start(f32[64,2048]{1,0:T(8,128)} %out_rows_ref.1) | copy-start | bytes 1572868
  497.2 99.0 %copy-start.18 = (f32[64,2048]{1,0:T(8,128)S(1)}, f32[64,2048]{1,0:T(8,128)}, u32[]{:S(2)}) copy-start(f32[64,2048]{1,0:T(8,128)} %param.37) | copy-start | bytes 1572868
  497.2 99.0 %copy-start.19 = (f32[64,2048]{1,0:T(8,128)S(1)}, f32[64,2048]{1,0:T(8,128)}, u32[]{:S(2)}) copy-start(f32[64,2048]{1,0:T(8,128)} %param.36) | copy-start | bytes 1572868
  497.2 103.0 %copy-start.20 = (f32[64,1024]{1,0:T(8,128)S(1)}, f32[64,1024]{1,0:T(8,128)}, u32[]{:S(2)}) copy-start(f32[64,1024]{1,0:T(8,128)} %param.34) | copy-start | bytes 786436
  497.2 106.0 %copy-start.7 = (f32[64,16384]{1,0:T(8,128)S(1)}, f32[64,16384]{1,0:T(8,128)}, u32[]{:S(2)}) copy-start(f32[64,16384]{1,0:T(8,128)} %param.39) | copy-start | bytes 12582916
  596.2 4.0 copy-start.9
  596.2 7.0 %copy-start = (f32[64,16384]{1,0:T(8,128)S(1)}, f32[64,16384]{1,0:T(8,128)}, u32[]{:S(2)}) copy-start(f32[64,16384]{1,0:T(8,128)} %blocks_ref.1) | copy-start | bytes 12582916
  596.3 7.0 %copy-start.6 = (f32[64,16384]{1,0:T(8,128)S(1)}, f32[64,16384]{1,0:T(8,128)}, u32[]{:S(2)}) copy-start(f32[64,16384]{1,0:T(8,128)} %param.40) | copy-start | bytes 12582916
  596.3 7.0 %copy-start.15 = (bf16[64,16384]{1,0:T(8,128)(2,1)S(1)}, bf16[64,16384]{1,0:T(8,128)(2,1)}, u32[]{:S(2)}) copy-start(bf16[64,16384]{1,0:T(8,128)(2,1)} %get-tuple-element.77) | copy-start | bytes 6291460
  600.1 9.0 %copy-start.14 = (f32[64,2048]{1,0:T(8,128)}, f32[64,2048]{1,0:T(8,128)S(1)}, u32[]{:S(2)}) copy-start(f32[64,2048]{1,0:T(8,128)S(1)} %get-tuple-element.147) | copy-start | bytes 1572868
  603.1 6.0 copy-start.17
  603.3 8.0 %copy-start.23 = (f32[2,64]{1,0:T(2,128)S(1)}, f32[2,64]{1,0:T(2,128)}, u32[]{:S(2)}) copy-start(f32[2,64]{1,0:T(2,128)} %param.27) | copy-start | bytes 1540
  609.1 2.1 copy-start.1
  609.1 2.1 copy-start.21
  609.1 3.1 copy-start.3
  609.1 3.7 copy-start.4
  609.2 4.4 copy-start.10
  609.2 5.0 copy-start.11
  614.1 4.2 copy-start.8
  (2 other events, 4.0 us)

commit v8 on v7

--- a/solution.py
+++ b/solution.py
@@ -162,6 +162,10 @@
     return [half * 4 + 1 - z, 2 - half, 3 - 3 * half]
 
 
+def is_inner(z):
+    return (z == 1) | (z == 2)
+
+
 class SequenceGather:
     def __init__(self, own, out, sems, chunks):
         self.own, self.out, self.chunks = own, out, chunks
@@ -211,18 +215,30 @@
     def first(self, by_block=False):
         self.local = pltpu.make_async_copy(self.own, self.out.at[self.c], self.local_sem)
         self.local.start()
-        near = near_first(self.z)
+        near, mid, _ = near_first(self.z)
         if by_block:
             for k in range(self.chunks):
                 self.start(self.across(self.z, k, self.part(self.own, k)))
-            for to in near:
+            for to in (mid, near):
                 for k in range(self.chunks):
                     self.start(self.along(to, k))
             return
         for k in range(self.chunks):
-            for to in near[::-1]:
+            for to in (mid, near):
                 self.start(self.along(to, k))
             self.start(self.across(self.z, k, self.part(self.own, k)))
+
+    def inward(self, i, source, k):
+        near, _, far = near_first(self.z)
+        block = self.part(self.out.at[source * YS + self.y], k)
+        return remote(
+            block,
+            block,
+            self.zs.at[(far, self.z)[i], k],
+            self.zr.at[source, k],
+            self.d,
+            near * YS + self.y,
+        )
 
     def relay_one(self, source, k):
         slot = source * YS + self.y
@@ -232,9 +248,22 @@
         ).wait_recv()
         self.start(self.across(source, k, block))
 
+    def relay_half(self):
+        for k in range(self.chunks):
+            self.relay_far(k)
+
+    def relay_far(self, k):
+        _, mid, far = near_first(self.z)
+        for i, source in enumerate((mid, far)):
+            self.relay_one(source, k)
+
+            @pl.when(is_inner(self.z))
+            def _(i=i, source=source):
+                self.inward(i, source, k).start()
+
     def relay(self, k):
-        for source in near_first(self.z):
-            self.relay_one(source, k)
+        self.relay_one(near_first(self.z)[0], k)
+        self.relay_far(k)
 
     def relay_block(self, source):
         for k in range(self.chunks):
@@ -255,6 +284,13 @@
     def finish(self):
         for copy in self.sent:
             copy.wait_send()
+        _, mid, far = near_first(self.z)
+
+        @pl.when(is_inner(self.z))
+        def _():
+            for k in range(self.chunks):
+                for i, source in enumerate((mid, far)):
+                    self.inward(i, source, k).wait_send()
 
     def last(self):
         for z in range(ZS):
@@ -296,14 +332,24 @@
             self.z * YS + 1 - self.y,
         )
 
-    def along(self, to, k):
+    def along(self, to, k, slot):
         return remote(
             self.ybuf.at[to, self.span(k)],
-            self.zbuf.at[self.z, self.span(k)],
+            self.zbuf.at[slot, self.span(k)],
             self.zs.at[to, k],
-            self.zr.at[self.z, k],
+            self.zr.at[slot, k],
             self.d,
             to * YS + self.y,
+        )
+
+    def inward(self, i, to, k):
+        return remote(
+            self.ybuf.at[to, self.span(k)],
+            self.zbuf.at[2 + i, self.span(k)],
+            self.zs.at[to, k],
+            self.zr.at[2 + i, k],
+            self.d,
+            near_first(self.z)[0] * YS + self.y,
         )
 
     def start(self, z, k):
@@ -316,37 +362,56 @@
             for z in (*near_first(self.z)[::-1], self.z):
                 self.start(z, k)
 
-    def relay_one(self, z, k):
+    def added(self, z, k):
         self.across(z, k).wait_recv()
         block = self.ybuf.at[z, self.span(k)]
         add_into(block, [self.parts.at[z * YS + self.y, self.span(k)], block], self.rows)
-        copy = self.along(z, k)
+
+    def relay_near(self, k):
+        near = near_first(self.z)[0]
+        self.added(near, k)
+        copy = self.along(near, k, 0)
         copy.start()
         self.sent.append(copy)
 
+    def relay_far(self, k):
+        _, mid, far = near_first(self.z)
+        for to in (far, mid):
+            self.added(to, k)
+
+            @pl.when(jnp.logical_not(is_inner(self.z)))
+            def _(to=to, i=0 if to is mid else 1):
+                self.inward(i, to, k).start()
+
+        @pl.when(is_inner(self.z))
+        def _():
+            for i, to in ((1, far), (0, mid)):
+                self.inward(i, to, k).wait_recv()
+                block = self.ybuf.at[to, self.span(k)]
+                add_into(block, [block, self.zbuf.at[2 + i, self.span(k)]], self.rows)
+                self.along(to, k, 1).start()
+
     def relay(self, k):
-        for z in near_first(self.z)[::-1]:
-            self.relay_one(z, k)
+        self.relay_far(k)
+        self.relay_near(k)
 
     def last(self, k):
         self.across(self.z, k).wait_recv()
         blocks = [self.parts.at[self.c, self.span(k)], self.ybuf.at[self.z, self.span(k)]]
-        for source in near_first(self.z):
-            block = self.zbuf.at[source, self.span(k)]
-            remote(
-                block,
-                block,
-                self.zs.at[source, k],
-                self.zr.at[source, k],
-                self.d,
-                source * YS + self.y,
-            ).wait_recv()
+        near, mid, _ = near_first(self.z)
+        for slot, source in enumerate((near, mid)):
+            block = self.zbuf.at[slot, self.span(k)]
+            self.along(source, k, slot).wait_recv()
             blocks.append(block)
         add_into(self.out.at[self.span(k)], blocks, self.rows)
 
     def finish(self):
         for copy in self.sent:
             copy.wait_send()
+        _, mid, far = near_first(self.z)
+        for k in range(self.chunks):
+            for to in (mid, far):
+                self.along(to, k, 1).wait_send()
 
 
 class ChipGather:
@@ -803,8 +868,7 @@
     table.relay(0)
     rows.relay_block(order[0])
     qkv.relay_chip()
-    rows.relay_block(order[1])
-    rows.relay_block(order[2])
+    rows.relay_half()
     weights.first()
     for off in range(1, PLANE):
         source = lax.rem(c + off, PLANE)
@@ -1109,8 +1173,7 @@
     rows.arrive_across(z)
     rows.arrive_across(near)
     forward(half)
-    rows.relay_block(mid)
-    rows.relay_block(far)
+    rows.relay_half()
     backward(half)
     inward(half)
     normed.start(near, 0)
@@ -1122,20 +1185,19 @@
     inward(1 - half)
     normed.start(far, 0)
     normed.start(mid, 0)
-    normed.relay_one(near, 0)
+    normed.relay_near(0)
     downward(1 - half)
     total.start(far, 0)
     total.start(mid, 0)
-    normed.relay_one(far, 0)
+    normed.relay_far(0)
     downward(half)
     total.start(near, 0)
     total.start(z, 0)
-    normed.relay_one(mid, 0)
     for i in range(2):
         weight_grad(i)
-    for pair in (far, mid, near):
-        total.relay_one(pair, 0)
-        weight_grad(len(copies))
+    total.relay_far(0)
+    weight_grad(len(copies))
+    total.relay_near(0)
     for i in range(len(copies), len(tiles)):
         weight_grad(i)
     normed.last(0)
@@ -1368,8 +1430,10 @@
         chip.total(j, outs_sum.at[j])
         if i < ZS:
             outs.start(places[i], 0)
-        if i >= ZS and i < 2 * ZS - 1:
-            outs.relay_one(places[i - ZS], 0)
+        if i == ZS + 1:
+            outs.relay_far(0)
+        if i == ZS + 2:
+            outs.relay_near(0)
     for j in range(DOWN_PARTS):
         down.total(j, down_out.at[j])
     for k in range(CHUNKS):

time: 632 us -> 618 us (0.978)
  Pallas kernels: 567 us -> 553 us
    pallas_call x1, Pallas kernels: 186 us -> 178 us  [feed(): pl.pallas_call(feed_kernel, out_shape=(summed, summed, jax.ShapeDtypeStru...]
where the time goes in v8:
time: 618 us; the launch traced here: 609 us
  Pallas kernels  553 us (89%)
  other arithmetic  30.2 us (5%)
  matrix products  13.2 us (2%)
  local copies, waits for them, and re-layouts  10.9 us (2%)
    pallas_call x1, Pallas kernels, attention(): pl.pallas_call(attention_kernel, out_shape=(jax.ShapeDtypeStruct((PLANE,...  207 us
    pallas_call x1, Pallas kernels, feed(): pl.pallas_call(feed_kernel, out_shape=(summed, summed, jax.ShapeDtypeStru...  178 us
    pallas_call x1, Pallas kernels, closing(): pl.pallas_call(closing_kernel, out_shape=(jax.ShapeDtypeStruct(rows.shape...  97.1 us
    pallas_call x1, Pallas kernels, attention_back(): pl.pallas_call(attention_back_kernel, out_shape=(jax.ShapeDtypeStruct(inp...  71.4 us
    sub x5, other arithmetic, adamw(): weight - rate * (first_hat / (jnp.sqrt(second_hat) + eps_adam) + decay *...  17 us

profile of v8, /device:TPU:0, one launch (start us, length us, event | category | flops | bytes accessed | tf_op | source)
XLA Modules:
  0.0 608.7 jit_solution(9983006085166034765)
XLA Ops:
  3.0 1.0 convert_element_type.66
  4.5 1.1 convert_element_type.65
  6.5 0.8 pad_maximum_fusion.qkv_ref
  7.3 206.7 %attention.1 = (bf16[8,128,2048]{2,1,0:T(8,128)(2,1)}, f32[8,128,128]{2,1,0:T(8,128)}, bf16[32,64,512]{2,1,0:T(8,128)(2,1)}, f32[8,2048]{1,0:T(8,128)}, bf16[8,2...) custom-call(s32[1,3]{1,0:T(1,128)} %starts_ref.1, ...), custom_call_target="tpu_custom_call" | custom-call | tf_op jit(solution)/shard_map/attention/pallas_call | solution.py:1002
  214.0 1.3 copy.61
  215.3 4.7 multiply_reduce_fusion.2
  220.1 0.9 fusion.22
  221.0 0.9 multiply_convert_fusion.rows_ref
  222.0 177.7 %feed.1 = (f32[128,2048]{1,0:T(8,128)}, f32[128,2048]{1,0:T(8,128)}, bf16[2048,2048]{1,0:T(8,128)(2,1)}, bf16[1024,2048]{1,0:T(8,128)(2,1)}) custom-call(bf16[128,2048]{1,0:T(8,128)(2,1)} %multiply_convert_fusion.rows_ref, bf16[8,128,2048]{2,1,0:T(8,128)(2,1)} %get-tuple-element.56.grads_all, bf16[2048,2048]{1,0:T(8,128)(2,1)} %bitcast.39, ...), custom_call_target="tpu_custom_call" | custom-call | tf_op jit(solution)/shard_map/feed/pallas_call | solution.py:1217
  399.6 1.5 multiply_reduce_fusion.1
  401.2 2.8 multiply_add_fusion.2
  404.0 5.6 convolution_convert_fusion
  409.6 2.9 convolution_convert_fusion.1
  412.8 1.0 copy.63
  413.8 71.4 %attention_back.1 = (bf16[8,128,2048]{2,1,0:T(8,128)(2,1)}, bf16[32,64,384]{2,1,0:T(8,128)(2,1)}, bf16[64,16384]{1,0:T(8,128)(2,1)}) custom-call(bf16[8,2,2,128,64]{4,3,2,1,0:T(8,128)(2,1)} %get-tuple-element.61.query_ref, bf16[8,128,64]{2,1,0:T(8,128)(2,1)} %get-tuple-element.62.key_ref, bf16[8,128,64]{2,1,0:T(8,128)(2,1)} %get-tuple-element.63.value_ref, ...), custom_call_target="tpu_custom_call" | custom-call | tf_op jit(solution)/shard_map/attention_back/pallas_call | solution.py:1361
  485.2 97.1 %closing.1 = (f32[128,2048]{1,0:T(8,128)}, bf16[64,2048]{1,0:T(8,128)(2,1)}, bf16[64,1024]{1,0:T(8,128)(2,1)}, f32[64,2048]{1,0:T(8,128)}, f32[4,64,2048]{2,1,0:T(8,128)}) custom-call(bf16[8,128,2048]{2,1,0:T(8,128)(2,1)} %get-tuple-element.71.rows_ref, bf16[32,64,384]{2,1,0:T(8,128)(2,1)} %get-tuple-element.72.parts_ref, bf16[32,64,2048]{2,1,0:T(8,128)(2,1)} %bitcast.34, ...), custom_call_target="tpu_custom_call" | custom-call | tf_op jit(solution)/shard_map/closing/pallas_call | solution.py:1462
  582.4 3.8 multiply_subtract_fusion.2
  586.4 2.9 multiply_subtract_fusion.4
  589.4 5.8 multiply_subtract_fusion
  595.8 1.6 copy-done.1
  600.3 4.0 multiply_subtract_fusion.1
  604.8 1.3 fusion.7
  606.1 0.8 copy.70
  606.9 1.3 copy.71
  (77 shorter events, 8.2 us)
Async XLA Ops:
  7.3 208.0 %copy-start.2 = (bf16[128,2048]{1,0:T(8,128)(2,1)S(1)}, bf16[128,2048]{1,0:T(8,128)(2,1)}, u32[]{:S(2)}) copy-start(bf16[128,2048]{1,0:T(8,128)(2,1)} %rows_ref.1) | copy-start | bytes 1572868
  222.0 179.2 %copy-start.12 = (bf16[128,2048]{1,0:T(8,128)(2,1)S(1)}, bf16[128,2048]{1,0:T(8,128)(2,1)}, u32[]{:S(2)}) copy-start(bf16[128,2048]{1,0:T(8,128)(2,1)} %grads_ref.1) | copy-start | bytes 1572868
  401.1 8.4 %slice-start = ((s8[8388608]{0:T(1024)(128)(4,1)}), s8[4194304]{0:T(1024)(128)(4,1)S(1)}, s32[]{:S(2)}) async-start(s8[8388608]{0:T(1024)(128)(4,1)} %bitcast.31), calls=%async_computation | async-start | bytes 8388608
  404.0 5.6 slice-start.1
  485.1 97.2 %copy-start.5 = (f32[64,2048]{1,0:T(8,128)S(1)}, f32[64,2048]{1,0:T(8,128)}, u32[]{:S(2)}) copy-start(f32[64,2048]{1,0:T(8,128)} %param.29) | copy-start | bytes 1572868
  485.2 97.2 %copy-start.16 = (f32[64,2048]{1,0:T(8,128)S(1)}, f32[64,2048]{1,0:T(8,128)}, u32[]{:S(2)}) copy-start(f32[64,2048]{1,0:T(8,128)} %out_rows_ref.1) | copy-start | bytes 1572868
  485.2 97.2 %copy-start.18 = (f32[64,2048]{1,0:T(8,128)S(1)}, f32[64,2048]{1,0:T(8,128)}, u32[]{:S(2)}) copy-start(f32[64,2048]{1,0:T(8,128)} %param.37) | copy-start | bytes 1572868
  485.2 97.2 %copy-start.19 = (f32[64,2048]{1,0:T(8,128)S(1)}, f32[64,2048]{1,0:T(8,128)}, u32[]{:S(2)}) copy-start(f32[64,2048]{1,0:T(8,128)} %param.36) | copy-start | bytes 1572868
  485.2 101.2 %copy-start.20 = (f32[64,1024]{1,0:T(8,128)S(1)}, f32[64,1024]{1,0:T(8,128)}, u32[]{:S(2)}) copy-start(f32[64,1024]{1,0:T(8,128)} %param.34) | copy-start | bytes 786436
  485.2 104.2 %copy-start.7 = (f32[64,16384]{1,0:T(8,128)S(1)}, f32[64,16384]{1,0:T(8,128)}, u32[]{:S(2)}) copy-start(f32[64,16384]{1,0:T(8,128)} %param.39) | copy-start | bytes 12582916
  582.4 4.0 copy-start.9
  582.4 7.0 %copy-start = (f32[64,16384]{1,0:T(8,128)S(1)}, f32[64,16384]{1,0:T(8,128)}, u32[]{:S(2)}) copy-start(f32[64,16384]{1,0:T(8,128)} %blocks_ref.1) | copy-start | bytes 12582916
  582.4 7.0 %copy-start.6 = (f32[64,16384]{1,0:T(8,128)S(1)}, f32[64,16384]{1,0:T(8,128)}, u32[]{:S(2)}) copy-start(f32[64,16384]{1,0:T(8,128)} %param.40) | copy-start | bytes 12582916
  582.4 7.0 %copy-start.15 = (bf16[64,16384]{1,0:T(8,128)(2,1)S(1)}, bf16[64,16384]{1,0:T(8,128)(2,1)}, u32[]{:S(2)}) copy-start(bf16[64,16384]{1,0:T(8,128)(2,1)} %get-tuple-element.77) | copy-start | bytes 6291460
  586.2 9.0 %copy-start.14 = (f32[64,2048]{1,0:T(8,128)}, f32[64,2048]{1,0:T(8,128)S(1)}, u32[]{:S(2)}) copy-start(f32[64,2048]{1,0:T(8,128)S(1)} %get-tuple-element.147) | copy-start | bytes 1572868
  589.2 6.0 copy-start.17
  589.4 8.0 %copy-start.23 = (f32[2,64]{1,0:T(2,128)S(1)}, f32[2,64]{1,0:T(2,128)}, u32[]{:S(2)}) copy-start(f32[2,64]{1,0:T(2,128)} %param.27) | copy-start | bytes 1540
  595.3 2.1 copy-start.1
  595.3 2.1 copy-start.21
  595.3 3.1 copy-start.3
  595.3 3.7 copy-start.4
  595.3 4.4 copy-start.10
  595.3 5.0 copy-start.11
  600.3 4.2 copy-start.8
  (2 other events, 4.0 us)

commit v9 on v8

--- a/solution.py
+++ b/solution.py
@@ -945,6 +945,8 @@
         outs.arrive_across(other)
         outs_chip.start(other * YS + 1 - y)
     grads.first()
+    out_order = [c, *(source * YS + y for source in order)]
+    out_order += [other * YS + 1 - y for other in range(ZS)]
 
     for step in range(1, PLANE + 1):
         block = lax.rem(c + step, PLANE)
@@ -972,13 +974,16 @@
         exchange.send(step)
         if step < PLANE:
             weights.relay(step)
+        if step == 2:
+            for j in range(DOWN_PARTS):
+                down.relay(j)
+        if 3 <= step < 7:
+            for j in out_order[2 * (step - 3) : 2 * (step - 2)]:
+                outs_chip.relay(j)
     for k in range(CHUNKS):
+        for off in (2 * k, 2 * k + 1):
+            weights.chip.relay(lax.rem(c + PLANE - off, PLANE))
         grads.relay(k)
-    for j in range(DOWN_PARTS):
-        down.relay(j)
-    for off in range(PLANE):
-        outs_chip.relay(lax.rem(c + off, PLANE))
-    weights.relay_chip()
     for off in range(1, PLANE + 1):
         exchange.arrive(off)
     grads.last()

time: 618 us -> 615 us (level)
    pallas_call x1, Pallas kernels: 178 us -> 170 us  [feed(): pl.pallas_call(feed_kernel, out_shape=(summed, summed, jax.ShapeDtypeStru...]
where the time goes in v9:
time: 615 us; the launch traced here: 606 us
  Pallas kernels  550 us (89%)
  other arithmetic  30.2 us (5%)
  matrix products  13.2 us (2%)
  local copies, waits for them, and re-layouts  10.9 us (2%)
    pallas_call x1, Pallas kernels, attention(): pl.pallas_call(attention_kernel, out_shape=(jax.ShapeDtypeStruct((PLANE,...  211 us
    pallas_call x1, Pallas kernels, feed(): pl.pallas_call(feed_kernel, out_shape=(summed, summed, jax.ShapeDtypeStru...  170 us
    pallas_call x1, Pallas kernels, closing(): pl.pallas_call(closing_kernel, out_shape=(jax.ShapeDtypeStruct(rows.shape...  97.4 us
    pallas_call x1, Pallas kernels, attention_back(): pl.pallas_call(attention_back_kernel, out_shape=(jax.ShapeDtypeStruct(inp...  72 us
    sub x5, other arithmetic, adamw(): weight - rate * (first_hat / (jnp.sqrt(second_hat) + eps_adam) + decay *...  17 us

profile of v9, /device:TPU:0, one launch (start us, length us, event | category | flops | bytes accessed | tf_op | source)
XLA Modules:
  0.0 606.1 jit_solution(1887593013666033339)
XLA Ops:
  3.0 1.0 convert_element_type.66
  4.5 1.1 convert_element_type.65
  6.5 0.8 pad_maximum_fusion.qkv_ref
  7.3 211.0 %attention.1 = (bf16[8,128,2048]{2,1,0:T(8,128)(2,1)}, f32[8,128,128]{2,1,0:T(8,128)}, bf16[32,64,512]{2,1,0:T(8,128)(2,1)}, f32[8,2048]{1,0:T(8,128)}, bf16[8,2...) custom-call(s32[1,3]{1,0:T(1,128)} %starts_ref.1, ...), custom_call_target="tpu_custom_call" | custom-call | tf_op jit(solution)/shard_map/attention/pallas_call | solution.py:1007
  218.3 1.3 copy.61
  219.6 4.7 multiply_reduce_fusion.2
  224.4 0.9 fusion.22
  225.3 0.9 multiply_convert_fusion.rows_ref
  226.3 169.9 %feed.1 = (f32[128,2048]{1,0:T(8,128)}, f32[128,2048]{1,0:T(8,128)}, bf16[2048,2048]{1,0:T(8,128)(2,1)}, bf16[1024,2048]{1,0:T(8,128)(2,1)}) custom-call(bf16[128,2048]{1,0:T(8,128)(2,1)} %multiply_convert_fusion.rows_ref, bf16[8,128,2048]{2,1,0:T(8,128)(2,1)} %get-tuple-element.56.grads_all, bf16[2048,2048]{1,0:T(8,128)(2,1)} %bitcast.39, ...), custom_call_target="tpu_custom_call" | custom-call | tf_op jit(solution)/shard_map/feed/pallas_call | solution.py:1222
  396.2 1.5 multiply_reduce_fusion.1
  397.7 2.8 multiply_add_fusion.2
  400.5 5.6 convolution_convert_fusion
  406.1 2.9 convolution_convert_fusion.1
  409.3 1.0 copy.63
  410.3 72.0 %attention_back.1 = (bf16[8,128,2048]{2,1,0:T(8,128)(2,1)}, bf16[32,64,384]{2,1,0:T(8,128)(2,1)}, bf16[64,16384]{1,0:T(8,128)(2,1)}) custom-call(bf16[8,2,2,128,64]{4,3,2,1,0:T(8,128)(2,1)} %get-tuple-element.61.query_ref, bf16[8,128,64]{2,1,0:T(8,128)(2,1)} %get-tuple-element.62.key_ref, bf16[8,128,64]{2,1,0:T(8,128)(2,1)} %get-tuple-element.63.value_ref, ...), custom_call_target="tpu_custom_call" | custom-call | tf_op jit(solution)/shard_map/attention_back/pallas_call | solution.py:1366
  482.4 97.4 %closing.1 = (f32[128,2048]{1,0:T(8,128)}, bf16[64,2048]{1,0:T(8,128)(2,1)}, bf16[64,1024]{1,0:T(8,128)(2,1)}, f32[64,2048]{1,0:T(8,128)}, f32[4,64,2048]{2,1,0:T(8,128)}) custom-call(bf16[8,128,2048]{2,1,0:T(8,128)(2,1)} %get-tuple-element.71.rows_ref, bf16[32,64,384]{2,1,0:T(8,128)(2,1)} %get-tuple-element.72.parts_ref, bf16[32,64,2048]{2,1,0:T(8,128)(2,1)} %bitcast.34, ...), custom_call_target="tpu_custom_call" | custom-call | tf_op jit(solution)/shard_map/closing/pallas_call | solution.py:1467
  579.8 3.8 multiply_subtract_fusion.2
  583.8 2.9 multiply_subtract_fusion.4
  586.8 5.8 multiply_subtract_fusion
  593.2 1.6 copy-done.1
  597.7 4.0 multiply_subtract_fusion.1
  602.2 1.3 fusion.7
  603.5 0.8 copy.70
  604.3 1.3 copy.71
  (77 shorter events, 8.2 us)
Async XLA Ops:
  7.3 212.3 %copy-start.2 = (bf16[128,2048]{1,0:T(8,128)(2,1)S(1)}, bf16[128,2048]{1,0:T(8,128)(2,1)}, u32[]{:S(2)}) copy-start(bf16[128,2048]{1,0:T(8,128)(2,1)} %rows_ref.1) | copy-start | bytes 1572868
  226.3 171.4 %copy-start.12 = (bf16[128,2048]{1,0:T(8,128)(2,1)S(1)}, bf16[128,2048]{1,0:T(8,128)(2,1)}, u32[]{:S(2)}) copy-start(bf16[128,2048]{1,0:T(8,128)(2,1)} %grads_ref.1) | copy-start | bytes 1572868
  397.7 8.4 %slice-start = ((s8[8388608]{0:T(1024)(128)(4,1)}), s8[4194304]{0:T(1024)(128)(4,1)S(1)}, s32[]{:S(2)}) async-start(s8[8388608]{0:T(1024)(128)(4,1)} %bitcast.31), calls=%async_computation | async-start | bytes 8388608
  400.5 5.6 slice-start.1
  482.3 97.5 %copy-start.5 = (f32[64,2048]{1,0:T(8,128)S(1)}, f32[64,2048]{1,0:T(8,128)}, u32[]{:S(2)}) copy-start(f32[64,2048]{1,0:T(8,128)} %param.29) | copy-start | bytes 1572868
  482.3 97.4 %copy-start.16 = (f32[64,2048]{1,0:T(8,128)S(1)}, f32[64,2048]{1,0:T(8,128)}, u32[]{:S(2)}) copy-start(f32[64,2048]{1,0:T(8,128)} %out_rows_ref.1) | copy-start | bytes 1572868
  482.3 97.4 %copy-start.18 = (f32[64,2048]{1,0:T(8,128)S(1)}, f32[64,2048]{1,0:T(8,128)}, u32[]{:S(2)}) copy-start(f32[64,2048]{1,0:T(8,128)} %param.37) | copy-start | bytes 1572868
  482.3 97.4 %copy-start.19 = (f32[64,2048]{1,0:T(8,128)S(1)}, f32[64,2048]{1,0:T(8,128)}, u32[]{:S(2)}) copy-start(f32[64,2048]{1,0:T(8,128)} %param.36) | copy-start | bytes 1572868
  482.3 101.4 %copy-start.20 = (f32[64,1024]{1,0:T(8,128)S(1)}, f32[64,1024]{1,0:T(8,128)}, u32[]{:S(2)}) copy-start(f32[64,1024]{1,0:T(8,128)} %param.34) | copy-start | bytes 786436
  482.3 104.4 %copy-start.7 = (f32[64,16384]{1,0:T(8,128)S(1)}, f32[64,16384]{1,0:T(8,128)}, u32[]{:S(2)}) copy-start(f32[64,16384]{1,0:T(8,128)} %param.39) | copy-start | bytes 12582916
  579.8 4.0 copy-start.9
  579.8 7.0 %copy-start = (f32[64,16384]{1,0:T(8,128)S(1)}, f32[64,16384]{1,0:T(8,128)}, u32[]{:S(2)}) copy-start(f32[64,16384]{1,0:T(8,128)} %blocks_ref.1) | copy-start | bytes 12582916
  579.8 7.0 %copy-start.6 = (f32[64,16384]{1,0:T(8,128)S(1)}, f32[64,16384]{1,0:T(8,128)}, u32[]{:S(2)}) copy-start(f32[64,16384]{1,0:T(8,128)} %param.40) | copy-start | bytes 12582916
  579.8 7.0 %copy-start.15 = (bf16[64,16384]{1,0:T(8,128)(2,1)S(1)}, bf16[64,16384]{1,0:T(8,128)(2,1)}, u32[]{:S(2)}) copy-start(bf16[64,16384]{1,0:T(8,128)(2,1)} %get-tuple-element.77) | copy-start | bytes 6291460
  583.6 9.0 %copy-start.14 = (f32[64,2048]{1,0:T(8,128)}, f32[64,2048]{1,0:T(8,128)S(1)}, u32[]{:S(2)}) copy-start(f32[64,2048]{1,0:T(8,128)S(1)} %get-tuple-element.147) | copy-start | bytes 1572868
  586.6 6.0 copy-start.17
  586.8 8.0 %copy-start.23 = (f32[2,64]{1,0:T(2,128)S(1)}, f32[2,64]{1,0:T(2,128)}, u32[]{:S(2)}) copy-start(f32[2,64]{1,0:T(2,128)} %param.27) | copy-start | bytes 1540
  592.6 2.1 copy-start.1
  592.6 2.1 copy-start.21
  592.7 3.1 copy-start.3
  592.7 3.7 copy-start.4
  592.7 4.4 copy-start.10
  592.7 5.0 copy-start.11
  597.7 4.2 copy-start.8
  (2 other events, 4.0 us)

commit v10 on v9

--- a/solution.py
+++ b/solution.py
@@ -167,8 +167,8 @@
 
 
 class SequenceGather:
-    def __init__(self, own, out, sems, chunks):
-        self.own, self.out, self.chunks = own, out, chunks
+    def __init__(self, own, out, sems, chunks, direct=False):
+        self.own, self.out, self.chunks, self.direct = own, out, chunks, direct
         self.zs, self.zr, self.ys, self.yr, self.local_sem = sems
         self.d, self.c, _, _, self.z, self.y = place()
         self.rows = own.shape[0] // chunks
@@ -215,16 +215,17 @@
     def first(self, by_block=False):
         self.local = pltpu.make_async_copy(self.own, self.out.at[self.c], self.local_sem)
         self.local.start()
-        near, mid, _ = near_first(self.z)
+        near, mid, far = near_first(self.z)
+        targets = (far, mid, near) if self.direct else (mid, near)
         if by_block:
             for k in range(self.chunks):
                 self.start(self.across(self.z, k, self.part(self.own, k)))
-            for to in (mid, near):
+            for to in targets:
                 for k in range(self.chunks):
                     self.start(self.along(to, k))
             return
         for k in range(self.chunks):
-            for to in (mid, near):
+            for to in targets:
                 self.start(self.along(to, k))
             self.start(self.across(self.z, k, self.part(self.own, k)))
 
@@ -256,6 +257,8 @@
         _, mid, far = near_first(self.z)
         for i, source in enumerate((mid, far)):
             self.relay_one(source, k)
+            if self.direct:
+                continue
 
             @pl.when(is_inner(self.z))
             def _(i=i, source=source):
@@ -284,6 +287,8 @@
     def finish(self):
         for copy in self.sent:
             copy.wait_send()
+        if self.direct:
+            return
         _, mid, far = near_first(self.z)
 
         @pl.when(is_inner(self.z))
@@ -807,7 +812,7 @@
     outs_chip = ChipGather(out_rows_out, take(4), PLANE)
     rows = SequenceGather(rows_ref, rows_all, take(5), 2)
     table = SequenceGather(table_ref, table_out, take(5), 1)
-    grads = SequenceGather(grads_ref, grads_out, take(5), CHUNKS)
+    grads = SequenceGather(grads_ref, grads_out, take(5), CHUNKS, direct=True)
     down_rows = down_ref.shape[0] // DOWN_PARTS
     down = ChipGather(down_out, take(4), DOWN_PARTS, down_rows)
     spot_send, spot_recv, spot_local, down_local = take(4)

time: 615 us -> 625 us (1.016)
  Pallas kernels: 550 us -> 560 us
    pallas_call x1, Pallas kernels: 211 us -> 220 us  [attention(): pl.pallas_call(attention_kernel, out_shape=(jax.ShapeDtypeStruct((PLANE,...]
where the time goes in v10:
time: 625 us; the launch traced here: 616 us
  Pallas kernels  560 us (90%)
  other arithmetic  30.2 us (5%)
  matrix products  13.2 us (2%)
  local copies, waits for them, and re-layouts  10.9 us (2%)
    pallas_call x1, Pallas kernels, attention(): pl.pallas_call(attention_kernel, out_shape=(jax.ShapeDtypeStruct((PLANE,...  220 us
    pallas_call x1, Pallas kernels, feed(): pl.pallas_call(feed_kernel, out_shape=(summed, summed, jax.ShapeDtypeStru...  167 us
    pallas_call x1, Pallas kernels, closing(): pl.pallas_call(closing_kernel, out_shape=(jax.ShapeDtypeStruct(rows.shape...  97.8 us
    pallas_call x1, Pallas kernels, attention_back(): pl.pallas_call(attention_back_kernel, out_shape=(jax.ShapeDtypeStruct(inp...  75.1 us
    sub x5, other arithmetic, adamw(): weight - rate * (first_hat / (jnp.sqrt(second_hat) + eps_adam) + decay *...  17 us

profile of v10, /device:TPU:0, one launch (start us, length us, event | category | flops | bytes accessed | tf_op | source)
XLA Modules:
  0.0 615.8 jit_solution(8159399744057111301)
XLA Ops:
  3.0 1.0 convert_element_type.66
  4.5 1.1 convert_element_type.65
  6.5 0.8 pad_maximum_fusion.qkv_ref
  7.3 219.7 %attention.1 = (bf16[8,128,2048]{2,1,0:T(8,128)(2,1)}, f32[8,128,128]{2,1,0:T(8,128)}, bf16[32,64,512]{2,1,0:T(8,128)(2,1)}, f32[8,2048]{1,0:T(8,128)}, bf16[8,2...) custom-call(s32[1,3]{1,0:T(1,128)} %starts_ref.1, ...), custom_call_target="tpu_custom_call" | custom-call | tf_op jit(solution)/shard_map/attention/pallas_call | solution.py:1012
  227.1 1.3 copy.61
  228.4 4.7 multiply_reduce_fusion.2
  233.1 0.9 fusion.22
  234.1 0.9 multiply_convert_fusion.rows_ref
  235.0 167.2 %feed.1 = (f32[128,2048]{1,0:T(8,128)}, f32[128,2048]{1,0:T(8,128)}, bf16[2048,2048]{1,0:T(8,128)(2,1)}, bf16[1024,2048]{1,0:T(8,128)(2,1)}) custom-call(bf16[128,2048]{1,0:T(8,128)(2,1)} %multiply_convert_fusion.rows_ref, bf16[8,128,2048]{2,1,0:T(8,128)(2,1)} %get-tuple-element.56.grads_all, bf16[2048,2048]{1,0:T(8,128)(2,1)} %bitcast.39, ...), custom_call_target="tpu_custom_call" | custom-call | tf_op jit(solution)/shard_map/feed/pallas_call | solution.py:1227
  402.3 1.5 multiply_reduce_fusion.1
  403.8 2.8 multiply_add_fusion.2
  406.6 5.6 convolution_convert_fusion
  412.2 2.9 convolution_convert_fusion.1
  415.4 1.0 copy.63
  416.4 75.1 %attention_back.1 = (bf16[8,128,2048]{2,1,0:T(8,128)(2,1)}, bf16[32,64,384]{2,1,0:T(8,128)(2,1)}, bf16[64,16384]{1,0:T(8,128)(2,1)}) custom-call(bf16[8,2,2,128,64]{4,3,2,1,0:T(8,128)(2,1)} %get-tuple-element.61.query_ref, bf16[8,128,64]{2,1,0:T(8,128)(2,1)} %get-tuple-element.62.key_ref, bf16[8,128,64]{2,1,0:T(8,128)(2,1)} %get-tuple-element.63.value_ref, ...), custom_call_target="tpu_custom_call" | custom-call | tf_op jit(solution)/shard_map/attention_back/pallas_call | solution.py:1371
  491.6 97.8 %closing.1 = (f32[128,2048]{1,0:T(8,128)}, bf16[64,2048]{1,0:T(8,128)(2,1)}, bf16[64,1024]{1,0:T(8,128)(2,1)}, f32[64,2048]{1,0:T(8,128)}, f32[4,64,2048]{2,1,0:T(8,128)}) custom-call(bf16[8,128,2048]{2,1,0:T(8,128)(2,1)} %get-tuple-element.71.rows_ref, bf16[32,64,384]{2,1,0:T(8,128)(2,1)} %get-tuple-element.72.parts_ref, bf16[32,64,2048]{2,1,0:T(8,128)(2,1)} %bitcast.34, ...), custom_call_target="tpu_custom_call" | custom-call | tf_op jit(solution)/shard_map/closing/pallas_call | solution.py:1472
  589.5 3.8 multiply_subtract_fusion.2
  593.5 2.9 multiply_subtract_fusion.4
  596.5 5.8 multiply_subtract_fusion
  602.9 1.6 copy-done.1
  607.4 4.0 multiply_subtract_fusion.1
  611.9 1.3 fusion.7
  613.2 0.8 copy.70
  614.0 1.3 copy.71
  (77 shorter events, 8.2 us)
Async XLA Ops:
  7.3 221.1 %copy-start.2 = (bf16[128,2048]{1,0:T(8,128)(2,1)S(1)}, bf16[128,2048]{1,0:T(8,128)(2,1)}, u32[]{:S(2)}) copy-start(bf16[128,2048]{1,0:T(8,128)(2,1)} %rows_ref.1) | copy-start | bytes 1572868
  235.0 168.8 %copy-start.12 = (bf16[128,2048]{1,0:T(8,128)(2,1)S(1)}, bf16[128,2048]{1,0:T(8,128)(2,1)}, u32[]{:S(2)}) copy-start(bf16[128,2048]{1,0:T(8,128)(2,1)} %grads_ref.1) | copy-start | bytes 1572868
  403.8 8.4 %slice-start = ((s8[8388608]{0:T(1024)(128)(4,1)}), s8[4194304]{0:T(1024)(128)(4,1)S(1)}, s32[]{:S(2)}) async-start(s8[8388608]{0:T(1024)(128)(4,1)} %bitcast.31), calls=%async_computation | async-start | bytes 8388608
  406.6 5.6 slice-start.1
  491.5 97.9 %copy-start.5 = (f32[64,2048]{1,0:T(8,128)S(1)}, f32[64,2048]{1,0:T(8,128)}, u32[]{:S(2)}) copy-start(f32[64,2048]{1,0:T(8,128)} %param.29) | copy-start | bytes 1572868
  491.5 97.9 %copy-start.16 = (f32[64,2048]{1,0:T(8,128)S(1)}, f32[64,2048]{1,0:T(8,128)}, u32[]{:S(2)}) copy-start(f32[64,2048]{1,0:T(8,128)} %out_rows_ref.1) | copy-start | bytes 1572868
  491.5 97.9 %copy-start.18 = (f32[64,2048]{1,0:T(8,128)S(1)}, f32[64,2048]{1,0:T(8,128)}, u32[]{:S(2)}) copy-start(f32[64,2048]{1,0:T(8,128)} %param.37) | copy-start | bytes 1572868
  491.5 97.9 %copy-start.19 = (f32[64,2048]{1,0:T(8,128)S(1)}, f32[64,2048]{1,0:T(8,128)}, u32[]{:S(2)}) copy-start(f32[64,2048]{1,0:T(8,128)} %param.36) | copy-start | bytes 1572868
  491.6 101.9 %copy-start.20 = (f32[64,1024]{1,0:T(8,128)S(1)}, f32[64,1024]{1,0:T(8,128)}, u32[]{:S(2)}) copy-start(f32[64,1024]{1,0:T(8,128)} %param.34) | copy-start | bytes 786436
  491.6 104.9 %copy-start.7 = (f32[64,16384]{1,0:T(8,128)S(1)}, f32[64,16384]{1,0:T(8,128)}, u32[]{:S(2)}) copy-start(f32[64,16384]{1,0:T(8,128)} %param.39) | copy-start | bytes 12582916
  589.5 4.0 copy-start.9
  589.5 7.0 %copy-start = (f32[64,16384]{1,0:T(8,128)S(1)}, f32[64,16384]{1,0:T(8,128)}, u32[]{:S(2)}) copy-start(f32[64,16384]{1,0:T(8,128)} %blocks_ref.1) | copy-start | bytes 12582916
  589.5 7.0 %copy-start.6 = (f32[64,16384]{1,0:T(8,128)S(1)}, f32[64,16384]{1,0:T(8,128)}, u32[]{:S(2)}) copy-start(f32[64,16384]{1,0:T(8,128)} %param.40) | copy-start | bytes 12582916
  589.5 7.0 %copy-start.15 = (bf16[64,16384]{1,0:T(8,128)(2,1)S(1)}, bf16[64,16384]{1,0:T(8,128)(2,1)}, u32[]{:S(2)}) copy-start(bf16[64,16384]{1,0:T(8,128)(2,1)} %get-tuple-element.77) | copy-start | bytes 6291460
  593.3 9.0 %copy-start.14 = (f32[64,2048]{1,0:T(8,128)}, f32[64,2048]{1,0:T(8,128)S(1)}, u32[]{:S(2)}) copy-start(f32[64,2048]{1,0:T(8,128)S(1)} %get-tuple-element.147) | copy-start | bytes 1572868
  596.3 6.0 copy-start.17
  596.5 8.0 %copy-start.23 = (f32[2,64]{1,0:T(2,128)S(1)}, f32[2,64]{1,0:T(2,128)}, u32[]{:S(2)}) copy-start(f32[2,64]{1,0:T(2,128)} %param.27) | copy-start | bytes 1540
  602.4 2.1 copy-start.1
  602.4 2.1 copy-start.21
  602.4 3.1 copy-start.3
  602.4 3.7 copy-start.4
  602.4 4.4 copy-start.10
  602.4 5.0 copy-start.11
  607.4 4.2 copy-start.8
  (2 other events, 4.0 us)
